TPU v7x, 32 devices: a whole 2x2x4 slice. The times are simulated.
32 devices in a mesh: dp: 2 (over core), fsdp: 16 (over z, y, x).
Axes of the slice: x: 2, y: 2, z: 4, core: 2. Of those that a mesh axis runs over, the one named last changes fastest.
Arguments:
- tokens: bfloat16 [32768, 768], P(('dp', 'fsdp')), may hold values from -6 to 6
- clip_frames: int32 [8], replicated, may hold values from 8 to 16, as said below
- tube_clip: int32 [128], P(('dp', 'fsdp')), may hold values from 0 to 7, as said below
- first_gain: bfloat16 [768], P('fsdp'), may hold values from 0.25 to 1.75
- first_shift: bfloat16 [768], P('fsdp'), may hold values from -1.75 to 1.75
- qkv_weight: bfloat16 [768, 2304], P('fsdp'), may hold values from -0.21875 to 0.21875
- query_bias: bfloat16 [768], P('fsdp'), may hold values from -1.75 to 1.75
- value_bias: bfloat16 [768], P('fsdp'), may hold values from -1.75 to 1.75
- out_weight: bfloat16 [768, 768], P('fsdp'), may hold values from -2.5 to 2.5
- out_bias: bfloat16 [768], P('fsdp'), may hold values from -1.75 to 1.75
- second_gain: bfloat16 [768], P('fsdp'), may hold values from 0.25 to 1.75
- second_shift: bfloat16 [768], P('fsdp'), may hold values from -1.75 to 1.75
- up_weight: bfloat16 [768, 3072], P('fsdp'), may hold values from -0.21875 to 0.21875
- up_bias: bfloat16 [3072], P('fsdp'), may hold values from -1.75 to 1.75
- down_weight: bfloat16 [3072, 768], P('fsdp'), may hold values from -0.109375 to 0.109375
- down_bias: bfloat16 [768], P('fsdp'), may hold values from -1.75 to 1.75
- cotangent: bfloat16 [32768, 768], P(('dp', 'fsdp')), may hold values from -6 to 6
Outputs:
- block_out: bfloat16 [32768, 768], P(('dp', 'fsdp'))
- tokens_grad: bfloat16 [32768, 768], P(('dp', 'fsdp'))
- first_gain_grad: float32 [768], P('fsdp')
- first_shift_grad: float32 [768], P('fsdp')
- qkv_weight_grad: float32 [768, 2304], P('fsdp')
- query_bias_grad: float32 [768], P('fsdp')
- value_bias_grad: float32 [768], P('fsdp')
- out_weight_grad: float32 [768, 768], P('fsdp')
- out_bias_grad: float32 [768], P('fsdp')
- second_gain_grad: float32 [768], P('fsdp')
- second_shift_grad: float32 [768], P('fsdp')
- up_weight_grad: float32 [768, 3072], P('fsdp')
- up_bias_grad: float32 [3072], P('fsdp')
- down_weight_grad: float32 [3072, 768], P('fsdp')
- down_bias_grad: float32 [768], P('fsdp')
Inputs may be any that keep to these rules, and one draw needn't show every extreme that they name: `clip_frames`: some clip has 16 real frames. `tube_clip`: each clip number names exactly 16 tubes.
All inputs are finite; a program needn't handle non-finite values.
Results may differ from a plain program's by a relative error of at most 0.014.
Values may be sent and summed in bfloat16 or wider, within the bound.
No kernel may reach another device: no remote copies, remote signals or barrier semaphores. Data moves between devices by JAX's collectives and lax.ppermute only.
A program may use at most 128 MiB of HBM per device.

v0:
```python
import jax
import jax.numpy as jnp
from jax import lax
from jax.sharding import PartitionSpec as P

HEADS = 12
HEAD_DIM = 64
PATCH = 16


EPSILON = 1e-05
SQRT_HALF = 0.7071067811865476
DENSITY = 0.3989422804014327


def norm_forward(values, gain, shift):
    average = jnp.mean(values, axis=-1, keepdims=True)
    centred = values - average
    spread = jnp.mean(centred * centred, axis=-1, keepdims=True)
    inverse = lax.rsqrt(spread + EPSILON)
    standard = centred * inverse
    return (standard, inverse, standard * gain + shift)


def norm_backward(upstream, standard, inverse, gain):
    scaled = upstream * gain
    first_mean = jnp.mean(scaled, axis=-1, keepdims=True)
    second_mean = jnp.mean(scaled * standard, axis=-1, keepdims=True)
    inputs_grad = inverse * (scaled - first_mean - standard * second_mean)
    return (inputs_grad, jnp.sum(upstream * standard, axis=0), jnp.sum(upstream, axis=0))


def split_heads(matrix, tubes_here):
    rows, width = matrix.shape
    return matrix.reshape(tubes_here, rows // tubes_here, HEADS, width // HEADS).transpose(
        2, 0, 1, 3
    )


def join_heads(stacked):
    heads, tubes_here, length, size = stacked.shape
    return stacked.transpose(1, 2, 0, 3).reshape(tubes_here * length, heads * size)


def head_probs(query_head, key_head, key_ok):
    scores = jnp.einsum(
        "btd,bsd->bts", query_head, key_head, preferred_element_type=jnp.float32
    ) * HEAD_DIM ** (-0.5)
    masked = jnp.where(key_ok[:, None, :], scores, -1e30)
    return jax.nn.softmax(masked, axis=-1)


def forward_pass(weights, tokens, key_ok):
    (
        first_gain,
        first_shift,
        qkv_weight,
        query_bias,
        value_bias,
        out_weight,
        out_bias,
        second_gain,
        second_shift,
        up_weight,
        up_bias,
        down_weight,
        down_bias,
    ) = weights
    tubes_here = key_ok.shape[0]
    width = tokens.shape[1]
    inputs = tokens.astype(jnp.float32)
    standard_one, inverse_one, normed = norm_forward(
        inputs, first_gain.astype(jnp.float32), first_shift.astype(jnp.float32)
    )
    normed_one = normed.astype(jnp.bfloat16)
    project = jnp.dot(normed_one, qkv_weight, preferred_element_type=jnp.float32)
    query = (project[:, :width] + query_bias.astype(jnp.float32)).astype(jnp.bfloat16)
    keys_part = project[:, width : 2 * width].astype(jnp.bfloat16)
    values_part = (project[:, 2 * width :] + value_bias.astype(jnp.float32)).astype(jnp.bfloat16)
    query_heads = split_heads(query, tubes_here)
    key_heads = split_heads(keys_part, tubes_here)
    value_heads = split_heads(values_part, tubes_here)

    def attend(item):
        query_head, key_head, value_head = item
        probs = head_probs(query_head, key_head, key_ok)
        return jnp.einsum(
            "bts,bsd->btd",
            probs.astype(jnp.bfloat16),
            value_head,
            preferred_element_type=jnp.float32,
        ).astype(jnp.bfloat16)

    mixed = join_heads(lax.map(attend, (query_heads, key_heads, value_heads)))
    attended = jnp.dot(mixed, out_weight, preferred_element_type=jnp.float32) + out_bias.astype(
        jnp.float32
    )
    resid = inputs + attended
    standard_two, inverse_two, normed = norm_forward(
        resid, second_gain.astype(jnp.float32), second_shift.astype(jnp.float32)
    )
    normed_two = normed.astype(jnp.bfloat16)
    hidden = jnp.dot(normed_two, up_weight, preferred_element_type=jnp.float32) + up_bias.astype(
        jnp.float32
    )
    active = jax.nn.gelu(hidden, approximate=False).astype(jnp.bfloat16)
    output = resid + (
        jnp.dot(active, down_weight, preferred_element_type=jnp.float32)
        + down_bias.astype(jnp.float32)
    )
    saved = (
        standard_one,
        inverse_one,
        normed_one,
        query_heads,
        key_heads,
        value_heads,
        mixed,
        standard_two,
        inverse_two,
        normed_two,
        hidden,
        active,
    )
    return (output, saved)


def local(
    tokens,
    clip_frames,
    tube_clip,
    first_gain,
    first_shift,
    qkv_weight,
    query_bias,
    value_bias,
    out_weight,
    out_bias,
    second_gain,
    second_shift,
    up_weight,
    up_bias,
    down_weight,
    down_bias,
    cotangent,
):
    gathered = (
        lax.all_gather(first_gain, "fsdp", axis=0, tiled=True),
        lax.all_gather(first_shift, "fsdp", axis=0, tiled=True),
        lax.all_gather(qkv_weight, "fsdp", axis=0, tiled=True),
        lax.all_gather(query_bias, "fsdp", axis=0, tiled=True),
        lax.all_gather(value_bias, "fsdp", axis=0, tiled=True),
        lax.all_gather(out_weight, "fsdp", axis=0, tiled=True),
        lax.all_gather(out_bias, "fsdp", axis=0, tiled=True),
        lax.all_gather(second_gain, "fsdp", axis=0, tiled=True),
        lax.all_gather(second_shift, "fsdp", axis=0, tiled=True),
        lax.all_gather(up_weight, "fsdp", axis=0, tiled=True),
        lax.all_gather(up_bias, "fsdp", axis=0, tiled=True),
        lax.all_gather(down_weight, "fsdp", axis=0, tiled=True),
        lax.all_gather(down_bias, "fsdp", axis=0, tiled=True),
    )
    tubes_here = tube_clip.shape[0]
    length = tokens.shape[0] // tubes_here
    clip_count = clip_frames.shape[0]
    matches = tube_clip[:, None] == jnp.arange(clip_count, dtype=jnp.int32)[None, :]
    tube_frames = jnp.sum(jnp.where(matches, clip_frames[None, :], 0), axis=1)
    key_ok = jnp.arange(length, dtype=jnp.int32)[None, :] // PATCH < tube_frames[:, None]
    row_ok = key_ok.reshape(tubes_here * length, 1).astype(jnp.float32)
    output, unused = forward_pass(gathered, tokens, key_ok)
    block_out = output.astype(jnp.bfloat16)
    second = (
        lax.all_gather(first_gain, "fsdp", axis=0, tiled=True),
        lax.all_gather(first_shift, "fsdp", axis=0, tiled=True),
        lax.all_gather(qkv_weight, "fsdp", axis=0, tiled=True),
        lax.all_gather(query_bias, "fsdp", axis=0, tiled=True),
        lax.all_gather(value_bias, "fsdp", axis=0, tiled=True),
        lax.all_gather(out_weight, "fsdp", axis=0, tiled=True),
        lax.all_gather(out_bias, "fsdp", axis=0, tiled=True),
        lax.all_gather(second_gain, "fsdp", axis=0, tiled=True),
        lax.all_gather(second_shift, "fsdp", axis=0, tiled=True),
        lax.all_gather(up_weight, "fsdp", axis=0, tiled=True),
        lax.all_gather(up_bias, "fsdp", axis=0, tiled=True),
        lax.all_gather(down_weight, "fsdp", axis=0, tiled=True),
        lax.all_gather(down_bias, "fsdp", axis=0, tiled=True),
    )
    (
        full_gain_one,
        full_shift_one,
        full_qkv,
        full_query_bias,
        full_value_bias,
        full_out,
        full_out_bias,
        full_gain_two,
        full_shift_two,
        full_up,
        full_up_bias,
        full_down,
        full_down_bias,
    ) = second
    again, saved = forward_pass(second, tokens, key_ok)
    (
        standard_one,
        inverse_one,
        normed_one,
        query_heads,
        key_heads,
        value_heads,
        mixed,
        standard_two,
        inverse_two,
        normed_two,
        hidden,
        active,
    ) = saved
    upstream = cotangent.astype(jnp.float32) * row_ok
    upstream_low = upstream.astype(jnp.bfloat16)
    down_grad = jnp.einsum("rf,rd->fd", active, upstream_low, preferred_element_type=jnp.float32)
    down_bias_grad = jnp.sum(upstream, axis=0)
    active_grad = jnp.einsum(
        "rd,fd->rf", upstream_low, full_down, preferred_element_type=jnp.float32
    )
    cumulative = 0.5 * (1.0 + jax.scipy.special.erf(hidden * SQRT_HALF))
    slope = cumulative + hidden * DENSITY * jnp.exp(-0.5 * hidden * hidden)
    hidden_grad = (active_grad * slope).astype(jnp.bfloat16)
    up_grad = jnp.einsum("rd,rf->df", normed_two, hidden_grad, preferred_element_type=jnp.float32)
    up_bias_grad = jnp.sum(hidden_grad.astype(jnp.float32), axis=0)
    normed_grad = jnp.einsum("rf,df->rd", hidden_grad, full_up, preferred_element_type=jnp.float32)
    resid_part, second_gain_grad, second_shift_grad = norm_backward(
        normed_grad, standard_two, inverse_two, full_gain_two.astype(jnp.float32)
    )
    resid_grad = upstream + resid_part
    attended_grad = resid_grad.astype(jnp.bfloat16)
    out_grad = jnp.einsum("rd,re->de", mixed, attended_grad, preferred_element_type=jnp.float32)
    out_bias_grad = jnp.sum(attended_grad.astype(jnp.float32), axis=0)
    mixed_grad = jnp.einsum(
        "re,de->rd", attended_grad, full_out, preferred_element_type=jnp.float32
    ).astype(jnp.bfloat16)
    mixed_heads = split_heads(mixed_grad, tubes_here)

    def attend_back(item):
        query_head, key_head, value_head, upper_head = item
        probs = head_probs(query_head, key_head, key_ok)
        probs_low = probs.astype(jnp.bfloat16)
        values_grad = jnp.einsum(
            "bts,btd->bsd", probs_low, upper_head, preferred_element_type=jnp.float32
        )
        probs_grad = jnp.einsum(
            "btd,bsd->bts", upper_head, value_head, preferred_element_type=jnp.float32
        )
        scores_grad = probs * (probs_grad - jnp.sum(probs_grad * probs, axis=-1, keepdims=True))
        scores_low = scores_grad.astype(jnp.bfloat16)
        query_grad = jnp.einsum(
            "bts,bsd->btd", scores_low, key_head, preferred_element_type=jnp.float32
        ) * HEAD_DIM ** (-0.5)
        keys_grad = jnp.einsum(
            "bts,btd->bsd", scores_low, query_head, preferred_element_type=jnp.float32
        ) * HEAD_DIM ** (-0.5)
        return (
            query_grad.astype(jnp.bfloat16),
            keys_grad.astype(jnp.bfloat16),
            values_grad.astype(jnp.bfloat16),
        )

    query_back, keys_back, values_back = lax.map(
        attend_back, (query_heads, key_heads, value_heads, mixed_heads)
    )
    query_grad = join_heads(query_back)
    values_grad = join_heads(values_back)
    project_grad = jnp.concatenate([query_grad, join_heads(keys_back), values_grad], axis=1)
    qkv_grad = jnp.einsum("rd,re->de", normed_one, project_grad, preferred_element_type=jnp.float32)
    query_bias_grad = jnp.sum(query_grad.astype(jnp.float32), axis=0)
    value_bias_grad = jnp.sum(values_grad.astype(jnp.float32), axis=0)
    normed_grad_one = jnp.einsum(
        "re,de->rd", project_grad, full_qkv, preferred_element_type=jnp.float32
    )
    inputs_part, first_gain_grad, first_shift_grad = norm_backward(
        normed_grad_one, standard_one, inverse_one, full_gain_one.astype(jnp.float32)
    )
    tokens_grad = (resid_grad + inputs_part).astype(jnp.bfloat16)
    pieces = (
        lax.psum_scatter(first_gain_grad, "fsdp", scatter_dimension=0, tiled=True),
        lax.psum_scatter(first_shift_grad, "fsdp", scatter_dimension=0, tiled=True),
        lax.psum_scatter(qkv_grad, "fsdp", scatter_dimension=0, tiled=True),
        lax.psum_scatter(query_bias_grad, "fsdp", scatter_dimension=0, tiled=True),
        lax.psum_scatter(value_bias_grad, "fsdp", scatter_dimension=0, tiled=True),
        lax.psum_scatter(out_grad, "fsdp", scatter_dimension=0, tiled=True),
        lax.psum_scatter(out_bias_grad, "fsdp", scatter_dimension=0, tiled=True),
        lax.psum_scatter(second_gain_grad, "fsdp", scatter_dimension=0, tiled=True),
        lax.psum_scatter(second_shift_grad, "fsdp", scatter_dimension=0, tiled=True),
        lax.psum_scatter(up_grad, "fsdp", scatter_dimension=0, tiled=True),
        lax.psum_scatter(up_bias_grad, "fsdp", scatter_dimension=0, tiled=True),
        lax.psum_scatter(down_grad, "fsdp", scatter_dimension=0, tiled=True),
        lax.psum_scatter(down_bias_grad, "fsdp", scatter_dimension=0, tiled=True),
    )
    totals = (
        lax.psum(pieces[0].astype(jnp.bfloat16), "dp").astype(jnp.float32),
        lax.psum(pieces[1].astype(jnp.bfloat16), "dp").astype(jnp.float32),
        lax.psum(pieces[2].astype(jnp.bfloat16), "dp").astype(jnp.float32),
        lax.psum(pieces[3].astype(jnp.bfloat16), "dp").astype(jnp.float32),
        lax.psum(pieces[4].astype(jnp.bfloat16), "dp").astype(jnp.float32),
        lax.psum(pieces[5].astype(jnp.bfloat16), "dp").astype(jnp.float32),
        lax.psum(pieces[6].astype(jnp.bfloat16), "dp").astype(jnp.float32),
        lax.psum(pieces[7].astype(jnp.bfloat16), "dp").astype(jnp.float32),
        lax.psum(pieces[8].astype(jnp.bfloat16), "dp").astype(jnp.float32),
        lax.psum(pieces[9].astype(jnp.bfloat16), "dp").astype(jnp.float32),
        lax.psum(pieces[10].astype(jnp.bfloat16), "dp").astype(jnp.float32),
        lax.psum(pieces[11].astype(jnp.bfloat16), "dp").astype(jnp.float32),
        lax.psum(pieces[12].astype(jnp.bfloat16), "dp").astype(jnp.float32),
    )
    return (
        block_out,
        tokens_grad,
        totals[0],
        totals[1],
        totals[2],
        totals[3],
        totals[4],
        totals[5],
        totals[6],
        totals[7],
        totals[8],
        totals[9],
        totals[10],
        totals[11],
        totals[12],
    )


def solution(mesh):
    return jax.shard_map(
        local,
        mesh=mesh,
        in_specs=(
            P(("dp", "fsdp"), None),
            P(),
            P(("dp", "fsdp")),
            P("fsdp"),
            P("fsdp"),
            P("fsdp", None),
            P("fsdp"),
            P("fsdp"),
            P("fsdp", None),
            P("fsdp"),
            P("fsdp"),
            P("fsdp"),
            P("fsdp", None),
            P("fsdp"),
            P("fsdp", None),
            P("fsdp"),
            P(("dp", "fsdp"), None),
        ),
        out_specs=(
            P(("dp", "fsdp"), None),
            P(("dp", "fsdp"), None),
            P("fsdp"),
            P("fsdp"),
            P("fsdp", None),
            P("fsdp"),
            P("fsdp"),
            P("fsdp", None),
            P("fsdp"),
            P("fsdp"),
            P("fsdp"),
            P("fsdp", None),
            P("fsdp"),
            P("fsdp", None),
            P("fsdp"),
        ),
        check_vma=False,
    )
```

profile of v0, /device:TPU:0, one launch (start us, length us, event | category | flops | bytes accessed | tf_op | source)
XLA Modules:
  0.0 1017.1 jit_solution(9514752362472423725)
XLA Ops:
  20.2 79.2 %all-reduce.19 = (bf16[768]{0:T(1024)(128)(2,1)S(1)}, bf16[768]{0:T(1024)(128)(2,1)S(1)}, bf16[768]{0:T(1024)(128)(2,1)S(1)}, bf16[768]{0:T(1024)(128)(2,1)S(1)}...) all-reduce(bf16[768]{0:T(1024)(128)(2,1)S(1)} %dynamic-update-slice, ...), channel_id=1, replica_groups=mesh['dp'=2,'fsdp'=16] {'fsdp'}, use_global_device_ids=true, to_apply=%add.1 | all-reduce | flops 9216 | bytes 36864
  104.1 6.3 fusion.138
  112.8 2.6 copy.110
  115.4 3.9 reshape.174
  119.3 2.9 copy.113
  122.1 2.6 copy.112
  124.7 3.9 reshape.176
  128.6 2.9 copy.115
  133.1 2.9 reshape.175
  137.6 40.5 %while.30 = (s32[]{:T(128)}, bf16[12,4,256,64]{2,3,1,0:T(8,128)(2,1)S(1)}, bf16[12,4,256,64]{2,3,1,0:T(8,128)(2,1)}, bf16[12,4,256,64]{2,3,1,0:T(8,128)(2,1)}, b...) while((s32[]{:T(128)}, ...), condition=%wide.region_6.7_spmd.clone, body=%wide.region_3.6_spmd.clone.sunk | while | flops 103090688 | bytes 801893 | solution.py:94
  179.7 3.5 fusion.153
  185.2 40.2 %all-gather.9.cloned.1.call-done = bf16[768,3072]{1,0:T(8,128)(2,1)} async-done(((bf16[48,3072]{1,0:T(8,128)(2,1)}), bf16[768,3072]{1,0:T(8,128)(2,1)}) %all-gather.9.cloned.1.call-update) | async-done | bytes 4718608 | tf_op jit(solution)/shard_map/all_gather | solution.py:157
  225.4 47.9 %fusion.98 = (bf16[1024,3072]{1,0:T(8,128)(2,1)}, f32[1024,3072]{1,0:T(8,128)}) fusion(f32[3072]{0:T(1024)S(1)} %convert_element_type.222, bf16[768,3072]{1,0:T(8,128)(2,1)} %all-gather.9.cloned.1.call-done, f32[1024,768]{0,1:T(8,128)} %copy-done.2, f32[768]{0:T(1024)S(1)} %convert_element_type.220, f32[768]{0:T(1024)S(1)} %convert_element_type.219, ...), kind=kOutput, calls=%fused_computation.74 | convolution fusion | flops 5043388416 | bytes 26765312 | tf_op jit(solution)/shard_map/dot_general | solution.py:103
  273.2 33.9 %all-gather.11.cloned.1.call-done = bf16[3072,768]{1,0:T(8,128)(2,1)} async-done(((bf16[192,768]{1,0:T(8,128)(2,1)}), bf16[3072,768]{1,0:T(8,128)(2,1)}) %all-gather.11.cloned.1.call-update) | async-done | bytes 4718608 | tf_op jit(solution)/shard_map/all_gather | solution.py:159
  307.2 12.2 %convert_reduce_fusion = (f32[3072]{0:T(1024)S(1)}, bf16[1024,3072]{1,0:T(8,128)(2,1)S(1)}) fusion(f32[1024,3072]{1,0:T(8,128)} %get-tuple-element.350, f32[3072]{0:T(1024)S(1)} %convert_element_type.222, bf16[3072,768]{1,0:T(8,128)(2,1)} %all-gather.11.cloned.1.call-done, bf16[1024,768]{0,1:T(8,128)(2,1)S(1)} %copy-done.8, f32[1024]{0:T(1024)S(1)} %bitcast.205), kind=kOutput, calls=%fused_computation.80 | convolution fusion | flops 4875088896 | bytes 25194496 | tf_op jit(solution)/shard_map/rd,fd->rf/dot_general | solution.py:220
  319.4 6.8 fusion.155
  326.2 3.7 copy.119
  329.9 3.0 multiply_reduce_fusion.1
  336.6 2.8 fusion.133
  339.4 3.3 convolution_convert_fusion.2
  343.5 2.4 reshape.178
  348.9 112.2 %while.31 = (s32[]{:T(128)}, bf16[12,4,256,64]{2,3,1,0:T(8,128)(2,1)S(1)}, bf16[12,4,256,64]{2,3,1,0:T(8,128)(2,1)}, bf16[12,4,256,64]{2,3,1,0:T(8,128)(2,1)}, b...) while((s32[]{:T(128)}, ...), condition=%wide.region_15.16_spmd.clone, body=%wide.region_11.15_spmd.clone.sunk | while | flops 205850112 | bytes 8684673 | solution.py:265
  356.1 2.4 fusion.213
  365.4 2.4 fusion.213
  374.7 2.4 fusion.213
  384.1 2.4 fusion.213
  393.4 2.4 fusion.213
  402.8 2.4 fusion.213
  412.1 2.4 fusion.213
  421.4 2.4 fusion.213
  430.7 2.4 fusion.213
  440.1 2.4 fusion.213
  449.4 2.4 fusion.213
  458.7 2.4 fusion.213
  468.4 6.4 fusion.136
  474.9 10.6 %fusion.140 = f32[768,3072]{1,0:T(8,128)} fusion(bf16[1024,3072]{1,0:T(8,128)(2,1)} %copy-done.28, f32[1024,768]{0,1:T(8,128)} %copy-done.2, f32[768]{0:T(1024)S(1)} %convert_element_type.220, f32[768]{0:T(1024)S(1)} %convert_element_type.219, f32[1024]{0:T(1024)S(1)} %add_rsqrt_fusion, f32[1024]{0:T(1024)S(1)} %broadcast_multiply_fusion.4), kind=kOutput, calls=%fused_computation.168 | convolution fusion | flops 4835770368 | bytes 18888704 | tf_op jit(solution)/shard_map/rd,rf->df/dot_general | solution.py:226
  485.6 10.3 %fusion.130 = f32[3072,768]{1,0:T(8,128)} fusion(bf16[1024,3072]{1,0:T(8,128)(2,1)} %get-tuple-element.349, bf16[1024,768]{0,1:T(8,128)(2,1)} %copy.118, f32[1024]{0:T(1024)S(1)} %bitcast.207), kind=kOutput, calls=%fused_computation.135 | convolution fusion | flops 4834197504 | bytes 17305600 | tf_op jit(solution)/shard_map/rf,rd->fd/dot_general | solution.py:218
  497.3 9.2 fusion.154
  506.4 3.6 copy.128
  512.1 3.0 fusion.124
  515.1 75.2 %all-reduce.18 = (bf16[768]{0:T(1024)(128)(2,1)S(1)}, bf16[768]{0:T(1024)(128)(2,1)S(1)}, bf16[768]{0:T(1024)(128)(2,1)S(1)}, bf16[768]{0:T(1024)(128)(2,1)S(1)}...) all-reduce(f32[768]{0:T(1024)S(1)} %get-tuple-element.267, ...), channel_id=2, replica_groups=mesh['dp'=2,'fsdp'=16] {'fsdp'}, use_global_device_ids=true, to_apply=%region_19.20.clone | all-reduce | flops 9216 | bytes 55296
  591.1 2.6 all-reduce.20
  598.4 10.3 %add_convert_fusion = bf16[1024,768]{0,1:T(8,128)(2,1)} fusion(f32[1024,768]{0,1:T(8,128)} %copy-done.2, bf16[1024,3072]{1,0:T(8,128)(2,1)} %get-tuple-element.349, bf16[3072,768]{1,0:T(8,128)(2,1)} %all-gather.11.cloned.1.call-done, f32[768]{0:T(1024)S(1)} %convert_element_type.224), kind=kOutput, calls=%fused_computation.128 | convolution fusion | flops 4834197504 | bytes 15731712 | tf_op jit(solution)/shard_map/dot_general | solution.py:108
  610.2 19.8 %reduce-scatter.5.cloned.1.call-done = f32[48,2304]{1,0:T(8,128)} async-done(((f32[768,2304]{1,0:T(8,128)}), f32[48,2304]{1,0:T(8,128)}) %reduce-scatter.5.cloned.1.call-update) | async-done | bytes 442384 | tf_op jit(solution)/shard_map/reduce_scatter | solution.py:284
  631.8 174.0 %reduce-scatter.9.cloned.1.call-done = f32[48,3072]{1,0:T(8,128)} async-done(((f32[768,3072]{1,0:T(8,128)}), f32[48,3072]{1,0:T(8,128)}) %reduce-scatter.9.cloned.1.call-update) | async-done | bytes 589840 | tf_op jit(solution)/shard_map/reduce_scatter | solution.py:291
  807.5 173.7 %reduce-scatter.11.cloned.1.call-done = f32[192,768]{1,0:T(8,128)} async-done(((f32[3072,768]{1,0:T(8,128)}), f32[192,768]{1,0:T(8,128)}) %reduce-scatter.11.cloned.1.call-update) | async-done | bytes 589840 | tf_op jit(solution)/shard_map/reduce_scatter | solution.py:293
  983.1 3.9 fusion.123
  990.1 13.4 %all-reduce.24.cloned.1.call-done = (bf16[48,2304]{1,0:T(8,128)(2,1)}, bf16[48,768]{1,0:T(8,128)(2,1)}, bf16[48,3072]{1,0:T(8,128)(2,1)}, bf16[192,768]{1,0:T(8,128)(2,1)}) async-done(((bf16[48,2304]{1,0:T(8,128)(2,1)}, bf16[48,768]{1,0:T(8,128)(2,1)}, bf16[48,3072]{1,0:T(8,128)(2,1)}, bf16[192,768]{1,0:T(8,128)(2,1)}), (bf16[48,2304]{1,0:T(8,128)(2,1)}, bf16[48,768]{1,0:T(8,128)(2,1)}, ...) | async-done | bytes 884752 | tf_op jit(solution)/shard_map/psum | solution.py:299
  (296 shorter events, 188.0 us)
Async XLA Ops:
  7.2 96.9 %all-gather.5.cloned.1.call-start = ((), (), s32[]{:S(2)}) async-start(), calls=%async_computation.4 | async-start | bytes 3760128 | tf_op jit(solution)/shard_map/all_gather | solution.py:150
  7.9 171.7 %all-gather.7.cloned.1.call-start = ((), (), s32[]{:S(2)}) async-start(), calls=%async_computation.5 | async-start | bytes 1253376 | tf_op jit(solution)/shard_map/all_gather | solution.py:153
  8.7 216.7 %all-gather.9.cloned.1.call-start = ((), (), s32[]{:S(2)}) async-start(), calls=%async_computation.6 | async-start | bytes 5013504 | tf_op jit(solution)/shard_map/all_gather | solution.py:157
  9.4 297.8 %all-gather.11.cloned.1.call-start = ((), (), s32[]{:S(2)}) async-start(), calls=%async_computation.7 | async-start | bytes 5013504 | tf_op jit(solution)/shard_map/all_gather | solution.py:159
  10.0 598.7 %reduce-scatter.7.cloned.1.call-start = ((), (), s32[]{:S(2)}) async-start(), calls=%async_computation.9 | async-start | bytes 2506752 | tf_op jit(solution)/shard_map/reduce_scatter | solution.py:287
  99.4 4.7 copy-start.17
  99.4 4.6 copy-start.21
  99.4 2.7 copy-start.26
  99.5 2.7 copy-start.27
  99.5 3.0 copy-start.10
  101.3 78.3 %copy-start = (bf16[1024,768]{0,1:T(8,128)(2,1)}, bf16[1024,768]{0,1:T(8,128)(2,1)S(1)}, u32[]{:S(2)}) copy-start(bf16[1024,768]{0,1:T(8,128)(2,1)S(1)} %copy.109) | copy-start | bytes 4718596
  101.6 8.8 copy-start.15
  102.1 8.3 copy-start.19
  179.6 3.5 copy-start.12
  183.1 1.6 copy-start.2
  185.2 122.0 %copy-start.8 = (bf16[1024,768]{0,1:T(8,128)(2,1)S(1)}, bf16[1024,768]{0,1:T(8,128)(2,1)}, u32[]{:S(2)}) copy-start(bf16[1024,768]{0,1:T(8,128)(2,1)} %copy.118) | copy-start | bytes 4718596
  307.2 12.2 %copy-start.24 = (bf16[768,3072]{1,0:T(8,128)(2,1)S(1)}, bf16[768,3072]{1,0:T(8,128)(2,1)}, u32[]{:S(2)}) copy-start(bf16[768,3072]{1,0:T(8,128)(2,1)} %all-gather.9.cloned.1.call-done) | copy-start | bytes 14155780
  319.4 6.8 copy-start.28
  326.2 3.7 copy-start.3
  329.9 3.1 copy-start.4
  329.9 3.3 copy-start.9
  333.2 3.4 copy-start.13
  334.9 1.7 copy-start.6
  336.6 2.8 copy-start.25
  346.0 284.1 %reduce-scatter.5.cloned.1.call-start = ((), (), s32[]{:S(2)}) async-start(), calls=%async_computation.8 | async-start | bytes 7520256 | tf_op jit(solution)/shard_map/reduce_scatter | solution.py:284
  461.1 1.6 copy-start.7
  462.7 1.6 copy-start.5
  466.0 2.4 copy-start.1
  466.0 2.4 copy-start.16
  466.0 2.4 copy-start.18
  466.0 2.4 copy-start.20
  466.1 2.4 copy-start.22
  466.3 2.1 copy-start.14
  474.9 330.9 %reduce-scatter.9.cloned.1.call-start = ((), (), s32[]{:S(2)}) async-start(), calls=%async_computation.10 | async-start | bytes 10027008 | tf_op jit(solution)/shard_map/reduce_scatter | solution.py:291
  485.5 495.7 %reduce-scatter.11.cloned.1.call-start = ((), (), s32[]{:S(2)}) async-start(), calls=%async_computation.11 | async-start | bytes 10027008 | tf_op jit(solution)/shard_map/reduce_scatter | solution.py:293
  495.9 1.4 copy-start.23
  495.9 507.6 %all-reduce.24.cloned.1.call-start = ((), (), s32[]{:S(2)}) async-start(), calls=%async_computation.12 | async-start | bytes 1769472 | tf_op jit(solution)/shard_map/psum | solution.py:299
  986.9 1.6 copy-start.11
Sparse Core Ops, SparseCore 0:
  10.8 74.8 all-gather.4
  88.5 54.8 all-gather.6
  146.2 79.1 all-gather.8
  228.0 79.0 all-gather.10
  346.1 127.1 reduce-scatter.6
  479.3 150.6 reduce-scatter.4
  636.6 169.0 reduce-scatter.8
  811.4 169.7 reduce-scatter.10
  985.1 18.3 all-reduce.23
where the time goes:
time: 1030 us; the launch traced here: 1020 us
  waiting for transfers between devices  458 us (44%)
  matrix products  266 us (26%)
  blocking collectives  157 us (15%)
  local copies, waits for them, and re-layouts  78.3 us (8%)
  other arithmetic  39.8 us (4%)
  between operations  17.3 us (2%)
    reduce_scatter x1, waiting for transfers between devices, local(): lax.psum_scatter(up_grad, 'fsdp', scatter_dimension=0, tiled=True)  174 us
    reduce_scatter x1, waiting for transfers between devices, local(): lax.psum_scatter(down_grad, 'fsdp', scatter_dimension=0, tiled=True)  174 us
    unnamed x2, blocking collectives  154 us
    dot_general x1, matrix products, forward_pass(): jnp.dot(normed_two, up_weight, preferred_element_type=jnp.float32)  47.9 us
    all_gather x1, waiting for transfers between devices, local(): lax.all_gather(up_weight, 'fsdp', axis=0, tiled=True)  40.2 us
    sub x24, matrix products, head_probs(): return jax.nn.softmax(masked, axis=-1)  36.5 us
    all_gather x1, waiting for transfers between devices, local(): lax.all_gather(down_weight, 'fsdp', axis=0, tiled=True)  33.9 us
    unnamed x100, local copies, waits for them, and re-layouts  30.7 us
  transfers between devices with their start and end apart: 9, of which 6 were waited for; matrix products, arithmetic and copies ran while one was open for 33% of the time, Pallas kernels for 0%

commit v1 on v0

v1 whole, which is shorter than its diff:
```python
import functools
import math

import jax
import jax.numpy as jnp
from jax import lax
from jax.experimental import pallas as pl
from jax.experimental.pallas import tpu as pltpu
from jax.sharding import PartitionSpec as P

HEADS = 12
HEAD_DIM = 64
PATCH = 16
EPSILON = 1e-05
SQRT_HALF = 0.7071067811865476
DENSITY = 0.3989422804014327
AXES = ("dp", "fsdp")
F32 = jnp.float32
BF16 = jnp.bfloat16
LANES = 128
MEBI = 1 << 20


def grid_of(shards):
    side = math.isqrt(shards // 4)
    assert 4 * side * side == shards
    return 4, side


def arrive(value, shards, kind, step):
    depth, side = grid_of(shards)
    pairs = []
    for core in range(2):
        for z in range(depth):
            for y in range(side):
                for x in range(side):
                    to = core * shards + (z * side + y) * side + x
                    at = [core, z, y, x]
                    if kind == "core":
                        at[0] = 1 - core
                    elif kind == "z":
                        at[1] = (z + step) % depth
                    elif (kind == "first") == (core == 0):
                        at[3] = (x + step) % side
                    else:
                        at[2] = (y + step) % side
                    pairs.append((at[0] * shards + (at[1] * side + at[2]) * side + at[3], to))
    return lax.ppermute(value, AXES, pairs)


def place(shards, half):
    _, side = grid_of(shards)
    at = lax.axis_index("fsdp")
    z, y, x = at // (side * side), (at // side) % side, at % side
    first = jnp.where(half == 0, x, y)
    second = jnp.where(half == 0, y, x)
    return jnp.stack([half, z, first, second, lax.axis_index("dp")]).astype(jnp.int32)


def gather(unit, shards):
    depth, side = grid_of(shards)
    got = jnp.stack([unit] + [arrive(unit, shards, "z", s) for s in range(1, depth)])
    got = jnp.stack([got] + [arrive(got, shards, "first", s) for s in range(1, side)])
    own = [got] + [arrive(got, shards, "second", s) for s in range(1, side)]
    return own, [arrive(part, shards, "core", 1) for part in own]


def row_of(where, depth, side, rel_second, rel_first, rel_z):
    z = lax.rem(where[1] + rel_z, depth)
    first = lax.rem(where[2] + rel_first, side)
    second = lax.rem(where[3] + rel_second, side)
    y = jnp.where(where[0] == 0, second, first)
    x = jnp.where(where[0] == 0, first, second)
    return (z * side + y) * side + x


def unroll_rows(parts, where, half, depth, side):
    rel = jnp.stack(parts)
    rel = jnp.roll(rel, where[3], axis=0)
    rel = jnp.roll(rel, where[2], axis=1)
    rel = jnp.roll(rel, where[1], axis=2)
    straight = jnp.where(half == 0, rel.transpose(2, 0, 1, 3, 4), rel.transpose(2, 1, 0, 3, 4))
    return straight.reshape(-1, rel.shape[-1])


def assemble(own, other, shards, cuts):
    depth, side = grid_of(shards)
    core = lax.axis_index("dp")
    here, there = place(shards, core), place(shards, 1 - core)
    mine = unroll_rows(own, here, core, depth, side)
    theirs = unroll_rows(other, there, 1 - core, depth, side)
    wholes = []
    for start, width, split in cuts:
        left, right = mine[:, start : start + width], theirs[:, start : start + width]
        if split:
            swapped = jnp.concatenate([right, left], axis=1)
            left = jnp.where(core == 0, jnp.concatenate([left, right], axis=1), swapped)
        wholes.append(left)
    return wholes


def grad_kernel(depth, side, rows, deep, adds, where, lhs, rhs, *refs):
    got = refs[0] if adds else None
    outs, acc = refs[adds : adds + side], refs[-1]
    acc[...] = lax.dot_general(lhs[...], rhs[...], (((0,), (0,)), ((), ())), preferred_element_type=F32)
    for second in range(side):
        for first in range(side):
            for z in range(deep):
                at = row_of(where, depth, side, second, first, z)
                if deep == 1:
                    at = lax.rem(at, side * side)
                piece = acc[pl.ds(pl.multiple_of(at * rows, 16), rows), :]
                if adds:
                    piece = piece + got[second, first, z].astype(F32)
                outs[second][first, z] = piece.astype(BF16)


def rel_grad(lhs, rhs, shards, half, got=None, tile=384):
    depth, side = grid_of(shards)
    length, features = lhs.shape
    width = rhs.shape[1] // 2
    rows = features // shards
    where = place(shards, half)
    if rows % 16 != 0:
        part = lax.dynamic_slice_in_dim(rhs, half * width, width, axis=1)
        whole = lax.dot_general(lhs, part, (((0,), (0,)), ((), ())), preferred_element_type=F32)
        whole = whole.reshape(depth, side, side, rows, width)
        rel = jnp.where(half == 0, whole.transpose(1, 2, 0, 3, 4), whole.transpose(2, 1, 0, 3, 4))
        rel = jnp.roll(rel, -where[3], axis=0)
        rel = jnp.roll(rel, -where[2], axis=1)
        rel = jnp.roll(rel, -where[1], axis=2)
        if got is not None:
            rel = rel + got.astype(F32)
        return [rel[s].astype(BF16) for s in range(side)]
    deep = depth if features <= 1024 else 1
    chunk = features if deep > 1 else features // depth
    tiles = width // tile
    adds = 0 if got is None else 1
    layers = depth // deep

    def lhs_at(k, j, where):
        return (0, 0) if deep > 1 else (0, lax.rem(where[1] + k, depth))

    def rhs_at(k, j, where):
        return (0, where[0] * tiles + j)

    def out_at(k, j, where):
        return (0, k, 0, j)

    in_specs = [pl.BlockSpec((length, chunk), lhs_at), pl.BlockSpec((length, tile), rhs_at)]
    args = [lhs, rhs]
    if adds:
        in_specs.append(pl.BlockSpec((side, side, deep, rows, tile), lambda k, j, where: (0, 0, k, 0, j)))
        args.append(got)
    return pl.pallas_call(
        functools.partial(grad_kernel, depth, side, rows, deep, adds),
        grid_spec=pltpu.PrefetchScalarGridSpec(
            num_scalar_prefetch=1,
            grid=(layers, tiles),
            in_specs=in_specs,
            out_specs=[pl.BlockSpec((side, deep, rows, tile), out_at)] * side,
            scratch_shapes=[pltpu.VMEM((chunk, tile), F32)],
        ),
        out_shape=[jax.ShapeDtypeStruct((side, depth, rows, width), BF16)] * side,
        compiler_params=pltpu.CompilerParams(vmem_limit_bytes=48 * MEBI),
        cost_estimate=pl.CostEstimate(
            flops=2 * length * features * width,
            bytes_accessed=2 * (length * (features + width) + features * width * (1 + adds)),
            transcendentals=0,
        ),
        name="grad",
    )(where, *args)


def reduce_half(lhs, rhs, shards, tile=384):
    depth, side = grid_of(shards)
    core = lax.axis_index("dp")
    away = jnp.stack(rel_grad(lhs, rhs, shards, 1 - core, None, tile))
    return reduce_tail(rel_grad(lhs, rhs, shards, core, arrive(away, shards, "core", 1), tile), shards)


def reduce_tail(parts, shards):
    depth, side = grid_of(shards)
    arrived = [arrive(parts[s], shards, "second", side - s) for s in range(1, side)]
    sums = []
    for f in range(side):
        total = parts[0][f].astype(F32)
        for part in arrived:
            total = total + part[f].astype(F32)
        sums.append(total.astype(BF16))
    arrived = [arrive(sums[f], shards, "first", side - f) for f in range(1, side)]
    layers = []
    for z in range(depth):
        total = sums[0][z].astype(F32)
        for part in arrived:
            total = total + part[z].astype(F32)
        layers.append(total.astype(BF16))
    total = layers[0].astype(F32)
    for z in range(1, depth):
        total = total + arrive(layers[z], shards, "z", depth - z).astype(F32)
    return total.astype(BF16)


def both_halves(mine, shards):
    theirs = arrive(mine, shards, "core", 1)
    core = lax.axis_index("dp")
    left = jnp.where(core == 0, mine, theirs)
    right = jnp.where(core == 0, theirs, mine)
    return jnp.concatenate([left, right], axis=1).astype(F32)


def relative(whole, shards):
    depth, side = grid_of(shards)
    core = lax.axis_index("dp")
    where = place(shards, core)
    whole = whole.reshape(depth, side, side, *whole.shape[1:])
    rel = jnp.where(core == 0, whole.transpose(1, 2, 0, 3, 4), whole.transpose(2, 1, 0, 3, 4))
    rel = jnp.roll(rel, -where[3], axis=0)
    rel = jnp.roll(rel, -where[2], axis=1)
    rel = jnp.roll(rel, -where[1], axis=2)
    return [rel[s] for s in range(side)]


GAIN_ONE, SHIFT_ONE, BIAS_QUERY, BIAS_VALUE, BIAS_OUT, GAIN_TWO, SHIFT_TWO, BIAS_DOWN = range(8)
SCALE = HEAD_DIM ** (-0.5)


def weight_copies(plan, here, there, parts, outs, sems, first=0):
    copies = []
    if plan is None:
        for part, out in zip(parts, outs):
            copies.append(pltpu.make_async_copy(part, out, sems.at[first + len(copies)]))
        return copies
    depth, side, rows, cuts = plan
    for group in range(2):
        where = here if group == 0 else there
        for second in range(side):
            for ahead in range(side):
                for z in range(depth):
                    at = pl.multiple_of(row_of(where, depth, side, second, ahead, z) * rows, 16)
                    source = parts[group * side + second].at[ahead, z]
                    for (start, width, split), out in zip(cuts, outs):
                        if group == 1 and not split:
                            continue
                        column = pl.multiple_of(where[0] * width, LANES) if split else 0
                        copies.append(
                            pltpu.make_async_copy(
                                source.at[:, pl.ds(start, width)],
                                out.at[pl.ds(at, rows), pl.ds(column, width)],
                                sems.at[first + len(copies)],
                            )
                        )
    return copies


def copies_of(plan, shards, cuts):
    if plan is None:
        return len(cuts)
    return shards * sum(2 if split else 1 for _, _, split in cuts)


def standardize(values):
    average = jnp.mean(values, axis=-1, keepdims=True)
    centred = values - average
    spread = jnp.mean(centred * centred, axis=-1, keepdims=True)
    inverse = lax.rsqrt(spread + EPSILON)
    return centred * inverse, inverse


def dot(a, b, dims=((1,), (0,))):
    return lax.dot_general(a, b, (dims, ((), ())), preferred_element_type=F32)


NT = ((1,), (1,))
TN = ((0,), (0,))


def attend_kernel(plan, count, here, there, frames, tokens, *refs):
    parts = refs[:count]
    normed_ref, qkv_ref, mixed_ref, probs_ref, lines_ref = refs[count : count + 5]
    weight, small, sems = refs[count + 5 :]
    tube = pl.program_id(0)
    width = tokens.shape[1]
    length = tokens.shape[0]

    @pl.when(tube == 0)
    def _():
        copies = weight_copies(plan, here, there, parts, (weight, small), sems)
        for copy in copies:
            copy.start()
        for copy in copies:
            copy.wait()
        lines_ref[...] = small[...].astype(F32).T[: lines_ref.shape[0], :]

    standard, _ = standardize(tokens[...].astype(F32))
    normed = (standard * lines_ref[pl.ds(GAIN_ONE, 1), :] + lines_ref[pl.ds(SHIFT_ONE, 1), :]).astype(BF16)
    normed_ref[...] = normed
    bias = (lines_ref[pl.ds(BIAS_QUERY, 1), :], None, lines_ref[pl.ds(BIAS_VALUE, 1), :])
    for part in range(3):
        columns = slice(part * width, (part + 1) * width)
        project = dot(normed, weight[:, columns])
        if bias[part] is not None:
            project = project + bias[part]
        qkv_ref[:, columns] = project.astype(BF16)
    key_ok = lax.broadcasted_iota(jnp.int32, (length, length), 1) < frames[tube] * PATCH
    lower = lax.broadcasted_iota(jnp.int32, (length, LANES), 1) < HEAD_DIM
    for pair in range(width // LANES):
        query = qkv_ref[:, pair * LANES : (pair + 1) * LANES]
        keys = qkv_ref[:, width + pair * LANES : width + (pair + 1) * LANES]
        values = qkv_ref[:, 2 * width + pair * LANES : 2 * width + (pair + 1) * LANES]
        mixed = []
        for k in range(2):
            own = jnp.where(lower if k == 0 else ~lower, query, jnp.zeros_like(query))
            scores = jnp.where(key_ok, dot(own, keys, NT) * SCALE, -1e30)
            top = jnp.max(scores, axis=-1, keepdims=True)
            power = jnp.exp(scores - top)
            probs = (power * (1.0 / jnp.sum(power, axis=-1, keepdims=True))).astype(BF16)
            probs_ref[0, 2 * pair + k] = probs
            mixed.append(dot(probs, values))
        mixed_ref[:, pair * LANES : (pair + 1) * LANES] = jnp.where(lower, mixed[0], mixed[1]).astype(BF16)


def feed_kernel(plan, count, here, there, frames, tokens, mixed, cotangent, lines, up_bias, *refs):
    parts = refs[:count]
    resid_ref, normed_ref, active_ref, slope_ref, upstream_ref = refs[count : count + 5]
    out_weight, up_weight, sems = refs[count + 5 :]
    tube = pl.program_id(0)

    @pl.when(tube == 0)
    def _():
        copies = weight_copies(plan, here, there, parts, (out_weight, up_weight), sems)
        for copy in copies:
            copy.start()
        for copy in copies:
            copy.wait()

    length = tokens.shape[0]
    row_ok = lax.broadcasted_iota(jnp.int32, (length, 1), 0) < frames[tube] * PATCH
    upstream_ref[...] = jnp.where(row_ok, cotangent[...], jnp.zeros_like(cotangent))
    attended = dot(mixed[...], out_weight[...]) + lines[pl.ds(BIAS_OUT, 1), :]
    resid = tokens[...].astype(F32) + attended
    resid_ref[...] = resid
    standard, _ = standardize(resid)
    normed = (standard * lines[pl.ds(GAIN_TWO, 1), :] + lines[pl.ds(SHIFT_TWO, 1), :]).astype(BF16)
    normed_ref[...] = normed
    units = up_weight.shape[1]
    step = 512
    for at in range(0, units, step):
        hidden = dot(normed, up_weight[:, at : at + step]) + up_bias[:, at : at + step]
        bell = jnp.exp(-0.5 * hidden * hidden)
        t = 1.0 / (1.0 + (0.3275911 * SQRT_HALF) * jnp.abs(hidden))
        series = t * (
            0.254829592 + t * (-0.284496736 + t * (1.421413741 + t * (-1.453152027 + t * 1.061405429)))
        )
        tail = 0.5 * series * bell
        cumulative = jnp.where(hidden >= 0.0, 1.0 - tail, tail)
        active_ref[:, at : at + step] = (hidden * cumulative).astype(BF16)
        slope_ref[:, at : at + step] = (cumulative + hidden * (DENSITY * bell)).astype(BF16)


def norm_back(grad, standard, inverse, gain):
    scaled = grad * gain
    first = jnp.mean(scaled, axis=-1, keepdims=True)
    second = jnp.mean(scaled * standard, axis=-1, keepdims=True)
    return inverse * (scaled - first - standard * second)


def column_sum(values):
    return jnp.sum(values, axis=0, keepdims=True)


SUM_GAIN_TWO, SUM_SHIFT_TWO, SUM_BIAS_OUT, SUM_BIAS_DOWN = range(4)


def feed_back_kernel(plans, counts, here, there, upstream, slope, resid, lines, *refs):
    ff_parts, down_parts = refs[: counts[0]], refs[counts[0] : sum(counts)]
    hidden_ref, resid_grad_ref, attended_ref, mixed_ref, sums_ref, up_sum_ref = refs[sum(counts) : sum(counts) + 6]
    out_weight, up_weight, down_weight, sems = refs[sum(counts) + 6 :]
    tube = pl.program_id(0)

    @pl.when(tube == 0)
    def _():
        copies = weight_copies(plans[1], here, there, down_parts, (down_weight,), sems)
        copies += weight_copies(plans[0], here, there, ff_parts, (out_weight, up_weight), sems, len(copies))
        for copy in copies:
            copy.start()
        for copy in copies:
            copy.wait()
        sums_ref[...] = jnp.zeros_like(sums_ref)
        up_sum_ref[...] = jnp.zeros_like(up_sum_ref)

    units = up_weight.shape[1]
    step = 768
    low = upstream[...]
    normed_grad = jnp.zeros(resid.shape, F32)
    for at in range(0, units, step):
        grad = dot(low, down_weight[at : at + step, :], NT) * slope[:, at : at + step].astype(F32)
        grad = grad.astype(BF16)
        hidden_ref[:, at : at + step] = grad
        up_sum_ref[:, at : at + step] += column_sum(grad.astype(F32))
        normed_grad = normed_grad + dot(grad, up_weight[:, at : at + step], NT)
    standard, inverse = standardize(resid[...])
    above = low.astype(F32)
    resid_grad = above + norm_back(normed_grad, standard, inverse, lines[pl.ds(GAIN_TWO, 1), :])
    resid_grad_ref[...] = resid_grad
    attended_grad = resid_grad.astype(BF16)
    attended_ref[...] = attended_grad
    mixed_ref[...] = dot(attended_grad, out_weight[...], NT).astype(BF16)
    sums_ref[pl.ds(SUM_GAIN_TWO, 1), :] += column_sum(normed_grad * standard)
    sums_ref[pl.ds(SUM_SHIFT_TWO, 1), :] += column_sum(normed_grad)
    sums_ref[pl.ds(SUM_BIAS_OUT, 1), :] += column_sum(attended_grad.astype(F32))
    sums_ref[pl.ds(SUM_BIAS_DOWN, 1), :] += column_sum(above)


def attend_back_kernel(qkv, probs_ref, mixed, mixed_grad, grad_ref, sums_ref):
    tube = pl.program_id(0)

    @pl.when(tube == 0)
    def _():
        sums_ref[...] = jnp.zeros_like(sums_ref)

    length, width = mixed.shape
    lower = lax.broadcasted_iota(jnp.int32, (length, LANES), 1) < HEAD_DIM
    for pair in range(width // LANES):
        lanes = slice(pair * LANES, (pair + 1) * LANES)
        query = qkv[:, lanes]
        keys = qkv[:, width + pair * LANES : width + (pair + 1) * LANES]
        values = qkv[:, 2 * width + pair * LANES : 2 * width + (pair + 1) * LANES]
        above = mixed_grad[:, lanes]
        product = above.astype(F32) * mixed[:, lanes].astype(F32)
        query_grad, keys_grad, values_grad = [], [], []
        for k in range(2):
            mine = lower if k == 0 else ~lower
            own = jnp.where(mine, above, jnp.zeros_like(above))
            probs = probs_ref[0, 2 * pair + k]
            inner = jnp.sum(jnp.where(mine, product, 0.0), axis=-1, keepdims=True)
            probs_grad = dot(own, values, NT)
            scores_grad = (probs.astype(F32) * (probs_grad - inner)).astype(BF16)
            values_grad.append(dot(probs, above, TN))
            query_grad.append(dot(scores_grad, keys))
            keys_grad.append(dot(scores_grad, query, TN))
        for part, (pieces, scale) in enumerate(((query_grad, SCALE), (keys_grad, SCALE), (values_grad, None))):
            piece = jnp.where(lower, pieces[0], pieces[1])
            if scale is not None:
                piece = piece * scale
            piece = piece.astype(BF16)
            grad_ref[:, part * width + pair * LANES : part * width + (pair + 1) * LANES] = piece
            if part != 1:
                sums_ref[pl.ds(part // 2, 1), lanes] += column_sum(piece.astype(F32))


def first_back_kernel(plan, count, here, there, tokens, project_grad, resid_grad, lines, *refs):
    parts = refs[:count]
    tokens_ref, sums_ref = refs[count : count + 2]
    weight, small, sems = refs[count + 2 :]
    tube = pl.program_id(0)

    @pl.when(tube == 0)
    def _():
        copies = weight_copies(plan, here, there, parts, (weight, small), sems)
        for copy in copies:
            copy.start()
        for copy in copies:
            copy.wait()
        sums_ref[...] = jnp.zeros_like(sums_ref)

    grad = dot(project_grad[...], weight[...], NT)
    standard, inverse = standardize(tokens[...].astype(F32))
    inputs_grad = norm_back(grad, standard, inverse, lines[pl.ds(GAIN_ONE, 1), :])
    tokens_ref[...] = (resid_grad[...] + inputs_grad).astype(BF16)
    sums_ref[pl.ds(0, 1), :] += column_sum(grad * standard)
    sums_ref[pl.ds(1, 1), :] += column_sum(grad)


def block_out_kernel(plan, count, here, there, active, resid, lines, *refs):
    parts = refs[:count]
    out_ref = refs[count]
    weight, sems = refs[count + 1 :]

    @pl.when(pl.program_id(0) == 0)
    def _():
        copies = weight_copies(plan, here, there, parts, (weight,), sems)
        for copy in copies:
            copy.start()
        for copy in copies:
            copy.wait()

    branch = dot(active[...], weight[...]) + lines[pl.ds(BIAS_DOWN, 1), :]
    out_ref[...] = (resid[...] + branch).astype(BF16)


SMEM = pl.BlockSpec(memory_space=pltpu.SMEM)
HBM = pl.BlockSpec(memory_space=pl.ANY)


def rows_of(width, length):
    return pl.BlockSpec((length, width), lambda t: (t, 0))


def fixed(*shape):
    return pl.BlockSpec(shape, lambda t: (0,) * len(shape))


def shape_of(*shape, kind=BF16):
    return jax.ShapeDtypeStruct(shape, kind)


def call(kernel, name, grid, in_specs, outs, scratch, flops, moved, vmem, *args):
    return pl.pallas_call(
        kernel,
        grid=(grid,),
        in_specs=in_specs,
        out_specs=[spec for spec, _ in outs],
        out_shape=[shape for _, shape in outs],
        scratch_shapes=scratch,
        compiler_params=pltpu.CompilerParams(vmem_limit_bytes=vmem * MEBI),
        cost_estimate=pl.CostEstimate(flops=flops, bytes_accessed=moved, transcendentals=0),
        name=name,
    )(*args)


def local(
    tokens,
    clip_frames,
    tube_clip,
    first_gain,
    first_shift,
    qkv_weight,
    query_bias,
    value_bias,
    out_weight,
    out_bias,
    second_gain,
    second_shift,
    up_weight,
    up_bias,
    down_weight,
    down_bias,
    cotangent,
):
    shards = lax.axis_size("fsdp")
    depth, side = grid_of(shards)
    core = lax.axis_index("dp")
    here, there = place(shards, core), place(shards, 1 - core)
    total, width = tokens.shape
    tubes = tube_clip.shape[0]
    length = total // tubes
    clip_count = clip_frames.shape[0]
    matches = tube_clip[:, None] == jnp.arange(clip_count, dtype=jnp.int32)[None, :]
    frames = jnp.sum(jnp.where(matches, clip_frames[None, :], 0), axis=1)

    def half(matrix):
        columns = matrix.shape[1] // 2
        return lax.dynamic_slice_in_dim(matrix, core * columns, columns, axis=1)

    small = jnp.stack(
        [first_gain, first_shift, query_bias, value_bias, out_bias, second_gain, second_shift, down_bias],
        axis=1,
    )
    small = jnp.concatenate([small, up_bias.reshape(-1, 4)], axis=1)
    small = jnp.pad(small, ((0, 0), (0, LANES - 12)))
    wide, full, ff = qkv_weight.shape[1] // 2, out_weight.shape[1] // 2, up_weight.shape[1] // 2
    units = 2 * ff
    packs = (
        jnp.concatenate([half(qkv_weight), small], axis=1),
        jnp.concatenate([half(out_weight), half(up_weight)], axis=1),
        half(down_weight),
    )
    cuts = (
        ((0, wide, True), (wide, LANES, False)),
        ((0, full, True), (full, ff, True)),
        ((0, full, True),),
    )
    plans, parts, counts = [], [], []
    for pack, cut in zip(packs, cuts):
        own, other = gather(pack, shards)
        rows = pack.shape[0]
        if rows % 16 == 0:
            plans.append((depth, side, rows, cut))
            parts.append([*own, *other])
        else:
            plans.append(None)
            parts.append(assemble(own, other, shards, cut))
        counts.append(len(parts[-1]))
    number = [copies_of(plan, shards, cut) for plan, cut in zip(plans, cuts)]
    sem = pltpu.SemaphoreType.DMA

    normed_one, qkv, mixed, probs, lines = call(
        functools.partial(attend_kernel, plans[0], counts[0]),
        "attend",
        tubes,
        [SMEM, SMEM, SMEM, rows_of(width, length)] + [HBM] * counts[0],
        [
            (rows_of(width, length), shape_of(total, width)),
            (rows_of(3 * width, length), shape_of(total, 3 * width)),
            (rows_of(width, length), shape_of(total, width)),
            (
                pl.BlockSpec((1, HEADS, length, length), lambda t: (t, 0, 0, 0)),
                shape_of(tubes, HEADS, length, length),
            ),
            (fixed(16, width), shape_of(16, width, kind=F32)),
        ],
        [pltpu.VMEM((width, 3 * width), BF16), pltpu.VMEM((width, LANES), BF16), sem((number[0],))],
        10 * total * width * width,
        20 * MEBI,
        48,
        here, there, frames, tokens, *parts[0],
    )
    up_row = lines[8:12].T.reshape(1, units)

    resid, normed_two, active, slope, upstream = call(
        functools.partial(feed_kernel, plans[1], counts[1]),
        "feed",
        tubes,
        [SMEM, SMEM, SMEM, rows_of(width, length), rows_of(width, length), rows_of(width, length)]
        + [fixed(16, width), fixed(1, units)]
        + [HBM] * counts[1],
        [
            (rows_of(width, length), shape_of(total, width, kind=F32)),
            (rows_of(width, length), shape_of(total, width)),
            (rows_of(units, length), shape_of(total, units)),
            (rows_of(units, length), shape_of(total, units)),
            (rows_of(width, length), shape_of(total, width)),
        ],
        [pltpu.VMEM((width, width), BF16), pltpu.VMEM((width, units), BF16), sem((number[1],))],
        10 * total * width * width,
        20 * MEBI,
        48,
        here, there, frames, tokens, mixed, cotangent, lines, up_row, *parts[1],
    )

    down_half = reduce_half(active, upstream, shards)

    hidden_grad, resid_grad, attended_grad, mixed_grad, sums_two, up_sum = call(
        functools.partial(feed_back_kernel, plans[1:], counts[1:]),
        "feed_back",
        tubes,
        [SMEM, SMEM, rows_of(width, length), rows_of(units, length), rows_of(width, length), fixed(16, width)]
        + [HBM] * (counts[1] + counts[2]),
        [
            (rows_of(units, length), shape_of(total, units)),
            (rows_of(width, length), shape_of(total, width, kind=F32)),
            (rows_of(width, length), shape_of(total, width)),
            (rows_of(width, length), shape_of(total, width)),
            (fixed(8, width), shape_of(8, width, kind=F32)),
            (fixed(1, units), shape_of(1, units, kind=F32)),
        ],
        [
            pltpu.VMEM((width, width), BF16),
            pltpu.VMEM((width, units), BF16),
            pltpu.VMEM((units, width), BF16),
            sem((number[1] + number[2],)),
        ],
        18 * total * width * width,
        30 * MEBI,
        52,
        here, there, upstream, slope, resid, lines, *parts[1], *parts[2],
    )
    up_half = reduce_half(normed_two, hidden_grad, shards)
    out_half = reduce_half(mixed, attended_grad, shards)

    project_grad, sums_heads = call(
        attend_back_kernel,
        "attend_back",
        tubes,
        [
            rows_of(3 * width, length),
            pl.BlockSpec((1, HEADS, length, length), lambda t: (t, 0, 0, 0)),
            rows_of(width, length),
            rows_of(width, length),
        ],
        [
            (rows_of(3 * width, length), shape_of(total, 3 * width)),
            (fixed(8, width), shape_of(8, width, kind=F32)),
        ],
        [],
        10 * total * width * width,
        20 * MEBI,
        40,
        qkv, probs, mixed, mixed_grad,
    )
    qkv_half = reduce_half(normed_one, project_grad, shards)

    tokens_grad, sums_one = call(
        functools.partial(first_back_kernel, plans[0], counts[0]),
        "first_back",
        tubes,
        [SMEM, SMEM, rows_of(width, length), rows_of(3 * width, length), rows_of(width, length)]
        + [fixed(16, width)]
        + [HBM] * counts[0],
        [
            (rows_of(width, length), shape_of(total, width)),
            (fixed(8, width), shape_of(8, width, kind=F32)),
        ],
        [pltpu.VMEM((width, 3 * width), BF16), pltpu.VMEM((width, LANES), BF16), sem((number[0],))],
        6 * total * width * width,
        14 * MEBI,
        40,
        here, there, tokens, project_grad, resid_grad, lines, *parts[0],
    )
    (block_out,) = call(
        functools.partial(block_out_kernel, plans[2], counts[2]),
        "block_out",
        tubes,
        [SMEM, SMEM, rows_of(units, length), rows_of(width, length), fixed(16, width)] + [HBM] * counts[2],
        [(rows_of(width, length), shape_of(total, width))],
        [pltpu.VMEM((units, width), BF16), sem((number[2],))],
        8 * total * width * width,
        16 * MEBI,
        40,
        here, there, active, resid, lines, *parts[2],
    )

    vectors = (
        sums_one[0], sums_one[1], sums_heads[0], sums_heads[1], sums_two[SUM_BIAS_OUT],
        sums_two[SUM_GAIN_TWO], sums_two[SUM_SHIFT_TWO], sums_two[SUM_BIAS_DOWN], up_sum[0],
    )
    packed = jnp.concatenate([v.reshape(shards, -1) for v in vectors], axis=1).astype(BF16)
    packed = (packed.astype(F32) + arrive(packed, shards, "core", 1).astype(F32)).astype(BF16)
    small_sum = reduce_tail(relative(packed[:, None, :], shards), shards)[0].astype(F32)
    rows = first_gain.shape[0]
    pieces = [small_sum[k * rows : (k + 1) * rows] for k in range(8)] + [small_sum[8 * rows :]]
    return (
        block_out,
        tokens_grad,
        pieces[0],
        pieces[1],
        both_halves(qkv_half, shards),
        pieces[2],
        pieces[3],
        both_halves(out_half, shards),
        pieces[4],
        pieces[5],
        pieces[6],
        both_halves(up_half, shards),
        pieces[8],
        both_halves(down_half, shards),
        pieces[7],
    )


def solution(mesh):
    return jax.shard_map(
        local,
        mesh=mesh,
        in_specs=(
            P(("dp", "fsdp"), None),
            P(),
            P(("dp", "fsdp")),
            P("fsdp"),
            P("fsdp"),
            P("fsdp", None),
            P("fsdp"),
            P("fsdp"),
            P("fsdp", None),
            P("fsdp"),
            P("fsdp"),
            P("fsdp"),
            P("fsdp", None),
            P("fsdp"),
            P("fsdp", None),
            P("fsdp"),
            P(("dp", "fsdp"), None),
        ),
        out_specs=(
            P(("dp", "fsdp"), None),
            P(("dp", "fsdp"), None),
            P("fsdp"),
            P("fsdp"),
            P("fsdp", None),
            P("fsdp"),
            P("fsdp"),
            P("fsdp", None),
            P("fsdp"),
            P("fsdp"),
            P("fsdp"),
            P("fsdp", None),
            P("fsdp"),
            P("fsdp", None),
            P("fsdp"),
        ),
        check_vma=False,
    )
```

time: 1030 us -> 346 us (0.34); the launches traced: 1020 us -> 345 us
  waiting for transfers between devices: 458 us -> 93.5 us
  matrix products: 266 us -> 0 us
  blocking collectives: 157 us -> 0 us
  Pallas kernels: 0 us -> 141 us
  starting transfers between devices: 0.36 us -> 64.4 us
  local copies, waits for them, and re-layouts: 78.3 us -> 30.6 us
  other arithmetic: 39.8 us -> 14.5 us
  between operations: 17.3 us -> 1.4 us
    reduce_scatter x4 -> x0, waiting for transfers between devices: 367 us -> none  [the longest x1 174 us: local(): lax.psum_scatter(up_grad, 'fsdp', scatter_dimension=0, tiled=True)]
    dot_general x72 -> x0, matrix products: 229 us -> none  [the longest x1 47.9 us: forward_pass(): jnp.dot(normed_two, up_weight, preferred_element_type=jnp.float32)]
    unnamed x2 -> x0, blocking collectives: 154 us -> none
    pallas_call x0 -> x14, Pallas kernels: none -> 141 us  [the longest x6 97.5 us: call(): pl.pallas_call(kernel, grid=(grid,), in_specs=in_specs, out_specs=[spec f...]
    ppermute x0 -> x55, waiting for transfers between devices: none -> 93.5 us  [arrive(): return lax.ppermute(value, AXES, pairs)]
    all_gather x4 -> x0, waiting for transfers between devices: 74.1 us -> none  [the longest x1 40.2 us: local(): lax.all_gather(up_weight, 'fsdp', axis=0, tiled=True)]
    ppermute x0 -> x55, starting transfers between devices: none -> 64.4 us  [arrive(): return lax.ppermute(value, AXES, pairs)]
    sub x24 -> x0, matrix products: 36.5 us -> none  [head_probs(): return jax.nn.softmax(masked, axis=-1)]
  transfers between devices with their start and end apart: 9 -> 55, of which waited for: 6 -> 20; matrix products, arithmetic and copies ran while one was open for 33% -> 7% of each run, Pallas kernels for 0% -> 28%
where the time goes in v1:
time: 346 us; the launch traced here: 345 us
  Pallas kernels  141 us (41%)
  waiting for transfers between devices  93.5 us (27%)
  starting transfers between devices  64.4 us (19%)
  local copies, waits for them, and re-layouts  30.6 us (9%)
  other arithmetic  14.5 us (4%)
    pallas_call x6, Pallas kernels, call(): pl.pallas_call(kernel, grid=(grid,), in_specs=in_specs, out_specs=[spec f...  97.5 us
    ppermute x55, waiting for transfers between devices, arrive(): return lax.ppermute(value, AXES, pairs)  93.5 us
    ppermute x55, starting transfers between devices, arrive(): return lax.ppermute(value, AXES, pairs)  64.4 us
    pallas_call x8, Pallas kernels, rel_grad(): pl.pallas_call(functools.partial(grad_kernel, depth, side, rows, deep, ad...  43 us
    unnamed x57, local copies, waits for them, and re-layouts  18.1 us
    another operation x4, other arithmetic, reduce_half(): away = jnp.stack(rel_grad(lhs, rhs, shards, 1 - core, None, tile))  7.3 us
  transfers between devices with their start and end apart: 55, of which 20 were waited for; matrix products, arithmetic and copies ran while one was open for 7% of the time, Pallas kernels for 28%

profile of v1, /device:TPU:0, one launch (start us, length us, event | category | flops | bytes accessed | tf_op | source)
XLA Modules:
  0.0 344.9 jit_solution(9796388812298063039)
XLA Ops:
  2.4 4.1 %collective-permute-start.8 = (bf16[48,1920]{1,0:T(8,128)(2,1)S(1)}, bf16[48,1920]{1,0:T(8,128)(2,1)S(1)}, u32[]{:S(2)}, u32[]{:S(2)}) collective-permute-start(bf16[48,1920]{1,0:T(8,128)(2,1)S(1)} %get-tuple-element.128), channel_id=1, source_target_pairs={{8,0},{9,1},{10,2},{11,3},{12,4},{13,5},{14,6},{15,7},{0,8},{1,9},... | collective-permute-start | bytes 552968 | tf_op jit(solution)/shard_map/ppermute | solution.py:48
  16.8 3.5 %collective-permute-done.9 = bf16[48,1920]{1,0:T(8,128)(2,1)S(1)} collective-permute-done((bf16[48,1920]{1,0:T(8,128)(2,1)S(1)}, bf16[48,1920]{1,0:T(8,128)(2,1)S(1)}, u32[]{:S(2)}, u32[]{:S(2)}) %collective-permute-start.9) | collective-permute-done | bytes 184352 | tf_op jit(solution)/shard_map/ppermute | solution.py:48
  22.0 5.5 %collective-permute-start.1 = (bf16[48,1280]{1,0:T(8,128)(2,1)S(1)}, bf16[48,1280]{1,0:T(8,128)(2,1)S(1)}, u32[]{:S(2)}, u32[]{:S(2)}) collective-permute-start(bf16[48,1280]{1,0:T(8,128)(2,1)S(1)} %get-tuple-element.130), channel_id=1, source_target_pairs={{8,0},{9,1},{10,2},{11,3},{12,4},{13,5},{14,6},{15,7},{0,8},{1,9},... | collective-permute-start | bytes 368648 | tf_op jit(solution)/shard_map/ppermute | solution.py:48
  29.5 6.8 %collective-permute-done.1 = bf16[48,1280]{1,0:T(8,128)(2,1)S(1)} collective-permute-done((bf16[48,1280]{1,0:T(8,128)(2,1)S(1)}, bf16[48,1280]{1,0:T(8,128)(2,1)S(1)}, u32[]{:S(2)}, u32[]{:S(2)}) %collective-permute-start.1) | collective-permute-done | bytes 122912 | tf_op jit(solution)/shard_map/ppermute | solution.py:48
  40.4 2.9 collective-permute-start.14
  44.1 4.2 %collective-permute-done.3 = bf16[4,48,1280]{2,1,0:T(8,128)(2,1)S(1)} collective-permute-done((bf16[4,48,1280]{2,1,0:T(8,128)(2,1)S(1)}, bf16[4,48,1280]{2,1,0:T(8,128)(2,1)S(1)}, u32[]{:S(2)}, u32[]{:S(2)}) %collective-permute-start.3) | collective-permute-done | bytes 491552 | tf_op jit(solution)/shard_map/ppermute | solution.py:48
  49.7 2.3 collective-permute-done.16
  52.2 1.7 collective-permute-start.17
  53.8 14.7 %collective-permute-done.17 = bf16[4,192,384]{2,1,0:T(8,128)(2,1)S(1)} collective-permute-done((bf16[4,192,384]{2,1,0:T(8,128)(2,1)S(1)}, bf16[4,192,384]{2,1,0:T(8,128)(2,1)S(1)}, u32[]{:S(2)}, u32[]{:S(2)}) %collective-permute-start.17) | collective-permute-done | bytes 589856 | tf_op jit(solution)/shard_map/ppermute | solution.py:48
  69.6 1.6 collective-permute-start.18
  71.3 8.6 %collective-permute-done.4.refs_1_ = bf16[2,4,48,1280]{3,2,1,0:T(8,128)(2,1)} collective-permute-done((bf16[2,4,48,1280]{3,2,1,0:T(8,128)(2,1)S(1)}, bf16[2,4,48,1280]{3,2,1,0:T(8,128)(2,1)}, u32[]{:S(2)}, u32[]{:S(2)}) %collective-permute-start.4) | collective-permute-done | bytes 983072 | tf_op jit(solution)/shard_map/ppermute | solution.py:48
  81.3 11.2 %collective-permute-done.18.refs_1_.refs_5_ = bf16[2,4,192,384]{3,2,1,0:T(8,128)(2,1)} collective-permute-done((bf16[2,4,192,384]{3,2,1,0:T(8,128)(2,1)}, bf16[2,4,192,384]{3,2,1,0:T(8,128)(2,1)}, u32[]{:S(2)}, u32[]{:S(2)}) %collective-permute-start.18) | collective-permute-done | bytes 1179680 | tf_op jit(solution)/shard_map/ppermute | solution.py:48
  92.5 18.3 %attend.1 = (bf16[1024,768]{1,0:T(8,128)(2,1)S(1)}, bf16[1024,2304]{1,0:T(8,128)(2,1)}, bf16[1024,768]{1,0:T(8,128)(2,1)}, bf16[4,12,256,256]{3,2,1,0:T(8,128)(2,1)}, f32[16,768]{1,0:T(8,128)S(1)}) custom-call(s32[5]{0:T(128)S(1)} %stack.214.here.where, s32[5]{0:T(128)S(1)} %stack.218.there.where, s32[4]{0:T(128)S(1)} %select_reduce_fusion.frames, ...), custom_call_target="tpu_custom_call" | custom-call | flops 6039797760 | bytes 20971520 | tf_op jit(solution)/shard_map/attend/pallas_call | solution.py:509
  112.5 25.5 %feed.1 = (f32[1024,768]{1,0:T(8,128)}, bf16[1024,768]{1,0:T(8,128)(2,1)}, bf16[1024,3072]{1,0:T(8,128)(2,1)}, bf16[1024,3072]{1,0:T(8,128)(2,1)}, bf16[1024,768]{1,0:T(8,128)(2,1)}) custom-call(s32[5]{0:T(128)S(1)} %stack.214.here.where, s32[5]{0:T(128)S(1)} %stack.218.there.where, s32[4]{0:T(128)S(1)} %select_reduce_fusion.frames, ...), custom_call_target="tpu_custom_call" | custom-call | flops 6039797760 | bytes 20971520 | tf_op jit(solution)/shard_map/feed/pallas_call | solution.py:509
  138.1 22.6 %feed_back.1 = (bf16[1024,3072]{1,0:T(8,128)(2,1)}, f32[1024,768]{1,0:T(8,128)}, bf16[1024,768]{1,0:T(8,128)(2,1)}, bf16[1024,768]{1,0:T(8,128)(2,1)}, f32[8,768]{1,0:T(8,128)S(1)}, /*index=5*/f32[1,3072]{1,0:T(1,128)S(1)}) custom-call(s32[5]{0:T(128)S(1)} %stack.214.here.where, s32[5]{0:T(128)S(1)} %stack.218.there.where, ...), custom_call_target="tpu_custom_call" | custom-call | flops 10871635968 | bytes 31457280 | tf_op jit(solution)/shard_map/feed_back/pallas_call | solution.py:509
  162.2 11.9 %attend_back.1 = (bf16[1024,2304]{1,0:T(8,128)(2,1)S(1)}, f32[8,768]{1,0:T(8,128)S(1)}) custom-call(bf16[1024,2304]{1,0:T(8,128)(2,1)S(1)} %bitcast.265, bf16[4,12,256,256]{3,2,1,0:T(8,128)(2,1)} %get-tuple-element.56.probs_ref, bf16[1024,768]{1,0:T(8,128)(2,1)S(1)} %copy-done.5, bf16[1024,768]{1,0:T(8,128)(2,1)S(1)} %copy-done.22), custom_call_target="tpu_custom_call" | custom-call | flops 6039797760 | bytes 20971520 | tf_op jit(solution)/shard_map/attend_back/pallas_call | solution.py:509
  174.1 2.1 copy-done.2
  176.5 2.3 copy-done.3
  180.1 1.9 copy-done.9
  183.4 9.5 %first_back.1 = (bf16[1024,768]{1,0:T(8,128)(2,1)}, f32[8,768]{1,0:T(8,128)S(1)}) custom-call(s32[5]{0:T(128)S(1)} %stack.214.here.where, s32[5]{0:T(128)S(1)} %stack.218.there.where, bf16[1024,768]{1,0:T(8,128)(2,1)S(1)} %copy-done.14, bf16[1024,2304]{1,0:T(8,128)(2,1)S(1)} %copy-done.3, f32[1024,768]{1,0:T(8,128)S(1)} %copy-done.9, ...), custom_call_target="tpu_custom_call" | custom-call | flops 3623878656 | bytes 14680064 | tf_op jit(solution)/shard_map/first_back/pallas_call | solution.py:509
  194.2 1.6 grad.10
  196.8 5.2 %grad.8 = (bf16[2,4,48,1152]{3,2,1,0:T(8,128)(2,1)S(1)}, bf16[2,4,48,1152]{3,2,1,0:T(8,128)(2,1)S(1)}) custom-call(s32[5]{0:T(128)S(1)} %stack.218.there.where, bf16[1024,768]{1,0:T(8,128)(2,1)S(1)} %copy-done.16, bf16[1024,2304]{1,0:T(8,128)(2,1)} %copy-done.2), custom_call_target="tpu_custom_call" | custom-call | flops 1811939328 | bytes 5701632 | tf_op jit(solution)/shard_map/grad/pallas_call | solution.py:155
  204.0 7.3 %grad.14 = (bf16[2,4,192,384]{3,2,1,0:T(8,128)(2,1)S(1)}, bf16[2,4,192,384]{3,2,1,0:T(8,128)(2,1)S(1)}) custom-call(s32[5]{0:T(128)S(1)} %stack.218.there.where, bf16[1024,3072]{1,0:T(8,128)(2,1)} %get-tuple-element.53.active.lhs, bf16[1024,768]{1,0:T(8,128)(2,1)S(1)} %copy-done.12), custom_call_target="tpu_custom_call" | custom-call | flops 2415919104 | bytes 9437184 | tf_op jit(solution)/shard_map/grad/pallas_call | solution.py:155
  211.3 1.7 pad_maximum_fusion.1
  213.5 6.4 %grad.12 = (bf16[2,4,48,1536]{3,2,1,0:T(8,128)(2,1)S(1)}, bf16[2,4,48,1536]{3,2,1,0:T(8,128)(2,1)S(1)}) custom-call(s32[5]{0:T(128)S(1)} %stack.218.there.where, bf16[1024,768]{1,0:T(8,128)(2,1)S(1)} %copy-done.10, bf16[1024,3072]{1,0:T(8,128)(2,1)} %get-tuple-element.78.rhs), custom_call_target="tpu_custom_call" | custom-call | flops 2415919104 | bytes 7077888 | tf_op jit(solution)/shard_map/grad/pallas_call | solution.py:155
  223.0 3.3 pad_maximum_fusion
  227.7 2.7 grad.11
  231.3 2.8 copy-done.4
  234.1 9.7 %block_out.1 = bf16[1024,768]{1,0:T(8,128)(2,1)} custom-call(s32[5]{0:T(128)S(1)} %stack.214.here.where, s32[5]{0:T(128)S(1)} %stack.218.there.where, bf16[1024,3072]{1,0:T(8,128)(2,1)S(1)} %copy-done.4, f32[1024,768]{1,0:T(8,128)S(1)} %copy-done.21, f32[16,768]{1,0:T(8,128)S(1)} %get-tuple-element.52.lines, ...), custom_call_target="tpu_custom_call" | custom-call | flops 4831838208 | bytes 16777216 | tf_op jit(solution)/shard_map/block_out/pallas_call | solution.py:509
  245.2 2.6 collective-permute-start.26
  249.3 5.6 %grad.9 = (bf16[2,4,48,1152]{3,2,1,0:T(8,128)(2,1)S(1)}, bf16[2,4,48,1152]{3,2,1,0:T(8,128)(2,1)S(1)}) custom-call(s32[5]{0:T(128)S(1)} %stack.214.here.where, bf16[1024,768]{1,0:T(8,128)(2,1)S(1)} %copy-done.17, bf16[1024,2304]{1,0:T(8,128)(2,1)} %copy-done.2, bf16[2,2,4,48,1152]{4,3,2,1,0:T(8,128)(2,1)} %collective-permute-done.27.refs_0_), custom_call_target="tpu_custom_call" | custom-call | flops 1811939328 | bytes 7471104 | tf_op jit(solution)/shard_map/grad/pallas_call | solution.py:155
  256.1 2.1 collective-permute-start.37
  259.8 1.7 collective-permute-start.39
  264.4 2.5 collective-permute-done.38
  267.0 1.6 collective-permute-done.28
  269.5 7.5 %grad.15 = (bf16[2,4,192,384]{3,2,1,0:T(8,128)(2,1)S(1)}, bf16[2,4,192,384]{3,2,1,0:T(8,128)(2,1)S(1)}) custom-call(s32[5]{0:T(128)S(1)} %stack.214.here.where, bf16[1024,3072]{1,0:T(8,128)(2,1)} %get-tuple-element.53.active.lhs, bf16[1024,768]{1,0:T(8,128)(2,1)S(1)} %copy-done.13, bf16[2,2,4,192,384]{4,3,2,1,0:T(8,128)(2,1)} %collective-permute-done.48.refs_0_), custom_call_target="tpu_custom_call" | custom-call | flops 2415919104 | bytes 11796480 | tf_op jit(solution)/shard_map/grad/pallas_call | solution.py:155
  278.3 2.1 collective-permute-start.30
  280.4 1.8 collective-permute-start.32
  284.3 6.8 %grad.13 = (bf16[2,4,48,1536]{3,2,1,0:T(8,128)(2,1)S(1)}, bf16[2,4,48,1536]{3,2,1,0:T(8,128)(2,1)S(1)}) custom-call(s32[5]{0:T(128)S(1)} %stack.214.here.where, bf16[1024,768]{1,0:T(8,128)(2,1)S(1)} %copy-done.11, bf16[1024,3072]{1,0:T(8,128)(2,1)} %get-tuple-element.78.rhs, bf16[2,2,4,48,1536]{4,3,2,1,0:T(8,128)(2,1)} %copy-done.23), custom_call_target="tpu_custom_call" | custom-call | flops 2415919104 | bytes 9437184 | tf_op jit(solution)/shard_map/grad/pallas_call | solution.py:155
  295.3 18.4 %collective-permute-done.42 = bf16[2,4,48,1536]{3,2,1,0:T(8,128)(2,1)S(1)} collective-permute-done((bf16[2,4,48,1536]{3,2,1,0:T(8,128)(2,1)S(1)}, bf16[2,4,48,1536]{3,2,1,0:T(8,128)(2,1)S(1)}, u32[]{:S(2)}, u32[]{:S(2)}) %collective-permute-start.42) | collective-permute-done | bytes 1179680 | tf_op jit(solution)/shard_map/ppermute | solution.py:48
  315.8 2.3 collective-permute-start.51
  318.1 2.1 collective-permute-start.53
  320.7 3.2 collective-permute-done.43
  324.1 1.6 collective-permute-start.44
  325.7 2.2 collective-permute-start.46
  328.0 3.3 collective-permute-start.45
  331.3 6.6 %collective-permute-done.52 = bf16[192,384]{1,0:T(8,128)(2,1)S(1)} collective-permute-done((bf16[192,384]{1,0:T(8,128)(2,1)S(1)}, bf16[192,384]{1,0:T(8,128)(2,1)S(1)}, u32[]{:S(2)}, u32[]{:S(2)}) %collective-permute-start.52) | collective-permute-done | bytes 147488 | tf_op jit(solution)/shard_map/ppermute | solution.py:48
  338.1 4.4 %collective-permute-done.45 = bf16[48,1536]{1,0:T(8,128)(2,1)S(1)} collective-permute-done((bf16[48,1536]{1,0:T(8,128)(2,1)S(1)}, bf16[48,1536]{1,0:T(8,128)(2,1)S(1)}, u32[]{:S(2)}, u32[]{:S(2)}) %collective-permute-start.45) | collective-permute-done | bytes 147488 | tf_op jit(solution)/shard_map/ppermute | solution.py:48
  (217 shorter events, 63.2 us)
Async XLA Ops:
  2.4 14.3 %collective-permute-start.8 = (bf16[48,1920]{1,0:T(8,128)(2,1)S(1)}, bf16[48,1920]{1,0:T(8,128)(2,1)S(1)}, u32[]{:S(2)}, u32[]{:S(2)}) collective-permute-start(bf16[48,1920]{1,0:T(8,128)(2,1)S(1)} %get-tuple-element.128), channel_id=1, source_target_pairs={{8,0},{9,1},{10,2},{11,3},{12,4},{13,5},{14,6},{15,7},{0,8},{1,9},... | collective-permute-start | bytes 552968 | tf_op jit(solution)/shard_map/ppermute | solution.py:48
  6.5 10.2 %collective-permute-start.7 = (bf16[48,1920]{1,0:T(8,128)(2,1)S(1)}, bf16[48,1920]{1,0:T(8,128)(2,1)S(1)}, u32[]{:S(2)}, u32[]{:S(2)}) collective-permute-start(bf16[48,1920]{1,0:T(8,128)(2,1)S(1)} %get-tuple-element.128), channel_id=1, source_target_pairs={{4,0},{5,1},{6,2},{7,3},{8,4},{9,5},{10,6},{11,7},{12,8},{13,9},{1... | collective-permute-start | bytes 552968 | tf_op jit(solution)/shard_map/ppermute | solution.py:48
  7.9 12.4 %collective-permute-start.9 = (bf16[48,1920]{1,0:T(8,128)(2,1)S(1)}, bf16[48,1920]{1,0:T(8,128)(2,1)S(1)}, u32[]{:S(2)}, u32[]{:S(2)}) collective-permute-start(bf16[48,1920]{1,0:T(8,128)(2,1)S(1)} %get-tuple-element.128), channel_id=1, source_target_pairs={{12,0},{13,1},{14,2},{15,3},{0,4},{1,5},{2,6},{3,7},{4,8},{5,9},{6... | collective-permute-start | bytes 552968 | tf_op jit(solution)/shard_map/ppermute | solution.py:48
  20.4 22.9 %collective-permute-start.10 = (bf16[4,48,1920]{2,1,0:T(8,128)(2,1)S(1)}, bf16[4,48,1920]{2,1,0:T(8,128)(2,1)S(1)}, u32[]{:S(2)}, u32[]{:S(2)}) collective-permute-start(bf16[4,48,1920]{2,1,0:T(8,128)(2,1)S(1)} %get-tuple-element.111), channel_id=1, source_target_pairs={{1,0},{0,1},{3,2},{2,3},{5,4},{4,5},{7,6},{6,7},{9,8},{8,9},{11,10... | collective-permute-start | bytes 2211848 | tf_op jit(solution)/shard_map/ppermute | solution.py:48
  22.0 14.3 %collective-permute-start.1 = (bf16[48,1280]{1,0:T(8,128)(2,1)S(1)}, bf16[48,1280]{1,0:T(8,128)(2,1)S(1)}, u32[]{:S(2)}, u32[]{:S(2)}) collective-permute-start(bf16[48,1280]{1,0:T(8,128)(2,1)S(1)} %get-tuple-element.130), channel_id=1, source_target_pairs={{8,0},{9,1},{10,2},{11,3},{12,4},{13,5},{14,6},{15,7},{0,8},{1,9},... | collective-permute-start | bytes 368648 | tf_op jit(solution)/shard_map/ppermute | solution.py:48
  27.5 9.7 %collective-permute-start = (bf16[48,1280]{1,0:T(8,128)(2,1)S(1)}, bf16[48,1280]{1,0:T(8,128)(2,1)S(1)}, u32[]{:S(2)}, u32[]{:S(2)}) collective-permute-start(bf16[48,1280]{1,0:T(8,128)(2,1)S(1)} %get-tuple-element.130), channel_id=1, source_target_pairs={{4,0},{5,1},{6,2},{7,3},{8,4},{9,5},{10,6},{11,7},{12,8},{13,9},{1... | collective-permute-start | bytes 368648 | tf_op jit(solution)/shard_map/ppermute | solution.py:48
  27.9 9.3 %collective-permute-start.2 = (bf16[48,1280]{1,0:T(8,128)(2,1)S(1)}, bf16[48,1280]{1,0:T(8,128)(2,1)S(1)}, u32[]{:S(2)}, u32[]{:S(2)}) collective-permute-start(bf16[48,1280]{1,0:T(8,128)(2,1)S(1)} %get-tuple-element.130), channel_id=1, source_target_pairs={{12,0},{13,1},{14,2},{15,3},{0,4},{1,5},{2,6},{3,7},{4,8},{5,9},{6... | collective-permute-start | bytes 368648 | tf_op jit(solution)/shard_map/ppermute | solution.py:48
  37.3 11.0 %collective-permute-start.3 = (bf16[4,48,1280]{2,1,0:T(8,128)(2,1)S(1)}, bf16[4,48,1280]{2,1,0:T(8,128)(2,1)S(1)}, u32[]{:S(2)}, u32[]{:S(2)}) collective-permute-start(bf16[4,48,1280]{2,1,0:T(8,128)(2,1)S(1)} %get-tuple-element.117), channel_id=1, source_target_pairs={{1,0},{0,1},{3,2},{2,3},{5,4},{4,5},{7,6},{6,7},{9,8},{8,9},{11,10... | collective-permute-start | bytes 1474568 | tf_op jit(solution)/shard_map/ppermute | solution.py:48
  38.9 10.9 %collective-permute-start.15 = (bf16[192,384]{1,0:T(8,128)(2,1)S(1)}, bf16[192,384]{1,0:T(8,128)(2,1)S(1)}, u32[]{:S(2)}, u32[]{:S(2)}) collective-permute-start(bf16[192,384]{1,0:T(8,128)(2,1)S(1)} %constant_dynamic-slice_fusion), channel_id=1, source_target_pairs={{8,0},{9,1},{10,2},{11,3},{12,4},{13,5},{14,6},{15,7},{0,8},{1,9},... | collective-permute-start | bytes 442376 | tf_op jit(solution)/shard_map/ppermute | solution.py:48
  40.4 9.3 %collective-permute-start.14 = (bf16[192,384]{1,0:T(8,128)(2,1)S(1)}, bf16[192,384]{1,0:T(8,128)(2,1)S(1)}, u32[]{:S(2)}, u32[]{:S(2)}) collective-permute-start(bf16[192,384]{1,0:T(8,128)(2,1)S(1)} %constant_dynamic-slice_fusion), channel_id=1, source_target_pairs={{4,0},{5,1},{6,2},{7,3},{8,4},{9,5},{10,6},{11,7},{12,8},{13,9},{1... | collective-permute-start | bytes 442376 | tf_op jit(solution)/shard_map/ppermute | solution.py:48
  43.3 8.7 %collective-permute-start.16 = (bf16[192,384]{1,0:T(8,128)(2,1)S(1)}, bf16[192,384]{1,0:T(8,128)(2,1)S(1)}, u32[]{:S(2)}, u32[]{:S(2)}) collective-permute-start(bf16[192,384]{1,0:T(8,128)(2,1)S(1)} %constant_dynamic-slice_fusion), channel_id=1, source_target_pairs={{12,0},{13,1},{14,2},{15,3},{0,4},{1,5},{2,6},{3,7},{4,8},{5,9},{6... | collective-permute-start | bytes 442376 | tf_op jit(solution)/shard_map/ppermute | solution.py:48
  43.5 36.9 %collective-permute-start.11 = (bf16[2,4,48,1920]{3,2,1,0:T(8,128)(2,1)S(1)}, bf16[2,4,48,1920]{3,2,1,0:T(8,128)(2,1)}, u32[]{:S(2)}, u32[]{:S(2)}) collective-permute-start(bf16[2,4,48,1920]{3,2,1,0:T(8,128)(2,1)S(1)} %pad_maximum_fusion.3.refs_0_), channel_id=1, source_target_pairs={{2,0},{3,1},{0,2},{1,3},{6,4},{7,5},{4,6},{5,7},{10,8},{11,9},{8,1... | collective-permute-start | bytes 4423688 | tf_op jit(solution)/shard_map/ppermute | solution.py:48
  48.4 31.5 %collective-permute-start.4 = (bf16[2,4,48,1280]{3,2,1,0:T(8,128)(2,1)S(1)}, bf16[2,4,48,1280]{3,2,1,0:T(8,128)(2,1)}, u32[]{:S(2)}, u32[]{:S(2)}) collective-permute-start(bf16[2,4,48,1280]{3,2,1,0:T(8,128)(2,1)S(1)} %pad_maximum_fusion.5.refs_0_), channel_id=1, source_target_pairs={{2,0},{3,1},{0,2},{1,3},{6,4},{7,5},{4,6},{5,7},{10,8},{11,9},{8,1... | collective-permute-start | bytes 2949128 | tf_op jit(solution)/shard_map/ppermute | solution.py:48
  52.2 16.3 %collective-permute-start.17 = (bf16[4,192,384]{2,1,0:T(8,128)(2,1)S(1)}, bf16[4,192,384]{2,1,0:T(8,128)(2,1)S(1)}, u32[]{:S(2)}, u32[]{:S(2)}) collective-permute-start(bf16[4,192,384]{2,1,0:T(8,128)(2,1)S(1)} %get-tuple-element.115), channel_id=1, source_target_pairs={{1,0},{0,1},{3,2},{2,3},{5,4},{4,5},{7,6},{6,7},{9,8},{8,9},{11,10... | collective-permute-start | bytes 1769480 | tf_op jit(solution)/shard_map/ppermute | solution.py:48
  69.6 22.9 %collective-permute-start.18 = (bf16[2,4,192,384]{3,2,1,0:T(8,128)(2,1)}, bf16[2,4,192,384]{3,2,1,0:T(8,128)(2,1)}, u32[]{:S(2)}, u32[]{:S(2)}) collective-permute-start(bf16[2,4,192,384]{3,2,1,0:T(8,128)(2,1)} %pad_maximum_fusion.4.refs_0_.refs_4_), channel_id=1, source_target_pairs={{2,0},{3,1},{0,2},{1,3},{6,4},{7,5},{4,6},{5,7},{10,8},{11,9},{8,1... | collective-permute-start | bytes 3538952 | tf_op jit(solution)/shard_map/ppermute | solution.py:48
  71.3 9.5 %collective-permute-start.5 = (bf16[2,4,48,1280]{3,2,1,0:T(8,128)(2,1)S(1)}, bf16[2,4,48,1280]{3,2,1,0:T(8,128)(2,1)}, u32[]{:S(2)}, u32[]{:S(2)}) collective-permute-start(bf16[2,4,48,1280]{3,2,1,0:T(8,128)(2,1)S(1)} %pad_maximum_fusion.5.refs_0_), channel_id=1, source_target_pairs={{16,0},{17,1},{18,2},{19,3},{20,4},{21,5},{22,6},{23,7},{24,8},{25... | collective-permute-start | bytes 2949128 | tf_op jit(solution)/shard_map/ppermute | solution.py:48
  79.9 12.6 %collective-permute-start.6 = (bf16[2,4,48,1280]{3,2,1,0:T(8,128)(2,1)}, bf16[2,4,48,1280]{3,2,1,0:T(8,128)(2,1)}, u32[]{:S(2)}, u32[]{:S(2)}) collective-permute-start(bf16[2,4,48,1280]{3,2,1,0:T(8,128)(2,1)} %collective-permute-done.4.refs_1_), channel_id=1, source_target_pairs={{16,0},{17,1},{18,2},{19,3},{20,4},{21,5},{22,6},{23,7},{24,8},{25... | collective-permute-start | bytes 2949128 | tf_op jit(solution)/shard_map/ppermute | solution.py:48
  79.9 32.6 %collective-permute-start.12 = (bf16[2,4,48,1920]{3,2,1,0:T(8,128)(2,1)S(1)}, bf16[2,4,48,1920]{3,2,1,0:T(8,128)(2,1)}, u32[]{:S(2)}, u32[]{:S(2)}) collective-permute-start(bf16[2,4,48,1920]{3,2,1,0:T(8,128)(2,1)S(1)} %pad_maximum_fusion.3.refs_0_), channel_id=1, source_target_pairs={{16,0},{17,1},{18,2},{19,3},{20,4},{21,5},{22,6},{23,7},{24,8},{25... | collective-permute-start | bytes 4423688 | tf_op jit(solution)/shard_map/ppermute | solution.py:48
  80.4 32.1 %collective-permute-start.13 = (bf16[2,4,48,1920]{3,2,1,0:T(8,128)(2,1)}, bf16[2,4,48,1920]{3,2,1,0:T(8,128)(2,1)}, u32[]{:S(2)}, u32[]{:S(2)}) collective-permute-start(bf16[2,4,48,1920]{3,2,1,0:T(8,128)(2,1)} %collective-permute-done.11.refs_1_), channel_id=1, source_target_pairs={{16,0},{17,1},{18,2},{19,3},{20,4},{21,5},{22,6},{23,7},{24,8},{25... | collective-permute-start | bytes 4423688 | tf_op jit(solution)/shard_map/ppermute | solution.py:48
  80.8 57.3 %collective-permute-start.19 = (bf16[2,4,192,384]{3,2,1,0:T(8,128)(2,1)}, bf16[2,4,192,384]{3,2,1,0:T(8,128)(2,1)}, u32[]{:S(2)}, u32[]{:S(2)}) collective-permute-start(bf16[2,4,192,384]{3,2,1,0:T(8,128)(2,1)} %pad_maximum_fusion.4.refs_0_.refs_4_), channel_id=1, source_target_pairs={{16,0},{17,1},{18,2},{19,3},{20,4},{21,5},{22,6},{23,7},{24,8},{25... | collective-permute-start | bytes 3538952 | tf_op jit(solution)/shard_map/ppermute | solution.py:48
  92.5 45.5 %collective-permute-start.20 = (bf16[2,4,192,384]{3,2,1,0:T(8,128)(2,1)}, bf16[2,4,192,384]{3,2,1,0:T(8,128)(2,1)}, u32[]{:S(2)}, u32[]{:S(2)}) collective-permute-start(bf16[2,4,192,384]{3,2,1,0:T(8,128)(2,1)} %collective-permute-done.18.refs_1_.refs_5_), channel_id=1, source_target_pairs={{16,0},{17,1},{18,2},{19,3},{20,4},{21,5},{22,6},{23,7},{24,8},{25... | collective-permute-start | bytes 3538952 | tf_op jit(solution)/shard_map/ppermute | solution.py:48
  193.6 28.3 %collective-permute-start.21 = (bf16[16,576]{1,0:T(8,128)(2,1)S(1)}, bf16[16,576]{1,0:T(8,128)(2,1)S(1)}, u32[]{:S(2)}, u32[]{:S(2)}) collective-permute-start(bf16[16,576]{1,0:T(8,128)(2,1)S(1)} %concatenate.40), channel_id=1, source_target_pairs={{16,0},{17,1},{18,2},{19,3},{20,4},{21,5},{22,6},{23,7},{24,8},{25... | collective-permute-start | bytes 55304 | tf_op jit(solution)/shard_map/ppermute | solution.py:48
  196.8 30.9 %collective-permute-start.34 = (bf16[2,2,4,48,384]{4,3,2,1,0:T(8,128)(2,1)}, bf16[2,2,4,48,384]{4,3,2,1,0:T(8,128)(2,1)}, u32[]{:S(2)}, u32[]{:S(2)}) collective-permute-start(bf16[2,2,4,48,384]{4,3,2,1,0:T(8,128)(2,1)} %pad_maximum_fusion.8), channel_id=1, source_target_pairs={{16,0},{17,1},{18,2},{19,3},{20,4},{21,5},{22,6},{23,7},{24,8},{25... | collective-permute-start | bytes 1769480 | tf_op jit(solution)/shard_map/ppermute | solution.py:48
  203.3 44.5 %collective-permute-start.27 = (bf16[2,2,4,48,1152]{4,3,2,1,0:T(8,128)(2,1)}, bf16[2,2,4,48,1152]{4,3,2,1,0:T(8,128)(2,1)}, u32[]{:S(2)}, u32[]{:S(2)}) collective-permute-start(bf16[2,2,4,48,1152]{4,3,2,1,0:T(8,128)(2,1)} %pad_maximum_fusion.2), channel_id=1, source_target_pairs={{16,0},{17,1},{18,2},{19,3},{20,4},{21,5},{22,6},{23,7},{24,8},{25... | collective-permute-start | bytes 5308424 | tf_op jit(solution)/shard_map/ppermute | solution.py:48
  213.0 56.4 %collective-permute-start.48 = (bf16[2,2,4,192,384]{4,3,2,1,0:T(8,128)(2,1)}, bf16[2,2,4,192,384]{4,3,2,1,0:T(8,128)(2,1)}, u32[]{:S(2)}, u32[]{:S(2)}) collective-permute-start(bf16[2,2,4,192,384]{4,3,2,1,0:T(8,128)(2,1)} %pad_maximum_fusion.1), channel_id=1, source_target_pairs={{16,0},{17,1},{18,2},{19,3},{20,4},{21,5},{22,6},{23,7},{24,8},{25... | collective-permute-start | bytes 7077896 | tf_op jit(solution)/shard_map/ppermute | solution.py:48
  226.3 56.5 %collective-permute-start.41 = (bf16[2,2,4,48,1536]{4,3,2,1,0:T(8,128)(2,1)}, bf16[2,2,4,48,1536]{4,3,2,1,0:T(8,128)(2,1)S(1)}, u32[]{:S(2)}, u32[]{:S(2)}) collective-permute-start(bf16[2,2,4,48,1536]{4,3,2,1,0:T(8,128)(2,1)} %pad_maximum_fusion), channel_id=1, source_target_pairs={{16,0},{17,1},{18,2},{19,3},{20,4},{21,5},{22,6},{23,7},{24,8},{25... | collective-permute-start | bytes 7077896 | tf_op jit(solution)/shard_map/ppermute | solution.py:48
  226.4 17.4 %collective-permute-start.23 = (bf16[4,1,576]{2,1,0:T(2,128)(2,1)S(1)}, bf16[4,1,576]{2,1,0:T(2,128)(2,1)S(1)}, u32[]{:S(2)}, u32[]{:S(2)}) collective-permute-start(bf16[4,1,576]{2,1,0:T(2,128)(2,1)S(1)} %get-tuple-element.134), channel_id=1, source_target_pairs={{1,0},{0,1},{3,2},{2,3},{5,4},{4,5},{7,6},{6,7},{9,8},{8,9},{11,10... | collective-permute-start | bytes 13832 | tf_op jit(solution)/shard_map/ppermute | solution.py:48
  230.4 14.8 %collective-permute-start.35 = (bf16[2,4,48,384]{3,2,1,0:T(8,128)(2,1)S(1)}, bf16[2,4,48,384]{3,2,1,0:T(8,128)(2,1)S(1)}, u32[]{:S(2)}, u32[]{:S(2)}) collective-permute-start(bf16[2,4,48,384]{3,2,1,0:T(8,128)(2,1)S(1)} %get-tuple-element.76), channel_id=1, source_target_pairs={{2,0},{3,1},{0,2},{1,3},{6,4},{7,5},{4,6},{5,7},{10,8},{11,9},{8,1... | collective-permute-start | bytes 884744 | tf_op jit(solution)/shard_map/ppermute | solution.py:48
  243.8 11.1 %collective-permute-start.24 = (bf16[1,576]{1,0:T(2,128)(2,1)S(1)}, bf16[1,576]{1,0:T(2,128)(2,1)S(1)}, u32[]{:S(2)}, u32[]{:S(2)}) collective-permute-start(bf16[1,576]{1,0:T(2,128)(2,1)S(1)} %get-tuple-element.135), channel_id=1, source_target_pairs={{12,0},{13,1},{14,2},{15,3},{0,4},{1,5},{2,6},{3,7},{4,8},{5,9},{6... | collective-permute-start | bytes 3464 | tf_op jit(solution)/shard_map/ppermute | solution.py:48
  245.2 10.9 %collective-permute-start.26 = (bf16[1,576]{1,0:T(2,128)(2,1)S(1)}, bf16[1,576]{1,0:T(2,128)(2,1)S(1)}, u32[]{:S(2)}, u32[]{:S(2)}) collective-permute-start(bf16[1,576]{1,0:T(2,128)(2,1)S(1)} %get-tuple-element.136), channel_id=1, source_target_pairs={{4,0},{5,1},{6,2},{7,3},{8,4},{9,5},{10,6},{11,7},{12,8},{13,9},{1... | collective-permute-start | bytes 3464 | tf_op jit(solution)/shard_map/ppermute | solution.py:48
  247.9 7.7 %collective-permute-start.36 = (bf16[4,48,384]{2,1,0:T(8,128)(2,1)S(1)}, bf16[4,48,384]{2,1,0:T(8,128)(2,1)S(1)}, u32[]{:S(2)}, u32[]{:S(2)}) collective-permute-start(bf16[4,48,384]{2,1,0:T(8,128)(2,1)S(1)} %get-tuple-element.113), channel_id=1, source_target_pairs={{1,0},{0,1},{3,2},{2,3},{5,4},{4,5},{7,6},{6,7},{9,8},{8,9},{11,10... | collective-permute-start | bytes 442376 | tf_op jit(solution)/shard_map/ppermute | solution.py:48
  255.5 13.0 %collective-permute-start.28 = (bf16[2,4,48,1152]{3,2,1,0:T(8,128)(2,1)S(1)}, bf16[2,4,48,1152]{3,2,1,0:T(8,128)(2,1)S(1)}, u32[]{:S(2)}, u32[]{:S(2)}) collective-permute-start(bf16[2,4,48,1152]{3,2,1,0:T(8,128)(2,1)S(1)} %get-tuple-element.71), channel_id=1, source_target_pairs={{2,0},{3,1},{0,2},{1,3},{6,4},{7,5},{4,6},{5,7},{10,8},{11,9},{8,1... | collective-permute-start | bytes 2654216 | tf_op jit(solution)/shard_map/ppermute | solution.py:48
  256.1 5.8 %collective-permute-start.37 = (bf16[48,384]{1,0:T(8,128)(2,1)S(1)}, bf16[48,384]{1,0:T(8,128)(2,1)S(1)}, u32[]{:S(2)}, u32[]{:S(2)}) collective-permute-start(bf16[48,384]{1,0:T(8,128)(2,1)S(1)} %get-tuple-element.122), channel_id=1, source_target_pairs={{12,0},{13,1},{14,2},{15,3},{0,4},{1,5},{2,6},{3,7},{4,8},{5,9},{6... | collective-permute-start | bytes 110600 | tf_op jit(solution)/shard_map/ppermute | solution.py:48
  261.9 4.9 %collective-permute-start.38 = (bf16[48,384]{1,0:T(8,128)(2,1)S(1)}, bf16[48,384]{1,0:T(8,128)(2,1)S(1)}, u32[]{:S(2)}, u32[]{:S(2)}) collective-permute-start(bf16[48,384]{1,0:T(8,128)(2,1)S(1)} %get-tuple-element.124), channel_id=1, source_target_pairs={{8,0},{9,1},{10,2},{11,3},{12,4},{13,5},{14,6},{15,7},{0,8},{1,9},... | collective-permute-start | bytes 110600 | tf_op jit(solution)/shard_map/ppermute | solution.py:48
  268.8 9.5 %collective-permute-start.29 = (bf16[4,48,1152]{2,1,0:T(8,128)(2,1)S(1)}, bf16[4,48,1152]{2,1,0:T(8,128)(2,1)S(1)}, u32[]{:S(2)}, u32[]{:S(2)}) collective-permute-start(bf16[4,48,1152]{2,1,0:T(8,128)(2,1)S(1)} %get-tuple-element.100), channel_id=1, source_target_pairs={{1,0},{0,1},{3,2},{2,3},{5,4},{4,5},{7,6},{6,7},{9,8},{8,9},{11,10... | collective-permute-start | bytes 1327112 | tf_op jit(solution)/shard_map/ppermute | solution.py:48
  277.0 16.6 %collective-permute-start.49 = (bf16[2,4,192,384]{3,2,1,0:T(8,128)(2,1)S(1)}, bf16[2,4,192,384]{3,2,1,0:T(8,128)(2,1)S(1)}, u32[]{:S(2)}, u32[]{:S(2)}) collective-permute-start(bf16[2,4,192,384]{3,2,1,0:T(8,128)(2,1)S(1)} %get-tuple-element.86), channel_id=1, source_target_pairs={{2,0},{3,1},{0,2},{1,3},{6,4},{7,5},{4,6},{5,7},{10,8},{11,9},{8,1... | collective-permute-start | bytes 3538952 | tf_op jit(solution)/shard_map/ppermute | solution.py:48
  278.3 13.7 %collective-permute-start.30 = (bf16[48,1152]{1,0:T(8,128)(2,1)S(1)}, bf16[48,1152]{1,0:T(8,128)(2,1)S(1)}, u32[]{:S(2)}, u32[]{:S(2)}) collective-permute-start(bf16[48,1152]{1,0:T(8,128)(2,1)S(1)} %get-tuple-element.107), channel_id=1, source_target_pairs={{12,0},{13,1},{14,2},{15,3},{0,4},{1,5},{2,6},{3,7},{4,8},{5,9},{6... | collective-permute-start | bytes 331784 | tf_op jit(solution)/shard_map/ppermute | solution.py:48
  280.4 11.6 %collective-permute-start.32 = (bf16[48,1152]{1,0:T(8,128)(2,1)S(1)}, bf16[48,1152]{1,0:T(8,128)(2,1)S(1)}, u32[]{:S(2)}, u32[]{:S(2)}) collective-permute-start(bf16[48,1152]{1,0:T(8,128)(2,1)S(1)} %get-tuple-element.108), channel_id=1, source_target_pairs={{4,0},{5,1},{6,2},{7,3},{8,4},{9,5},{10,6},{11,7},{12,8},{13,9},{1... | collective-permute-start | bytes 331784 | tf_op jit(solution)/shard_map/ppermute | solution.py:48
  282.2 9.8 %collective-permute-start.31 = (bf16[48,1152]{1,0:T(8,128)(2,1)S(1)}, bf16[48,1152]{1,0:T(8,128)(2,1)S(1)}, u32[]{:S(2)}, u32[]{:S(2)}) collective-permute-start(bf16[48,1152]{1,0:T(8,128)(2,1)S(1)} %get-tuple-element.109), channel_id=1, source_target_pairs={{8,0},{9,1},{10,2},{11,3},{12,4},{13,5},{14,6},{15,7},{0,8},{1,9},... | collective-permute-start | bytes 331784 | tf_op jit(solution)/shard_map/ppermute | solution.py:48
  291.1 22.6 %collective-permute-start.42 = (bf16[2,4,48,1536]{3,2,1,0:T(8,128)(2,1)S(1)}, bf16[2,4,48,1536]{3,2,1,0:T(8,128)(2,1)S(1)}, u32[]{:S(2)}, u32[]{:S(2)}) collective-permute-start(bf16[2,4,48,1536]{3,2,1,0:T(8,128)(2,1)S(1)} %get-tuple-element.82), channel_id=1, source_target_pairs={{2,0},{3,1},{0,2},{1,3},{6,4},{7,5},{4,6},{5,7},{10,8},{11,9},{8,1... | collective-permute-start | bytes 3538952 | tf_op jit(solution)/shard_map/ppermute | solution.py:48
  293.9 21.8 %collective-permute-start.50 = (bf16[4,192,384]{2,1,0:T(8,128)(2,1)S(1)}, bf16[4,192,384]{2,1,0:T(8,128)(2,1)S(1)}, u32[]{:S(2)}, u32[]{:S(2)}) collective-permute-start(bf16[4,192,384]{2,1,0:T(8,128)(2,1)S(1)} %get-tuple-element.96), channel_id=1, source_target_pairs={{1,0},{0,1},{3,2},{2,3},{5,4},{4,5},{7,6},{6,7},{9,8},{8,9},{11,10... | collective-permute-start | bytes 1769480 | tf_op jit(solution)/shard_map/ppermute | solution.py:48
  314.0 9.9 %collective-permute-start.43 = (bf16[4,48,1536]{2,1,0:T(8,128)(2,1)S(1)}, bf16[4,48,1536]{2,1,0:T(8,128)(2,1)S(1)}, u32[]{:S(2)}, u32[]{:S(2)}) collective-permute-start(bf16[4,48,1536]{2,1,0:T(8,128)(2,1)S(1)} %get-tuple-element.98), channel_id=1, source_target_pairs={{1,0},{0,1},{3,2},{2,3},{5,4},{4,5},{7,6},{6,7},{9,8},{8,9},{11,10... | collective-permute-start | bytes 1769480 | tf_op jit(solution)/shard_map/ppermute | solution.py:48
  315.8 12.2 %collective-permute-start.51 = (bf16[192,384]{1,0:T(8,128)(2,1)S(1)}, bf16[192,384]{1,0:T(8,128)(2,1)S(1)}, u32[]{:S(2)}, u32[]{:S(2)}) collective-permute-start(bf16[192,384]{1,0:T(8,128)(2,1)S(1)} %get-tuple-element.101), channel_id=1, source_target_pairs={{12,0},{13,1},{14,2},{15,3},{0,4},{1,5},{2,6},{3,7},{4,8},{5,9},{6... | collective-permute-start | bytes 442376 | tf_op jit(solution)/shard_map/ppermute | solution.py:48
  318.1 13.2 %collective-permute-start.53 = (bf16[192,384]{1,0:T(8,128)(2,1)S(1)}, bf16[192,384]{1,0:T(8,128)(2,1)S(1)}, u32[]{:S(2)}, u32[]{:S(2)}) collective-permute-start(bf16[192,384]{1,0:T(8,128)(2,1)S(1)} %get-tuple-element.102), channel_id=1, source_target_pairs={{4,0},{5,1},{6,2},{7,3},{8,4},{9,5},{10,6},{11,7},{12,8},{13,9},{1... | collective-permute-start | bytes 442376 | tf_op jit(solution)/shard_map/ppermute | solution.py:48
  320.2 17.7 %collective-permute-start.52 = (bf16[192,384]{1,0:T(8,128)(2,1)S(1)}, bf16[192,384]{1,0:T(8,128)(2,1)S(1)}, u32[]{:S(2)}, u32[]{:S(2)}) collective-permute-start(bf16[192,384]{1,0:T(8,128)(2,1)S(1)} %get-tuple-element.103), channel_id=1, source_target_pairs={{8,0},{9,1},{10,2},{11,3},{12,4},{13,5},{14,6},{15,7},{0,8},{1,9},... | collective-permute-start | bytes 442376 | tf_op jit(solution)/shard_map/ppermute | solution.py:48
  324.1 14.0 %collective-permute-start.44 = (bf16[48,1536]{1,0:T(8,128)(2,1)S(1)}, bf16[48,1536]{1,0:T(8,128)(2,1)S(1)}, u32[]{:S(2)}, u32[]{:S(2)}) collective-permute-start(bf16[48,1536]{1,0:T(8,128)(2,1)S(1)} %get-tuple-element.104), channel_id=1, source_target_pairs={{12,0},{13,1},{14,2},{15,3},{0,4},{1,5},{2,6},{3,7},{4,8},{5,9},{6... | collective-permute-start | bytes 442376 | tf_op jit(solution)/shard_map/ppermute | solution.py:48
  325.7 12.4 %collective-permute-start.46 = (bf16[48,1536]{1,0:T(8,128)(2,1)S(1)}, bf16[48,1536]{1,0:T(8,128)(2,1)S(1)}, u32[]{:S(2)}, u32[]{:S(2)}) collective-permute-start(bf16[48,1536]{1,0:T(8,128)(2,1)S(1)} %get-tuple-element.105), channel_id=1, source_target_pairs={{4,0},{5,1},{6,2},{7,3},{8,4},{9,5},{10,6},{11,7},{12,8},{13,9},{1... | collective-permute-start | bytes 442376 | tf_op jit(solution)/shard_map/ppermute | solution.py:48
  328.0 14.5 %collective-permute-start.45 = (bf16[48,1536]{1,0:T(8,128)(2,1)S(1)}, bf16[48,1536]{1,0:T(8,128)(2,1)S(1)}, u32[]{:S(2)}, u32[]{:S(2)}) collective-permute-start(bf16[48,1536]{1,0:T(8,128)(2,1)S(1)} %get-tuple-element.106), channel_id=1, source_target_pairs={{8,0},{9,1},{10,2},{11,3},{12,4},{13,5},{14,6},{15,7},{0,8},{1,9},... | collective-permute-start | bytes 442376 | tf_op jit(solution)/shard_map/ppermute | solution.py:48
  (35 other events, 403.4 us)

commit v2 on v1

v2 whole, which is shorter than its diff:
```python
import functools
import math

import jax
import jax.numpy as jnp
from jax import lax
from jax.experimental import pallas as pl
from jax.experimental.pallas import tpu as pltpu
from jax.sharding import PartitionSpec as P

HEADS = 12
HEAD_DIM = 64
PATCH = 16
EPSILON = 1e-05
SQRT_HALF = 0.7071067811865476
LOG2_E = 1.4426950408889634
LOG2_DENSITY = -1.3257480647361593
AXES = ("dp", "fsdp")
F32 = jnp.float32
BF16 = jnp.bfloat16
LANES = 128
MEBI = 1 << 20
VMEM_MOST = 60
SMEM = pl.BlockSpec(memory_space=pltpu.SMEM)
HBM = pl.BlockSpec(memory_space=pl.ANY)


def grid_of(shards):
    side = math.isqrt(shards // 4)
    assert 4 * side * side == shards
    return 4, side


def arrive(value, shards, kind, step):
    depth, side = grid_of(shards)
    pairs = []
    for core in range(2):
        for z in range(depth):
            for y in range(side):
                for x in range(side):
                    to = core * shards + (z * side + y) * side + x
                    at = [core, z, y, x]
                    if kind == "core":
                        at[0] = 1 - core
                    elif kind == "z":
                        at[1] = (z + step) % depth
                    elif (kind == "first") == (core == 0):
                        at[3] = (x + step) % side
                    else:
                        at[2] = (y + step) % side
                    pairs.append((at[0] * shards + (at[1] * side + at[2]) * side + at[3], to))
    with jax.named_scope(f"{kind}_exchange"):
        return lax.ppermute(value, AXES, pairs)


def place(shards, half):
    _, side = grid_of(shards)
    at = lax.axis_index("fsdp")
    z, y, x = at // (side * side), (at // side) % side, at % side
    first = jnp.where(half == 0, x, y)
    second = jnp.where(half == 0, y, x)
    return jnp.stack([half, z, first, second, lax.axis_index("dp")]).astype(jnp.int32)


def after(value, *earlier):
    return lax.optimization_barrier((value, *earlier))[0]


def spread_lines(vectors, shards):
    unit = jnp.concatenate(vectors)
    unit = jnp.pad(unit, (0, -unit.shape[0] % 1024)).reshape(1, -1, LANES)
    at = lax.broadcasted_iota(jnp.int32, (shards, 1, 1), 0) == lax.axis_index("fsdp")
    return jnp.where(at, unit, jnp.zeros_like(unit))


def join_lines(spread, count, rows):
    shards = spread.shape[0]
    whole = spread.reshape(shards, -1)[:, : count * rows].reshape(shards, count, rows)
    whole = whole.transpose(1, 0, 2).reshape(count, -1)
    return jnp.pad(whole.astype(F32), ((0, 16 - count), (0, 0)))


def gather_z(unit, shards):
    depth, _ = grid_of(shards)
    return jnp.stack([unit] + [arrive(unit, shards, "z", s) for s in range(1, depth)])


def gather_first(got, shards):
    _, side = grid_of(shards)
    return jnp.stack([got] + [arrive(got, shards, "first", s) for s in range(1, side)])


def gather_second(got, shards):
    _, side = grid_of(shards)
    return [got] + [arrive(got, shards, "second", s) for s in range(1, side)]


def gather_core(own, shards):
    return [arrive(part, shards, "core", 1) for part in own]


def row_of(where, depth, side, rel_second, rel_first, rel_z):
    z = lax.rem(where[1] + rel_z, depth)
    first = lax.rem(where[2] + rel_first, side)
    second = lax.rem(where[3] + rel_second, side)
    y = jnp.where(where[0] == 0, second, first)
    x = jnp.where(where[0] == 0, first, second)
    return (z * side + y) * side + x


def unroll_rows(parts, where, half, depth, side):
    rel = jnp.stack(parts)
    rel = jnp.roll(rel, where[3], axis=0)
    rel = jnp.roll(rel, where[2], axis=1)
    rel = jnp.roll(rel, where[1], axis=2)
    straight = jnp.where(half == 0, rel.transpose(2, 0, 1, 3, 4), rel.transpose(2, 1, 0, 3, 4))
    return straight.reshape(-1, rel.shape[-1])


def assemble(own, other, shards, cuts):
    depth, side = grid_of(shards)
    core = lax.axis_index("dp")
    here, there = place(shards, core), place(shards, 1 - core)
    mine = unroll_rows(own, here, core, depth, side)
    theirs = unroll_rows(other, there, 1 - core, depth, side)
    wholes = []
    for start, width, split in cuts:
        left, right = mine[:, start : start + width], theirs[:, start : start + width]
        if split:
            swapped = jnp.concatenate([right, left], axis=1)
            left = jnp.where(core == 0, jnp.concatenate([left, right], axis=1), swapped)
        wholes.append(left)
    return wholes


def tiles_of(widths):
    tiles, start = [], 0
    for k, width in enumerate(widths):
        at = 0
        while at < width:
            step = min(768, width - at)
            tiles.append((k, at, start + at, step))
            at += step
        start += width
    return tiles


def put_pieces(acc, sums, group, columns, where, depth, side, rows, deep, ahead):
    step = columns.stop - columns.start
    for second in range(side):
        for first in range(side):
            for z in range(deep):
                from_row = row_of(where, depth, side, second, first, z)
                if deep == 1:
                    from_row = lax.rem(from_row, side * side)
                piece = acc[pl.ds(pl.multiple_of(from_row * rows, 16), rows), :step]
                sums[group, second, first, ahead + z, :, columns] = piece.astype(BF16)


def grad_kernel(depth, side, rows, deep, widths, there, here, *refs):
    count = len(widths)
    layers = depth // deep
    tiles = tiles_of(widths)
    pairs, refs = refs[: 2 * count], refs[2 * count :]
    away, outs, refs = refs[0], refs[1 : 1 + side], refs[1 + side :]
    left, turned, right, acc, sums, left_sems, right_sems, out_sems = refs
    chunk = left.shape[2]

    def left_copy(k, layer):
        column = pl.multiple_of(lax.rem(there[1] + layer, layers) * chunk, LANES) if layers > 1 else 0
        return pltpu.make_async_copy(
            pairs[2 * k].at[:, pl.ds(column, chunk)], left.at[k * layers + layer], left_sems.at[k * layers + layer]
        )

    def right_copy(group, t):
        k, at, start, step = tiles[t]
        half = (there if group == 0 else here)[0]
        column = pl.multiple_of(half * widths[k] + at, LANES)
        return pltpu.make_async_copy(
            pairs[2 * k + 1].at[:, pl.ds(column, step)],
            right.at[group, :, pl.ds(start, step)],
            right_sems.at[group, t],
        )

    def out_copies(group):
        if group == 0:
            return [pltpu.make_async_copy(sums.at[0], away, out_sems.at[0])]
        return [pltpu.make_async_copy(sums.at[1, s], outs[s], out_sems.at[1 + s]) for s in range(side)]

    for layer in range(layers):
        for k in range(count):
            left_copy(k, layer).start()
            if layer == 0:
                for t in range(len(tiles)):
                    if tiles[t][0] == k:
                        right_copy(0, t).start()
    for t in range(len(tiles)):
        right_copy(1, t).start()
    for group in range(2):
        where = there if group == 0 else here
        for layer in range(layers):
            for t, (k, at, start, step) in enumerate(tiles):
                if group == 0 and at == 0:
                    left_copy(k, layer).wait()
                    turned[k * layers + layer] = left[k * layers + layer].T
                if layer == 0:
                    right_copy(group, t).wait()
                columns = slice(start, start + step)
                acc[:, :step] = dot(turned[k * layers + layer], right[group, :, columns])
                put_pieces(acc, sums, group, columns, where, depth, side, rows, deep, layer * deep)
        for copy in out_copies(group):
            copy.start()
    for group in range(2):
        for copy in out_copies(group):
            copy.wait()


def rel_grad(pairs, shards):
    depth, side = grid_of(shards)
    length, features = pairs[0][0].shape
    widths = [rhs.shape[1] // 2 for _, rhs in pairs]
    width = sum(widths)
    rows = features // shards
    core = lax.axis_index("dp")
    there, here = place(shards, 1 - core), place(shards, core)
    if rows % 16 != 0:
        both = []
        for half, where in ((1 - core, there), (core, here)):
            wholes = [
                lax.dot_general(
                    lhs,
                    lax.dynamic_slice_in_dim(rhs, half * (rhs.shape[1] // 2), rhs.shape[1] // 2, axis=1),
                    (((0,), (0,)), ((), ())),
                    preferred_element_type=F32,
                )
                for lhs, rhs in pairs
            ]
            whole = jnp.concatenate(wholes, axis=1).reshape(depth, side, side, rows, width)
            rel = jnp.where(half == 0, whole.transpose(1, 2, 0, 3, 4), whole.transpose(2, 1, 0, 3, 4))
            rel = jnp.roll(rel, -where[3], axis=0)
            rel = jnp.roll(rel, -where[2], axis=1)
            both.append(jnp.roll(rel, -where[1], axis=2).astype(BF16))
        return both[0], [both[1][s] for s in range(side)]
    deep = depth if features <= 1024 else 1
    chunk = features if deep > 1 else features // depth
    layers = depth // deep
    count, pieces = len(pairs), len(tiles_of(widths))
    out = pl.pallas_call(
        functools.partial(grad_kernel, depth, side, rows, deep, widths),
        in_specs=[SMEM, SMEM] + [HBM] * (2 * count),
        out_specs=[HBM] * (1 + side),
        out_shape=[jax.ShapeDtypeStruct((side, side, depth, rows, width), BF16)]
        + [jax.ShapeDtypeStruct((side, depth, rows, width), BF16)] * side,
        scratch_shapes=[
            pltpu.VMEM((count * layers, length, chunk), BF16),
            pltpu.VMEM((count * layers, chunk, length), BF16),
            pltpu.VMEM((2, length, width), BF16),
            pltpu.VMEM((chunk, min(768, max(widths))), F32),
            pltpu.VMEM((2, side, side, depth, rows, width), BF16),
            pltpu.SemaphoreType.DMA((count * layers,)),
            pltpu.SemaphoreType.DMA((2, pieces)),
            pltpu.SemaphoreType.DMA((1 + side,)),
        ],
        compiler_params=pltpu.CompilerParams(vmem_limit_bytes=VMEM_MOST * MEBI),
        cost_estimate=pl.CostEstimate(flops=4 * length * features * width, bytes_accessed=20 * MEBI, transcendentals=0),
        name="grad",
    )(there, here, *(operand for pair in pairs for operand in pair))
    return out[0], out[1:]


def sum_of(*values):
    total = values[0].astype(F32)
    for value in values[1:]:
        total = total + value.astype(F32)
    return total.astype(BF16)


def reduce_second(own, got, shards):
    _, side = grid_of(shards)
    came = [arrive(sum_of(own[s], got[s]), shards, "second", side - s) for s in range(1, side)]
    return [sum_of(own[0][f], got[0, f], *(part[f] for part in came)) for f in range(side)]


def reduce_first(sums, shards):
    depth, side = grid_of(shards)
    came = [arrive(sums[f], shards, "first", side - f) for f in range(1, side)]
    return [sum_of(sums[0][z], *(part[z] for part in came)) for z in range(depth)]


def reduce_z(sums, shards):
    depth, _ = grid_of(shards)
    return sum_of(sums[0], *(arrive(sums[z], shards, "z", depth - z) for z in range(1, depth)))


def exchange_lines(lines, shards, kind):
    depth, side = grid_of(shards)
    count = {"z": depth, "core": 2}.get(kind, side)
    return sum_of(lines, *(arrive(lines, shards, kind, step) for step in range(1, count)))


def both_halves(mine, shards, widths):
    theirs = arrive(mine, shards, "core", 1)
    core = lax.axis_index("dp")
    left = jnp.where(core == 0, mine, theirs)
    right = jnp.where(core == 0, theirs, mine)
    wholes, start = [], 0
    for width in widths:
        columns = slice(start, start + width)
        wholes.append(jnp.concatenate([left[:, columns], right[:, columns]], axis=1).astype(F32))
        start += width
    return wholes


GAIN_ONE, SHIFT_ONE, BIAS_QUERY, BIAS_VALUE, BIAS_OUT, GAIN_TWO, SHIFT_TWO, BIAS_DOWN = range(8)
SCALE = HEAD_DIM ** (-0.5)


def weight_copies(plan, here, there, parts, outs, sems, first=0):
    groups = [[] for _ in outs]
    if plan is None:
        for k, (part, out) in enumerate(zip(parts, outs)):
            groups[k].append(pltpu.make_async_copy(part, out, sems.at[first + k]))
        return groups
    depth, side, rows, cuts = plan
    used = first
    for group in range(2):
        where = here if group == 0 else there
        for second in range(side):
            for ahead in range(side):
                for z in range(depth):
                    at = pl.multiple_of(row_of(where, depth, side, second, ahead, z) * rows, 16)
                    source = parts[group * side + second].at[ahead, z]
                    for k, ((start, width, split), out) in enumerate(zip(cuts, outs)):
                        if group == 1 and not split:
                            continue
                        column = pl.multiple_of(where[0] * width, LANES) if split else 0
                        groups[k].append(
                            pltpu.make_async_copy(
                                source.at[:, pl.ds(start, width)],
                                out.at[pl.ds(at, rows), pl.ds(column, width)],
                                sems.at[used],
                            )
                        )
                        used += 1
    return groups


def bring(groups):
    for group in groups:
        for copy in group:
            copy.start()
    for group in groups:
        for copy in group:
            copy.wait()


def copies_of(plan, shards, cuts):
    if plan is None:
        return len(cuts)
    return shards * sum(2 if split else 1 for _, _, split in cuts)


def standardize(values):
    average = jnp.mean(values, axis=-1, keepdims=True)
    centred = values - average
    spread = jnp.mean(centred * centred, axis=-1, keepdims=True)
    inverse = lax.rsqrt(spread + EPSILON)
    return centred * inverse, inverse


def dot(a, b, dims=((1,), (0,))):
    return lax.dot_general(a, b, (dims, ((), ())), preferred_element_type=F32)


NT = ((1,), (1,))
TN = ((0,), (0,))


def project_kernel(plan, count, here, there, tokens, lines, *refs):
    parts = refs[:count]
    normed_ref, qkv_ref = refs[count : count + 2]
    weight, sems = refs[count + 2 :]
    width = tokens.shape[1]

    @pl.when(pl.program_id(0) == 0)
    def _():
        bring(weight_copies(plan, here, there, parts, (weight,), sems))

    standard, _ = standardize(tokens[...].astype(F32))
    normed = (standard * lines[pl.ds(GAIN_ONE, 1), :] + lines[pl.ds(SHIFT_ONE, 1), :]).astype(BF16)
    normed_ref[...] = normed
    bias = (lines[pl.ds(BIAS_QUERY, 1), :], None, lines[pl.ds(BIAS_VALUE, 1), :])
    for part in range(3):
        columns = slice(part * width, (part + 1) * width)
        project = dot(normed, weight[:, columns])
        if bias[part] is not None:
            project = project + bias[part]
        qkv_ref[:, columns] = project.astype(BF16)


def attend_kernel(frames, qkv_ref, mixed_ref, power_ref, inverse_ref):
    tube = pl.program_id(0)
    length, width = mixed_ref.shape
    mask = jnp.where(lax.broadcasted_iota(jnp.int32, (1, length), 1) < frames[tube] * PATCH, 0.0, -1e30)
    lower = lax.broadcasted_iota(jnp.int32, (length, LANES), 1) < HEAD_DIM
    ones = jnp.ones((length, LANES), BF16)
    for pair in range(width // LANES):
        query = qkv_ref[:, pair * LANES : (pair + 1) * LANES] * jnp.asarray(SCALE, BF16)
        keys = qkv_ref[:, width + pair * LANES : width + (pair + 1) * LANES]
        values = qkv_ref[:, 2 * width + pair * LANES : 2 * width + (pair + 1) * LANES]
        values = jnp.concatenate([values, ones], axis=1)
        both = []
        for k in range(2):
            own = jnp.where(lower if k == 0 else ~lower, query, jnp.zeros_like(query))
            scores = dot(own, keys, NT) + mask
            power = jnp.exp(scores - jnp.max(scores, axis=-1, keepdims=True)).astype(BF16)
            power_ref[0, 2 * pair + k] = power
            both.append(dot(power, values))
        inverse = 1.0 / jnp.where(lower, both[0][:, LANES:], both[1][:, LANES:])
        inverse_ref[:, pair * LANES : (pair + 1) * LANES] = inverse.astype(BF16)
        mixed = jnp.where(lower, both[0][:, :LANES], both[1][:, :LANES]) * inverse
        mixed_ref[:, pair * LANES : (pair + 1) * LANES] = mixed.astype(BF16)


def feed_kernel(plan, count, here, there, frames, tokens, mixed, cotangent, lines, up_bias, *refs):
    parts = refs[:count]
    resid_ref, normed_ref, active_ref, slope_ref, upstream_ref = refs[count : count + 5]
    out_weight, up_weight, sems = refs[count + 5 :]
    tube = pl.program_id(0)
    first, last = weight_copies(plan, here, there, parts, (out_weight, up_weight), sems)

    @pl.when(tube == 0)
    def _():
        for copy in first + last:
            copy.start()
        for copy in first:
            copy.wait()

    length = tokens.shape[0]
    row_ok = lax.broadcasted_iota(jnp.int32, (length, 1), 0) < frames[tube] * PATCH
    upstream_ref[...] = jnp.where(row_ok, cotangent[...], jnp.zeros_like(cotangent))
    attended = dot(mixed[...], out_weight[...]) + lines[pl.ds(BIAS_OUT, 1), :]
    resid = tokens[...].astype(F32) + attended
    resid_ref[...] = resid.astype(BF16)
    standard, _ = standardize(resid)
    normed = (standard * lines[pl.ds(GAIN_TWO, 1), :] + lines[pl.ds(SHIFT_TWO, 1), :]).astype(BF16)
    normed_ref[...] = normed

    @pl.when(tube == 0)
    def _():
        for copy in last:
            copy.wait()

    units = up_weight.shape[1]
    step = 512
    for at in range(0, units, step):
        hidden = dot(normed, up_weight[:, at : at + step]) + up_bias[:, at : at + step]
        cumulative = 0.5 + 0.5 * lax.erf(hidden * SQRT_HALF)
        density = jnp.exp2(hidden * hidden * (-0.5 * LOG2_E) + LOG2_DENSITY)
        active_ref[:, at : at + step] = (hidden * cumulative).astype(BF16)
        slope_ref[:, at : at + step] = (cumulative + hidden * density).astype(BF16)


def norm_back(grad, standard, inverse, gain):
    scaled = grad * gain
    first = jnp.mean(scaled, axis=-1, keepdims=True)
    second = jnp.mean(scaled * standard, axis=-1, keepdims=True)
    return inverse * (scaled - first - standard * second)


def column_sum(values):
    return jnp.sum(values, axis=0, keepdims=True)


SUM_GAIN_TWO, SUM_SHIFT_TWO, SUM_BIAS_OUT, SUM_BIAS_DOWN = range(4)


def feed_back_kernel(plans, counts, depth, side, rows, direct, here, there, upstream, slope, resid, inverse_sums, lines, *refs):
    mixed_hbm, normed_hbm, refs = refs[0], refs[1], refs[2:]
    ff_parts, refs = refs[: counts[0]], refs[counts[0] :]
    down_parts, refs = refs[: counts[1]], refs[counts[1] :]
    attended_ref, scaled_ref, sums_ref, up_sum_ref = refs[:4]
    refs = refs[4:]
    if direct:
        away, outs, refs = refs[0], refs[1 : 1 + side], refs[1 + side :]
    else:
        hidden_hbm, refs = refs[0], refs[1:]
    out_weight, up_weight, down_weight, hidden_all, attended_all, sems, more_sems = refs[:7]
    tube, last = pl.program_id(0), pl.num_programs(0) - 1
    length, width = upstream.shape
    units = up_weight.shape[1]
    (down_copies,) = weight_copies(plans[1], here, there, down_parts, (down_weight,), sems)
    ff_copies = weight_copies(plans[0], here, there, ff_parts, (out_weight, up_weight), sems, len(down_copies))
    if direct:
        left, turned, acc, sums = refs[7:]
        left_copies = [
            pltpu.make_async_copy(mixed_hbm, left.at[0], more_sems.at[0]),
            pltpu.make_async_copy(normed_hbm, left.at[1], more_sems.at[1]),
        ]

    @pl.when(tube == 0)
    def _():
        for copy in down_copies:
            copy.start()
        for group in reversed(ff_copies):
            for copy in group:
                copy.start()
        if direct:
            for copy in left_copies:
                copy.start()
        sums_ref[...] = jnp.zeros_like(sums_ref)
        up_sum_ref[...] = jnp.zeros_like(up_sum_ref)
        for copy in down_copies:
            copy.wait()

    here_rows = pl.ds(pl.multiple_of(tube * length, 16), length)
    low = upstream[...]
    step = 768
    for at in range(0, units, step):
        grad = dot(low, down_weight[at : at + step, :], NT) * slope[:, at : at + step].astype(F32)
        hidden_all[here_rows, at : at + step] = grad.astype(BF16)
        up_sum_ref[:, at : at + step] += column_sum(grad)

    @pl.when(tube == 0)
    def _():
        for group in ff_copies:
            for copy in group:
                copy.wait()

    normed_grad = dot(hidden_all[here_rows, :], up_weight[...], NT)
    standard, inverse = standardize(resid[...].astype(F32))
    above = low.astype(F32)
    resid_grad = above + norm_back(normed_grad, standard, inverse, lines[pl.ds(GAIN_TWO, 1), :])
    attended_grad = resid_grad.astype(BF16)
    attended_ref[...] = attended_grad
    attended_all[here_rows, :] = attended_grad
    scaled_ref[...] = (dot(attended_grad, out_weight[...], NT) * inverse_sums[...].astype(F32)).astype(BF16)
    sums_ref[pl.ds(SUM_GAIN_TWO, 1), :] += column_sum(normed_grad * standard)
    sums_ref[pl.ds(SUM_SHIFT_TWO, 1), :] += column_sum(normed_grad)
    sums_ref[pl.ds(SUM_BIAS_OUT, 1), :] += column_sum(attended_grad.astype(F32))
    sums_ref[pl.ds(SUM_BIAS_DOWN, 1), :] += column_sum(above)

    if not direct:

        @pl.when(tube == last)
        def _():
            copy = pltpu.make_async_copy(hidden_all, hidden_hbm, more_sems.at[0])
            copy.start()
            copy.wait()

        return

    @pl.when(tube == 1)
    def _():
        for k in range(2):
            left_copies[k].wait()
            turned[k] = left[k].T

    @pl.when(tube == last)
    def _():
        waits = []
        for group in range(2):
            where = there if group == 0 else here
            for k, at, start, size in tiles_of((width // 2, units // 2)):
                right = attended_all if k == 0 else hidden_all
                column = pl.multiple_of(where[0] * (right.shape[1] // 2) + at, LANES)
                acc[:, :size] = dot(turned[k], right[:, pl.ds(column, size)])
                put_pieces(acc, sums, group, slice(start, start + size), where, depth, side, rows, depth, 0)
            if group == 0:
                waits.append(pltpu.make_async_copy(sums.at[0], away, more_sems.at[2]))
                waits[-1].start()
            else:
                for s in range(side):
                    waits.append(pltpu.make_async_copy(sums.at[1, s], outs[s], more_sems.at[3 + s]))
                    waits[-1].start()
        for copy in waits:
            copy.wait()


def attend_back_kernel(qkv, power_ref, mixed, scaled_grad, grad_ref, sums_ref):
    tube = pl.program_id(0)

    @pl.when(tube == 0)
    def _():
        sums_ref[...] = jnp.zeros_like(sums_ref)

    length, width = mixed.shape
    lower = lax.broadcasted_iota(jnp.int32, (length, LANES), 1) < HEAD_DIM
    for pair in range(width // LANES):
        lanes = slice(pair * LANES, (pair + 1) * LANES)
        query = qkv[:, lanes]
        keys = qkv[:, width + pair * LANES : width + (pair + 1) * LANES]
        values = qkv[:, 2 * width + pair * LANES : 2 * width + (pair + 1) * LANES]
        above = scaled_grad[:, lanes]
        product = above.astype(F32) * mixed[:, lanes].astype(F32)
        query_grad, keys_grad, values_grad = [], [], []
        for k in range(2):
            mine = lower if k == 0 else ~lower
            own = jnp.where(mine, above, jnp.zeros_like(above))
            power = power_ref[0, 2 * pair + k]
            inner = jnp.sum(jnp.where(mine, product, 0.0), axis=-1, keepdims=True)
            scores_grad = (power.astype(F32) * (dot(own, values, NT) - inner)).astype(BF16)
            values_grad.append(dot(power, above, TN))
            query_grad.append(dot(scores_grad, keys))
            keys_grad.append(dot(scores_grad, query, TN))
        for part, (pieces, scale) in enumerate(((query_grad, SCALE), (keys_grad, SCALE), (values_grad, None))):
            piece = jnp.where(lower, pieces[0], pieces[1])
            if scale is not None:
                piece = piece * scale
            grad_ref[:, part * width + pair * LANES : part * width + (pair + 1) * LANES] = piece.astype(BF16)
            if part != 1:
                sums_ref[pl.ds(part // 2, 1), lanes] += column_sum(piece)


def first_back_kernel(plan, count, here, there, tokens, project_grad, attended_grad, lines, *refs):
    parts = refs[:count]
    tokens_ref, sums_ref = refs[count : count + 2]
    weight, sems = refs[count + 2 :]
    tube = pl.program_id(0)

    @pl.when(tube == 0)
    def _():
        bring(weight_copies(plan, here, there, parts, (weight,), sems))
        sums_ref[...] = jnp.zeros_like(sums_ref)

    grad = dot(project_grad[...], weight[...], NT)
    standard, inverse = standardize(tokens[...].astype(F32))
    inputs_grad = norm_back(grad, standard, inverse, lines[pl.ds(GAIN_ONE, 1), :])
    tokens_ref[...] = (attended_grad[...].astype(F32) + inputs_grad).astype(BF16)
    sums_ref[pl.ds(0, 1), :] += column_sum(grad * standard)
    sums_ref[pl.ds(1, 1), :] += column_sum(grad)


def block_out_kernel(plan, count, here, there, active, resid, lines, *refs):
    parts = refs[:count]
    out_ref = refs[count]
    weight, sems = refs[count + 1 :]

    @pl.when(pl.program_id(0) == 0)
    def _():
        bring(weight_copies(plan, here, there, parts, (weight,), sems))

    branch = dot(active[...], weight[...]) + lines[pl.ds(BIAS_DOWN, 1), :]
    out_ref[...] = (resid[...].astype(F32) + branch).astype(BF16)


def rows_of(width, length):
    return pl.BlockSpec((length, width), lambda t: (t, 0))


def fixed(*shape):
    return pl.BlockSpec(shape, lambda t: (0,) * len(shape))


def shape_of(*shape, kind=BF16):
    return jax.ShapeDtypeStruct(shape, kind)


def call(kernel, name, grid, in_specs, outs, scratch, flops, *args):
    return pl.pallas_call(
        kernel,
        grid=(grid,),
        in_specs=in_specs,
        out_specs=[spec for spec, _ in outs],
        out_shape=[shape for _, shape in outs],
        scratch_shapes=scratch,
        compiler_params=pltpu.CompilerParams(vmem_limit_bytes=VMEM_MOST * MEBI),
        cost_estimate=pl.CostEstimate(flops=flops, bytes_accessed=16 * MEBI, transcendentals=0),
        name=name,
    )(*args)


def local(
    tokens,
    clip_frames,
    tube_clip,
    first_gain,
    first_shift,
    qkv_weight,
    query_bias,
    value_bias,
    out_weight,
    out_bias,
    second_gain,
    second_shift,
    up_weight,
    up_bias,
    down_weight,
    down_bias,
    cotangent,
):
    shards = lax.axis_size("fsdp")
    depth, side = grid_of(shards)
    core = lax.axis_index("dp")
    here, there = place(shards, core), place(shards, 1 - core)
    total, width = tokens.shape
    tubes = tube_clip.shape[0]
    length = total // tubes
    clip_count = clip_frames.shape[0]
    matches = tube_clip[:, None] == jnp.arange(clip_count, dtype=jnp.int32)[None, :]
    frames = jnp.sum(jnp.where(matches, clip_frames[None, :], 0), axis=1)

    def half(matrix):
        columns = matrix.shape[1] // 2
        return lax.dynamic_slice_in_dim(matrix, core * columns, columns, axis=1)

    wide, full, ff = qkv_weight.shape[1] // 2, out_weight.shape[1] // 2, up_weight.shape[1] // 2
    units = 2 * ff
    rows = first_gain.shape[0]
    vectors = [first_gain, first_shift, query_bias, value_bias, out_bias, second_gain, second_shift, down_bias]
    vectors += [up_bias[k * rows : (k + 1) * rows] for k in range(4)]
    pack_one = half(qkv_weight)
    pack_two = jnp.concatenate([half(out_weight), half(up_weight)], axis=1)
    pack_three = half(down_weight)
    cuts = (
        ((0, wide, True),),
        ((0, full, True), (full, ff, True)),
        ((0, full, True),),
    )
    plans, counts = [], []
    for pack, cut in zip((pack_one, pack_two, pack_three), cuts):
        direct = pack.shape[0] % 16 == 0
        plans.append((depth, side, pack.shape[0], cut) if direct else None)
        counts.append(2 * side if direct else len(cut))

    def finish(k, own, other):
        return [*own, *other] if plans[k] is not None else assemble(own, other, shards, cuts[k])

    number = [copies_of(plan, shards, cut) for plan, cut in zip(plans, cuts)]
    sem = pltpu.SemaphoreType.DMA
    big = 2 * total * width * width
    narrow, wide_rows, deep_rows = rows_of(width, length), rows_of(3 * width, length), rows_of(units, length)
    tall = total // 2
    tall_narrow, tall_wide, tall_deep = rows_of(width, tall), rows_of(3 * width, tall), rows_of(units, tall)
    probs_spec = pl.BlockSpec((1, HEADS, length, length), lambda t: (t, 0, 0, 0))

    z_one = gather_z(pack_one, shards)
    spread = spread_lines(vectors, shards)
    z_one, spread, pack_two, pack_three = lax.optimization_barrier((z_one, spread, pack_two, pack_three))
    first_one = gather_first(z_one, shards)
    spread = exchange_lines(spread, shards, "first")
    first_one, spread, pack_two = lax.optimization_barrier((first_one, spread, pack_two))
    second_one = gather_second(first_one, shards)
    z_two = gather_z(pack_two, shards)
    spread = exchange_lines(spread, shards, "z")
    second_one, z_two, pack_three, spread = lax.optimization_barrier((second_one, z_two, pack_three, spread))
    core_one = gather_core(second_one, shards)
    lines = join_lines(exchange_lines(spread, shards, "second"), len(vectors), rows)
    core_one, z_two, pack_three, tokens, lines = lax.optimization_barrier((core_one, z_two, pack_three, tokens, lines))
    parts_one = finish(0, second_one, core_one)
    first_two = gather_first(z_two, shards)

    normed_one, qkv = call(
        functools.partial(project_kernel, plans[0], counts[0]),
        "project",
        tubes,
        [SMEM, SMEM, narrow, fixed(16, width)] + [HBM] * counts[0],
        [(narrow, shape_of(total, width)), (wide_rows, shape_of(total, 3 * width))],
        [pltpu.VMEM((width, 3 * width), BF16), sem((number[0],))],
        3 * big,
        here, there, tokens, lines, *parts_one,
    )
    first_two, pack_three, qkv = lax.optimization_barrier((first_two, pack_three, qkv))
    second_two = gather_second(first_two, shards)
    z_three = gather_z(pack_three, shards)

    mixed, power, inverse = call(
        attend_kernel,
        "attend",
        tubes,
        [SMEM, wide_rows],
        [
            (narrow, shape_of(total, width)),
            (probs_spec, shape_of(tubes, HEADS, length, length)),
            (narrow, shape_of(total, width)),
        ],
        [],
        4 * big,
        frames, qkv,
    )
    up_row = lines[8:12].reshape(4, shards, rows).transpose(1, 0, 2).reshape(1, units)
    second_two, mixed, z_three = lax.optimization_barrier((second_two, mixed, z_three))
    core_two = gather_core(second_two, shards)
    core_two, z_three, mixed = lax.optimization_barrier((core_two, z_three, mixed))
    parts_two = finish(1, second_two, core_two)
    first_three = gather_first(z_three, shards)

    resid, normed_two, active, slope, upstream = call(
        functools.partial(feed_kernel, plans[1], counts[1]),
        "feed",
        tubes,
        [SMEM, SMEM, SMEM, narrow, narrow, narrow, fixed(16, width), fixed(1, units)] + [HBM] * counts[1],
        [
            (narrow, shape_of(total, width)),
            (narrow, shape_of(total, width)),
            (deep_rows, shape_of(total, units)),
            (deep_rows, shape_of(total, units)),
            (narrow, shape_of(total, width)),
        ],
        [pltpu.VMEM((width, width), BF16), pltpu.VMEM((width, units), BF16), sem((number[1],))],
        8 * big,
        here, there, frames, tokens, mixed, cotangent, lines, up_row, *parts_two,
    )
    first_three, active, upstream = lax.optimization_barrier((first_three, active, upstream))
    second_three = gather_second(first_three, shards)
    down_away, down_own = rel_grad([(active, upstream)], shards)
    second_three, down_away, slope = lax.optimization_barrier((second_three, down_away, slope))
    core_three = gather_core(second_three, shards)
    down_got = arrive(down_away, shards, "core", 1)
    core_three, down_got, slope = lax.optimization_barrier((core_three, down_got, slope))
    parts_three = finish(2, second_three, core_three)
    down_second = reduce_second(down_own, down_got, shards)

    direct = rows % 16 == 0
    ff_width = full + ff
    outs = [
        (narrow, shape_of(total, width)),
        (narrow, shape_of(total, width)),
        (fixed(8, width), shape_of(8, width, kind=F32)),
        (fixed(1, units), shape_of(1, units, kind=F32)),
    ]
    scratch = [
        pltpu.VMEM((width, width), BF16),
        pltpu.VMEM((width, units), BF16),
        pltpu.VMEM((units, width), BF16),
        pltpu.VMEM((total, units), BF16),
        pltpu.VMEM((total, width), BF16),
        sem((number[1] + number[2],)),
        sem((3 + side,)),
    ]
    if direct:
        outs.append((HBM, shape_of(side, side, depth, rows, ff_width)))
        outs += [(HBM, shape_of(side, depth, rows, ff_width))] * side
        scratch += [
            pltpu.VMEM((2, total, width), BF16),
            pltpu.VMEM((2, width, total), BF16),
            pltpu.VMEM((width, 768), F32),
            pltpu.VMEM((2, side, side, depth, rows, ff_width), BF16),
        ]
    else:
        outs.append((HBM, shape_of(total, units)))
    attended_grad, scaled_grad, sums_two, up_sum, *more = call(
        functools.partial(feed_back_kernel, plans[1:], counts[1:], depth, side, rows, direct),
        "feed_back",
        tubes,
        [SMEM, SMEM, narrow, deep_rows, narrow, narrow, fixed(16, width)] + [HBM] * (2 + counts[1] + counts[2]),
        outs,
        scratch,
        14 * big,
        here, there, upstream, slope, resid, inverse, lines, mixed, normed_two, *parts_two, *parts_three,
    )
    if direct:
        ff_away, ff_own = more[0], more[1:]
    else:
        ff_away, ff_own = rel_grad([(mixed, attended_grad), (normed_two, more[0])], shards)
    down_second, ff_away, scaled_grad = lax.optimization_barrier((down_second, ff_away, scaled_grad))
    ff_got = arrive(ff_away, shards, "core", 1)
    down_first = reduce_first(down_second, shards)

    project_grad, sums_heads = call(
        attend_back_kernel,
        "attend_back",
        tubes,
        [wide_rows, probs_spec, narrow, narrow],
        [(wide_rows, shape_of(total, 3 * width)), (fixed(8, width), shape_of(8, width, kind=F32))],
        [],
        4 * big,
        qkv, power, mixed, scaled_grad,
    )
    ff_got, down_first, project_grad = lax.optimization_barrier((ff_got, down_first, project_grad))
    ff_second = reduce_second(ff_own, ff_got, shards)
    down_half = reduce_z(down_first, shards)
    qkv_away, qkv_own = rel_grad([(normed_one, project_grad)], shards)
    qkv_away, project_grad, ff_second, down_half = lax.optimization_barrier((qkv_away, project_grad, ff_second, down_half))
    qkv_got = arrive(qkv_away, shards, "core", 1)
    ff_first = reduce_first(ff_second, shards)
    (down_whole,) = both_halves(down_half, shards, (full,))

    tokens_grad, sums_one = call(
        functools.partial(first_back_kernel, plans[0], counts[0]),
        "first_back",
        2,
        [SMEM, SMEM, tall_narrow, tall_wide, tall_narrow, fixed(16, width)] + [HBM] * counts[0],
        [(tall_narrow, shape_of(total, width)), (fixed(8, width), shape_of(8, width, kind=F32))],
        [pltpu.VMEM((width, 3 * width), BF16), sem((number[0],))],
        3 * big,
        here, there, tokens, project_grad, attended_grad, lines, *parts_one,
    )
    qkv_got, ff_first, tokens_grad, sums_one, active = lax.optimization_barrier(
        (qkv_got, ff_first, tokens_grad, sums_one, active)
    )
    sums = jnp.concatenate(
        [
            sums_one[:2],
            sums_heads[:2],
            sums_two[SUM_BIAS_OUT : SUM_BIAS_OUT + 1],
            sums_two[SUM_GAIN_TWO : SUM_GAIN_TWO + 1],
            sums_two[SUM_SHIFT_TWO : SUM_SHIFT_TWO + 1],
            sums_two[SUM_BIAS_DOWN : SUM_BIAS_DOWN + 1],
            up_sum.reshape(-1, width),
        ],
        axis=0,
    ).astype(BF16)
    qkv_second = reduce_second(qkv_own, qkv_got, shards)
    ff_half = reduce_z(ff_first, shards)
    sums = exchange_lines(sums, shards, "first")

    (block_out,) = call(
        functools.partial(block_out_kernel, plans[2], counts[2]),
        "block_out",
        tubes,
        [SMEM, SMEM, deep_rows, narrow, fixed(16, width)] + [HBM] * counts[2],
        [(narrow, shape_of(total, width))],
        [pltpu.VMEM((units, width), BF16), sem((number[2],))],
        4 * big,
        here, there, active, resid, lines, *parts_three,
    )
    qkv_second, ff_half, block_out, sums = lax.optimization_barrier((qkv_second, ff_half, block_out, sums))
    qkv_first = reduce_first(qkv_second, shards)
    out_whole, up_whole = both_halves(ff_half, shards, (full, ff))
    sums = exchange_lines(sums, shards, "second")
    qkv_first, sums, out_whole, up_whole = lax.optimization_barrier((qkv_first, sums, out_whole, up_whole))
    qkv_half = reduce_z(qkv_first, shards)
    sums = exchange_lines(sums, shards, "z")
    qkv_half, sums = lax.optimization_barrier((qkv_half, sums))
    sums = exchange_lines(sums, shards, "core")
    (qkv_whole,) = both_halves(qkv_half, shards, (wide,))
    at = lax.axis_index("fsdp")
    sums_here = lax.dynamic_slice_in_dim(sums[:8], at * rows, rows, axis=1).astype(F32)
    up_here = lax.dynamic_slice_in_dim(sums[8:].reshape(-1), at * up_bias.shape[0], up_bias.shape[0]).astype(F32)
    return (
        block_out,
        tokens_grad,
        sums_here[0],
        sums_here[1],
        qkv_whole,
        sums_here[2],
        sums_here[3],
        out_whole,
        sums_here[4],
        sums_here[5],
        sums_here[6],
        up_whole,
        up_here,
        down_whole,
        sums_here[7],
    )


def solution(mesh):
    return jax.shard_map(
        local,
        mesh=mesh,
        in_specs=(
            P(("dp", "fsdp"), None),
            P(),
            P(("dp", "fsdp")),
            P("fsdp"),
            P("fsdp"),
            P("fsdp", None),
            P("fsdp"),
            P("fsdp"),
            P("fsdp", None),
            P("fsdp"),
            P("fsdp"),
            P("fsdp"),
            P("fsdp", None),
            P("fsdp"),
            P("fsdp", None),
            P("fsdp"),
            P(("dp", "fsdp"), None),
        ),
        out_specs=(
            P(("dp", "fsdp"), None),
            P(("dp", "fsdp"), None),
            P("fsdp"),
            P("fsdp"),
            P("fsdp", None),
            P("fsdp"),
            P("fsdp"),
            P("fsdp", None),
            P("fsdp"),
            P("fsdp"),
            P("fsdp"),
            P("fsdp", None),
            P("fsdp"),
            P("fsdp", None),
            P("fsdp"),
        ),
        check_vma=False,
    )
```

time: 346 us -> 294 us (0.85)
  waiting for transfers between devices: 93.5 us -> 58 us
  local copies, waits for them, and re-layouts: 30.6 us -> 17.4 us
  Pallas kernels: 141 us -> 130 us
  other arithmetic: 14.5 us -> 23.1 us
  starting transfers between devices: 64.4 us -> 59.1 us
    ppermute x55 -> x53, waiting for transfers between devices: 93.5 us -> 58 us  [arrive(): return lax.ppermute(value, AXES, pairs)]
    pallas_call x8 -> x2, Pallas kernels: 43 us -> 23.4 us  [rel_grad(): pl.pallas_call(functools.partial(grad_kernel, depth, side, rows, deep, wi...]
    convert_element_type x20 -> x25, other arithmetic: 4.75 us -> 20.9 us  [the longest x19 17 us: sum_of(): return total.astype(BF16)]
    unnamed x57 -> x37, local copies, waits for them, and re-layouts: 18.1 us -> 3.34 us
    pallas_call x6 -> x7, Pallas kernels: 97.5 us -> 107 us  [call(): pl.pallas_call(kernel, grid=(grid,), in_specs=in_specs, out_specs=[spec f...]
    another operation x16 -> x8, other arithmetic: 9.15 us -> 0.7 us  [the longest x3 0.38 us: gather_first(): jnp.stack([got] + [arrive(got, shards, 'first', s) for s in range(1, side)])]
    another operation x19 -> x1, local copies, waits for them, and re-layouts: 6.86 us -> 0.91 us  [gather_z(): jnp.stack([unit] + [arrive(unit, shards, 'z', s) for s in range(1, depth)])]
    concatenate x2, local copies, waits for them, and re-layouts: 0.22 us -> 6.14 us  [the longest x1 6.09 us: spread_lines(): unit = jnp.concatenate(vectors)]
  transfers between devices with their start and end apart: 55 -> 53, of which waited for: 20 -> 19; matrix products, arithmetic and copies ran while one was open for 7% -> 8% of each run, Pallas kernels for 28% -> 45%
where the time goes in v2:
time: 294 us; the launch traced here: 290 us
  Pallas kernels  130 us (44%)
  starting transfers between devices  59.1 us (20%)
  waiting for transfers between devices  58 us (20%)
  other arithmetic  23.1 us (8%)
  local copies, waits for them, and re-layouts  17.4 us (6%)
    pallas_call x7, Pallas kernels, call(): pl.pallas_call(kernel, grid=(grid,), in_specs=in_specs, out_specs=[spec f...  107 us
    ppermute x53, starting transfers between devices, arrive(): return lax.ppermute(value, AXES, pairs)  59.1 us
    ppermute x53, waiting for transfers between devices, arrive(): return lax.ppermute(value, AXES, pairs)  58 us
    pallas_call x2, Pallas kernels, rel_grad(): pl.pallas_call(functools.partial(grad_kernel, depth, side, rows, deep, wi...  23.4 us
    convert_element_type x19, other arithmetic, sum_of(): return total.astype(BF16)  17 us
    concatenate x1, local copies, waits for them, and re-layouts, spread_lines(): unit = jnp.concatenate(vectors)  6.09 us
  transfers between devices with their start and end apart: 53, of which 19 were waited for; matrix products, arithmetic and copies ran while one was open for 8% of the time, Pallas kernels for 45%

profile of v2, /device:TPU:0, one launch (start us, length us, event | category | flops | bytes accessed | tf_op | source)
XLA Modules:
  0.0 289.5 jit_solution(17065820850747211051)
XLA Ops:
  1.6 3.1 %collective-permute-start.2 = (bf16[48,1152]{1,0:T(8,128)(2,1)S(1)}, bf16[48,1152]{1,0:T(8,128)(2,1)S(1)}, u32[]{:S(2)}, u32[]{:S(2)}) collective-permute-start(bf16[48,1152]{1,0:T(8,128)(2,1)S(1)} %constant_dynamic-slice_fusion.3), channel_id=1, source_target_pairs={{12,0},{13,1},{14,2},{15,3},{0,4},{1,5},{2,6},{3,7},{4,8},{5,9},{6... | collective-permute-start | bytes 331784 | tf_op jit(solution)/shard_map/z_exchange/ppermute | solution.py:53
  4.7 2.6 collective-permute-start.1
  7.3 1.3 collective-permute-start
  9.6 6.1 %concatenate.24 = bf16[576]{0:T(1024)(128)(2,1)S(1)} concatenate(bf16[48]{0:T(256)(128)(2,1)} %param.20, bf16[48]{0:T(256)(128)(2,1)} %param.21, bf16[48]{0:T(256)(128)(2,1)} %param.23, bf16[48]{0:T(256)(128)(2,1)} %param.24, bf16[48]{0:T(256)(128)(2,1)} %param.26, bf16[48]{0:T(256)(128)(2,1)} %param.27, bf16[48]{0:T(256)(128)(2,1)} %param.28, bf16[48]{0:T(256)(128)(2,1)} %param.32, ...), dimensions={0} | concatenate | bytes 2304 | tf_op jit(solution)/shard_map/concatenate | solution.py:70
  17.6 1.6 collective-permute-start.3
  19.7 6.6 %collective-permute-done.4 = bf16[16,8,128]{2,1,0:T(8,128)(2,1)S(1)} collective-permute-done((bf16[16,8,128]{2,1,0:T(8,128)(2,1)S(1)}, bf16[16,8,128]{2,1,0:T(8,128)(2,1)S(1)}, u32[]{:S(2)}, u32[]{:S(2)}) %collective-permute-start.4) | collective-permute-done | bytes 32800 | tf_op jit(solution)/shard_map/first_exchange/ppermute | solution.py:53
  26.5 1.6 collective-permute-start.5
  29.6 2.3 collective-permute-start.9
  32.5 1.7 collective-permute-done.11
  35.0 3.5 %collective-permute-start.6 = (bf16[48,1920]{1,0:T(8,128)(2,1)S(1)}, bf16[48,1920]{1,0:T(8,128)(2,1)S(1)}, u32[]{:S(2)}, u32[]{:S(2)}) collective-permute-start(bf16[48,1920]{1,0:T(8,128)(2,1)S(1)} %pad_maximum_fusion.6), channel_id=1, source_target_pairs={{4,0},{5,1},{6,2},{7,3},{8,4},{9,5},{10,6},{11,7},{12,8},{13,9},{1... | collective-permute-start | bytes 552968 | tf_op jit(solution)/shard_map/z_exchange/ppermute | solution.py:53
  38.5 2.8 collective-permute-done.8
  41.3 5.8 %collective-permute-done.7 = bf16[48,1920]{1,0:T(8,128)(2,1)S(1)} collective-permute-done((bf16[48,1920]{1,0:T(8,128)(2,1)S(1)}, bf16[48,1920]{1,0:T(8,128)(2,1)S(1)}, u32[]{:S(2)}, u32[]{:S(2)}) %collective-permute-start.7) | collective-permute-done | bytes 184352 | tf_op jit(solution)/shard_map/z_exchange/ppermute | solution.py:53
  48.7 3.0 %collective-permute-done.14 = bf16[16,8,128]{2,1,0:T(8,128)(2,1)S(1)} collective-permute-done((bf16[16,8,128]{2,1,0:T(8,128)(2,1)S(1)}, bf16[16,8,128]{2,1,0:T(8,128)(2,1)S(1)}, u32[]{:S(2)}, u32[]{:S(2)}) %collective-permute-start.14) | collective-permute-done | bytes 32800 | tf_op jit(solution)/shard_map/second_exchange/ppermute | solution.py:53
  55.8 9.7 %project.1 = (bf16[1024,768]{1,0:T(8,128)(2,1)}, bf16[1024,2304]{1,0:T(8,128)(2,1)}) custom-call(s32[5]{0:T(128)} %stack.134.here, s32[5]{0:T(128)} %stack.131.there, bf16[1024,768]{1,0:T(8,128)(2,1)} %tokens.2, f32[16,768]{1,0:T(8,128)} %pad_convert_fusion.lines, bf16[2,4,48,1152]{3,2,1,0:T(8,128)(2,1)} %copy-done.6, ...), custom_call_target="tpu_custom_call" | custom-call | flops 3623878656 | bytes 16777216 | tf_op jit(solution)/shard_map/project/pallas_call | solution.py:660
  67.5 3.9 %collective-permute-start.19 = (bf16[192,384]{1,0:T(8,128)(2,1)S(1)}, bf16[192,384]{1,0:T(8,128)(2,1)S(1)}, u32[]{:S(2)}, u32[]{:S(2)}) collective-permute-start(bf16[192,384]{1,0:T(8,128)(2,1)S(1)} %constant_dynamic-slice_fusion), channel_id=1, source_target_pairs={{12,0},{13,1},{14,2},{15,3},{0,4},{1,5},{2,6},{3,7},{4,8},{5,9},{6... | collective-permute-start | bytes 442376 | tf_op jit(solution)/shard_map/z_exchange/ppermute | solution.py:53
  72.3 1.6 collective-permute-start.17
  73.9 8.4 %attend.1 = (bf16[1024,768]{1,0:T(8,128)(2,1)}, bf16[4,12,256,256]{3,2,1,0:T(8,128)(2,1)}, bf16[1024,768]{1,0:T(8,128)(2,1)}) custom-call(s32[4]{0:T(128)} %select_reduce_fusion.frames, bf16[1024,2304]{1,0:T(8,128)(2,1)} %get-tuple-element.140.qkv_ref.qkv), custom_call_target="tpu_custom_call" | custom-call | flops 4831838208 | bytes 16777216 | tf_op jit(solution)/shard_map/attend/pallas_call | solution.py:660
  82.4 2.9 collective-permute-done.16.refs_1_.refs_3_
  86.6 4.2 %collective-permute-done.20.refs_2_.refs_4_ = bf16[2,4,48,1920]{3,2,1,0:T(8,128)(2,1)} collective-permute-done((bf16[2,4,48,1920]{3,2,1,0:T(8,128)(2,1)S(1)}, bf16[2,4,48,1920]{3,2,1,0:T(8,128)(2,1)}, u32[]{:S(2)}, u32[]{:S(2)}) %collective-permute-start.20) | collective-permute-done | bytes 1474592 | tf_op jit(solution)/shard_map/core_exchange/ppermute | solution.py:53
  92.0 18.6 %feed.1 = (bf16[1024,768]{1,0:T(8,128)(2,1)}, bf16[1024,768]{1,0:T(8,128)(2,1)}, bf16[1024,3072]{1,0:T(8,128)(2,1)}, bf16[1024,3072]{1,0:T(8,128)(2,1)}, bf16[1024,768]{1,0:T(8,128)(2,1)}) custom-call(s32[5]{0:T(128)} %stack.134.here, s32[5]{0:T(128)} %stack.131.there, s32[4]{0:T(128)} %select_reduce_fusion.frames, bf16[1024,768]{1,0:T(8,128)(2,1)} %tokens.2, ...), custom_call_target="tpu_custom_call" | custom-call | flops 9663676416 | bytes 16777216 | tf_op jit(solution)/shard_map/feed/pallas_call | solution.py:660
  111.8 12.5 %grad.2 = (bf16[2,2,4,192,384]{4,3,2,1,0:T(8,128)(2,1)}, bf16[2,4,192,384]{3,2,1,0:T(8,128)(2,1)}, bf16[2,4,192,384]{3,2,1,0:T(8,128)(2,1)}) custom-call(s32[5]{0:T(128)} %stack.131.there, s32[5]{0:T(128)} %stack.134.here, bf16[1024,3072]{1,0:T(8,128)(2,1)} %get-tuple-element.202.refs_0_.active, bf16[1024,768]{1,0:T(8,128)(2,1)} %get-tuple-element.154.refs_1_.upstream), custom_call_target="tpu_custom_call" | custom-call | flops 4831838208 | bytes 20971520 | tf_op jit(solution)/shard_map/grad/pallas_call | solution.py:248
  124.3 2.8 collective-permute-done.23.refs_7_.refs_1_
  128.6 7.0 %collective-permute-done.24.refs_8_.refs_2_ = bf16[2,4,192,384]{3,2,1,0:T(8,128)(2,1)S(1)} collective-permute-done((bf16[2,4,192,384]{3,2,1,0:T(8,128)(2,1)S(1)}, bf16[2,4,192,384]{3,2,1,0:T(8,128)(2,1)S(1)}, u32[]{:S(2)}, u32[]{:S(2)}) %collective-permute-start.24) | collective-permute-done | bytes 1179680 | tf_op jit(solution)/shard_map/core_exchange/ppermute | solution.py:53
  137.3 1.6 fusion.1
  139.8 34.1 %feed_back.1 = (bf16[1024,768]{1,0:T(8,128)(2,1)}, bf16[1024,768]{1,0:T(8,128)(2,1)}, f32[8,768]{1,0:T(8,128)}, f32[1,3072]{1,0:T(1,128)}, bf16[2,2,4,48,1920]{4...) custom-call(s32[5]{0:T(128)} %stack.134.here, s32[5]{0:T(128)} %stack.131.there, ...), custom_call_target="tpu_custom_call" | custom-call | flops 16911433728 | bytes 16777216 | tf_op jit(solution)/shard_map/feed_back/pallas_call | solution.py:660
  173.9 2.9 fusion.5
  177.9 13.9 %attend_back.1 = (bf16[1024,2304]{1,0:T(8,128)(2,1)}, f32[8,768]{1,0:T(8,128)}) custom-call(bf16[1024,2304]{1,0:T(8,128)(2,1)} %get-tuple-element.140.qkv_ref.qkv, bf16[4,12,256,256]{3,2,1,0:T(8,128)(2,1)} %get-tuple-element.176.power_ref, bf16[1024,768]{1,0:T(8,128)(2,1)} %get-tuple-element.148.mixed.refs_0_, bf16[1024,768]{1,0:T(8,128)(2,1)} %get-tuple-element.177.scaled_grad), custom_call_target="tpu_custom_call" | custom-call | flops 4831838208 | bytes 16777216 | tf_op jit(solution)/shard_map/attend_back/pallas_call | solution.py:660
  191.8 1.4 fusion.16
  193.5 1.5 fusion
  196.0 4.4 %collective-permute-start.33 = (bf16[192,384]{1,0:T(8,128)(2,1)S(1)}, bf16[192,384]{1,0:T(8,128)(2,1)S(1)}, u32[]{:S(2)}, u32[]{:S(2)}) collective-permute-start(bf16[192,384]{1,0:T(8,128)(2,1)S(1)} %get-tuple-element.188), channel_id=1, source_target_pairs={{4,0},{5,1},{6,2},{7,3},{8,4},{9,5},{10,6},{11,7},{12,8},{13,9},{1... | collective-permute-start | bytes 442376 | tf_op jit(solution)/shard_map/z_exchange/ppermute | solution.py:53
  201.3 10.9 %grad.3 = (bf16[2,2,4,48,1152]{4,3,2,1,0:T(8,128)(2,1)}, bf16[2,4,48,1152]{3,2,1,0:T(8,128)(2,1)}, bf16[2,4,48,1152]{3,2,1,0:T(8,128)(2,1)}) custom-call(s32[5]{0:T(128)} %stack.131.there, s32[5]{0:T(128)} %stack.134.here, bf16[1024,768]{1,0:T(8,128)(2,1)} %get-tuple-element.135.refs_0_, bf16[1024,2304]{1,0:T(8,128)(2,1)} %get-tuple-element.192.refs_1_.project_grad), custom_call_target="tpu_custom_call" | custom-call | flops 3623878656 | bytes 20971520 | tf_op jit(solution)/shard_map/grad/pallas_call | solution.py:248
  212.2 2.2 collective-permute-done.32
  214.7 3.2 %fusion.3 = (bf16[4,48,1920]{2,1,0:T(8,128)(2,1)}, bf16[4,48,1920]{2,1,0:T(8,128)(2,1)S(1)}) fusion(bf16[2,4,48,1920]{3,2,1,0:T(8,128)(2,1)} %collective-permute-done.30, bf16[2,2,4,48,1920]{4,3,2,1,0:T(8,128)(2,1)S(1)} %collective-permute-done.28, bf16[2,4,48,1920]{3,2,1,0:T(8,128)(2,1)} %get-tuple-element.182), kind=kLoop, calls=%fused_computation.8 | loop fusion | flops 4423680 | bytes 5898240 | tf_op jit(solution)/shard_map/convert_element_type | solution.py:275
  219.7 11.2 %first_back.1 = (bf16[1024,768]{1,0:T(8,128)(2,1)}, f32[8,768]{1,0:T(8,128)}) custom-call(s32[5]{0:T(128)} %stack.134.here, s32[5]{0:T(128)} %stack.131.there, bf16[1024,768]{1,0:T(8,128)(2,1)} %tokens.2, bf16[1024,2304]{1,0:T(8,128)(2,1)} %get-tuple-element.192.refs_1_.project_grad, bf16[1024,768]{1,0:T(8,128)(2,1)} %get-tuple-element.193.attended_grad, ...), custom_call_target="tpu_custom_call" | custom-call | flops 3623878656 | bytes 16777216 | tf_op jit(solution)/shard_map/first_back/pallas_call | solution.py:660
  230.9 2.2 fusion.12
  233.1 1.2 fusion.2
  235.4 4.2 %collective-permute-start.39 = (bf16[48,1920]{1,0:T(8,128)(2,1)}, bf16[48,1920]{1,0:T(8,128)(2,1)S(1)}, u32[]{:S(2)}, u32[]{:S(2)}) collective-permute-start(bf16[48,1920]{1,0:T(8,128)(2,1)} %get-tuple-element.201), channel_id=1, source_target_pairs={{4,0},{5,1},{6,2},{7,3},{8,4},{9,5},{10,6},{11,7},{12,8},{13,9},{1... | collective-permute-start | bytes 552968 | tf_op jit(solution)/shard_map/z_exchange/ppermute | solution.py:53
  239.5 1.2 collective-permute-start.38
  242.5 11.0 %block_out.1 = bf16[1024,768]{1,0:T(8,128)(2,1)} custom-call(s32[5]{0:T(128)} %stack.134.here, s32[5]{0:T(128)} %stack.131.there, bf16[1024,3072]{1,0:T(8,128)(2,1)} %get-tuple-element.202.refs_0_.active, bf16[1024,768]{1,0:T(8,128)(2,1)} %get-tuple-element.166.resid, f32[16,768]{1,0:T(8,128)} %pad_convert_fusion.lines, bf16[2,4,192,384]{3,2,1,0:T(8,128)(2,1)} %copy-done.4, ...), custom_call_target="tpu_custom_call" | custom-call | flops 4831838208 | bytes 16777216 | tf_op jit(solution)/shard_map/block_out/pallas_call | solution.py:660
  253.6 3.7 %collective-permute-done.38 = bf16[48,1920]{1,0:T(8,128)(2,1)S(1)} collective-permute-done((bf16[48,1920]{1,0:T(8,128)(2,1)}, bf16[48,1920]{1,0:T(8,128)(2,1)S(1)}, u32[]{:S(2)}, u32[]{:S(2)}) %collective-permute-start.38) | collective-permute-done | bytes 184352 | tf_op jit(solution)/shard_map/z_exchange/ppermute | solution.py:53
  257.3 1.7 add_convert_fusion
  262.3 1.6 collective-permute-done.42
  265.5 4.1 %collective-permute-done.41 = bf16[4,48,1152]{2,1,0:T(8,128)(2,1)S(1)} collective-permute-done((bf16[4,48,1152]{2,1,0:T(8,128)(2,1)}, bf16[4,48,1152]{2,1,0:T(8,128)(2,1)S(1)}, u32[]{:S(2)}, u32[]{:S(2)}) %collective-permute-start.41) | collective-permute-done | bytes 442400 | tf_op jit(solution)/shard_map/first_exchange/ppermute | solution.py:53
  269.8 1.3 collective-permute-start.48
  271.1 2.8 collective-permute-start.47
  274.3 1.5 collective-permute-start.45
  275.8 1.9 collective-permute-start.44
  278.9 6.7 %collective-permute-done.45 = bf16[48,1152]{1,0:T(8,128)(2,1)S(1)} collective-permute-done((bf16[48,1152]{1,0:T(8,128)(2,1)S(1)}, bf16[48,1152]{1,0:T(8,128)(2,1)S(1)}, u32[]{:S(2)}, u32[]{:S(2)}) %collective-permute-start.45) | collective-permute-done | bytes 110624 | tf_op jit(solution)/shard_map/z_exchange/ppermute | solution.py:53
  (178 shorter events, 42.3 us)
Async XLA Ops:
  1.6 15.9 %collective-permute-start.2 = (bf16[48,1152]{1,0:T(8,128)(2,1)S(1)}, bf16[48,1152]{1,0:T(8,128)(2,1)S(1)}, u32[]{:S(2)}, u32[]{:S(2)}) collective-permute-start(bf16[48,1152]{1,0:T(8,128)(2,1)S(1)} %constant_dynamic-slice_fusion.3), channel_id=1, source_target_pairs={{12,0},{13,1},{14,2},{15,3},{0,4},{1,5},{2,6},{3,7},{4,8},{5,9},{6... | collective-permute-start | bytes 331784 | tf_op jit(solution)/shard_map/z_exchange/ppermute | solution.py:53
  4.7 12.8 %collective-permute-start.1 = (bf16[48,1152]{1,0:T(8,128)(2,1)S(1)}, bf16[48,1152]{1,0:T(8,128)(2,1)S(1)}, u32[]{:S(2)}, u32[]{:S(2)}) collective-permute-start(bf16[48,1152]{1,0:T(8,128)(2,1)S(1)} %constant_dynamic-slice_fusion.3), channel_id=1, source_target_pairs={{8,0},{9,1},{10,2},{11,3},{12,4},{13,5},{14,6},{15,7},{0,8},{1,9},... | collective-permute-start | bytes 331784 | tf_op jit(solution)/shard_map/z_exchange/ppermute | solution.py:53
  7.3 10.3 %collective-permute-start = (bf16[48,1152]{1,0:T(8,128)(2,1)S(1)}, bf16[48,1152]{1,0:T(8,128)(2,1)S(1)}, u32[]{:S(2)}, u32[]{:S(2)}) collective-permute-start(bf16[48,1152]{1,0:T(8,128)(2,1)S(1)} %constant_dynamic-slice_fusion.3), channel_id=1, source_target_pairs={{4,0},{5,1},{6,2},{7,3},{8,4},{9,5},{10,6},{11,7},{12,8},{13,9},{1... | collective-permute-start | bytes 331784 | tf_op jit(solution)/shard_map/z_exchange/ppermute | solution.py:53
  17.6 8.7 %collective-permute-start.3 = (bf16[4,48,1152]{2,1,0:T(8,128)(2,1)S(1)}, bf16[4,48,1152]{2,1,0:T(8,128)(2,1)S(1)}, u32[]{:S(2)}, u32[]{:S(2)}) collective-permute-start(bf16[4,48,1152]{2,1,0:T(8,128)(2,1)S(1)} %pad_maximum_fusion.5), channel_id=1, source_target_pairs={{1,0},{0,1},{3,2},{2,3},{5,4},{4,5},{7,6},{6,7},{9,8},{8,9},{11,10... | collective-permute-start | bytes 1327112 | tf_op jit(solution)/shard_map/first_exchange/ppermute | solution.py:53
  19.2 7.2 %collective-permute-start.4 = (bf16[16,8,128]{2,1,0:T(8,128)(2,1)S(1)}, bf16[16,8,128]{2,1,0:T(8,128)(2,1)S(1)}, u32[]{:S(2)}, u32[]{:S(2)}) collective-permute-start(bf16[16,8,128]{2,1,0:T(8,128)(2,1)S(1)} %broadcast_select_fusion.6), channel_id=1, source_target_pairs={{1,0},{0,1},{3,2},{2,3},{5,4},{4,5},{7,6},{6,7},{9,8},{8,9},{11,10... | collective-permute-start | bytes 98312 | tf_op jit(solution)/shard_map/first_exchange/ppermute | solution.py:53
  26.5 20.7 %collective-permute-start.5 = (bf16[2,4,48,1152]{3,2,1,0:T(8,128)(2,1)S(1)}, bf16[2,4,48,1152]{3,2,1,0:T(8,128)(2,1)}, u32[]{:S(2)}, u32[]{:S(2)}) collective-permute-start(bf16[2,4,48,1152]{3,2,1,0:T(8,128)(2,1)S(1)} %pad_maximum_fusion.2.refs_0_), channel_id=1, source_target_pairs={{2,0},{3,1},{0,2},{1,3},{6,4},{7,5},{4,6},{5,7},{10,8},{11,9},{8,1... | collective-permute-start | bytes 2654216 | tf_op jit(solution)/shard_map/second_exchange/ppermute | solution.py:53
  28.1 6.1 %collective-permute-start.11 = (bf16[16,8,128]{2,1,0:T(8,128)(2,1)S(1)}, bf16[16,8,128]{2,1,0:T(8,128)(2,1)S(1)}, u32[]{:S(2)}, u32[]{:S(2)}) collective-permute-start(bf16[16,8,128]{2,1,0:T(8,128)(2,1)S(1)} %add_convert_fusion.17), channel_id=1, source_target_pairs={{12,0},{13,1},{14,2},{15,3},{0,4},{1,5},{2,6},{3,7},{4,8},{5,9},{6... | collective-permute-start | bytes 98312 | tf_op jit(solution)/shard_map/z_exchange/ppermute | solution.py:53
  28.8 6.2 %collective-permute-start.10 = (bf16[16,8,128]{2,1,0:T(8,128)(2,1)S(1)}, bf16[16,8,128]{2,1,0:T(8,128)(2,1)S(1)}, u32[]{:S(2)}, u32[]{:S(2)}) collective-permute-start(bf16[16,8,128]{2,1,0:T(8,128)(2,1)S(1)} %add_convert_fusion.17), channel_id=1, source_target_pairs={{8,0},{9,1},{10,2},{11,3},{12,4},{13,5},{14,6},{15,7},{0,8},{1,9},... | collective-permute-start | bytes 98312 | tf_op jit(solution)/shard_map/z_exchange/ppermute | solution.py:53
  29.6 8.9 %collective-permute-start.9 = (bf16[16,8,128]{2,1,0:T(8,128)(2,1)S(1)}, bf16[16,8,128]{2,1,0:T(8,128)(2,1)S(1)}, u32[]{:S(2)}, u32[]{:S(2)}) collective-permute-start(bf16[16,8,128]{2,1,0:T(8,128)(2,1)S(1)} %add_convert_fusion.17), channel_id=1, source_target_pairs={{4,0},{5,1},{6,2},{7,3},{8,4},{9,5},{10,6},{11,7},{12,8},{13,9},{1... | collective-permute-start | bytes 98312 | tf_op jit(solution)/shard_map/z_exchange/ppermute | solution.py:53
  31.9 9.4 %collective-permute-start.8 = (bf16[48,1920]{1,0:T(8,128)(2,1)S(1)}, bf16[48,1920]{1,0:T(8,128)(2,1)S(1)}, u32[]{:S(2)}, u32[]{:S(2)}) collective-permute-start(bf16[48,1920]{1,0:T(8,128)(2,1)S(1)} %pad_maximum_fusion.6), channel_id=1, source_target_pairs={{12,0},{13,1},{14,2},{15,3},{0,4},{1,5},{2,6},{3,7},{4,8},{5,9},{6... | collective-permute-start | bytes 552968 | tf_op jit(solution)/shard_map/z_exchange/ppermute | solution.py:53
  34.1 13.0 %collective-permute-start.7 = (bf16[48,1920]{1,0:T(8,128)(2,1)S(1)}, bf16[48,1920]{1,0:T(8,128)(2,1)S(1)}, u32[]{:S(2)}, u32[]{:S(2)}) collective-permute-start(bf16[48,1920]{1,0:T(8,128)(2,1)S(1)} %pad_maximum_fusion.6), channel_id=1, source_target_pairs={{8,0},{9,1},{10,2},{11,3},{12,4},{13,5},{14,6},{15,7},{0,8},{1,9},... | collective-permute-start | bytes 552968 | tf_op jit(solution)/shard_map/z_exchange/ppermute | solution.py:53
  35.0 12.1 %collective-permute-start.6 = (bf16[48,1920]{1,0:T(8,128)(2,1)S(1)}, bf16[48,1920]{1,0:T(8,128)(2,1)S(1)}, u32[]{:S(2)}, u32[]{:S(2)}) collective-permute-start(bf16[48,1920]{1,0:T(8,128)(2,1)S(1)} %pad_maximum_fusion.6), channel_id=1, source_target_pairs={{4,0},{5,1},{6,2},{7,3},{8,4},{9,5},{10,6},{11,7},{12,8},{13,9},{1... | collective-permute-start | bytes 552968 | tf_op jit(solution)/shard_map/z_exchange/ppermute | solution.py:53
  47.2 5.4 %collective-permute-start.12 = (bf16[2,4,48,1152]{3,2,1,0:T(8,128)(2,1)S(1)}, bf16[2,4,48,1152]{3,2,1,0:T(8,128)(2,1)S(1)}, u32[]{:S(2)}, u32[]{:S(2)}) collective-permute-start(bf16[2,4,48,1152]{3,2,1,0:T(8,128)(2,1)S(1)} %pad_maximum_fusion.2.refs_0_), channel_id=1, source_target_pairs={{16,0},{17,1},{18,2},{19,3},{20,4},{21,5},{22,6},{23,7},{24,8},{25... | collective-permute-start | bytes 2654216 | tf_op jit(solution)/shard_map/core_exchange/ppermute | solution.py:53
  47.3 6.3 %collective-permute-start.13 = (bf16[2,4,48,1152]{3,2,1,0:T(8,128)(2,1)}, bf16[2,4,48,1152]{3,2,1,0:T(8,128)(2,1)}, u32[]{:S(2)}, u32[]{:S(2)}) collective-permute-start(bf16[2,4,48,1152]{3,2,1,0:T(8,128)(2,1)} %collective-permute-done.5.refs_1_), channel_id=1, source_target_pairs={{16,0},{17,1},{18,2},{19,3},{20,4},{21,5},{22,6},{23,7},{24,8},{25... | collective-permute-start | bytes 2654216 | tf_op jit(solution)/shard_map/core_exchange/ppermute | solution.py:53
  53.6 11.9 %collective-permute-start.15 = (bf16[4,48,1920]{2,1,0:T(8,128)(2,1)S(1)}, bf16[4,48,1920]{2,1,0:T(8,128)(2,1)S(1)}, u32[]{:S(2)}, u32[]{:S(2)}) collective-permute-start(bf16[4,48,1920]{2,1,0:T(8,128)(2,1)S(1)} %pad_maximum_fusion.3), channel_id=1, source_target_pairs={{1,0},{0,1},{3,2},{2,3},{5,4},{4,5},{7,6},{6,7},{9,8},{8,9},{11,10... | collective-permute-start | bytes 2211848 | tf_op jit(solution)/shard_map/first_exchange/ppermute | solution.py:53
  65.7 19.5 %collective-permute-start.16 = (bf16[2,4,48,1920]{3,2,1,0:T(8,128)(2,1)S(1)}, bf16[2,4,48,1920]{3,2,1,0:T(8,128)(2,1)}, u32[]{:S(2)}, u32[]{:S(2)}) collective-permute-start(bf16[2,4,48,1920]{3,2,1,0:T(8,128)(2,1)S(1)} %pad_maximum_fusion.refs_0_.refs_2_), channel_id=1, source_target_pairs={{2,0},{3,1},{0,2},{1,3},{6,4},{7,5},{4,6},{5,7},{10,8},{11,9},{8,1... | collective-permute-start | bytes 4423688 | tf_op jit(solution)/shard_map/second_exchange/ppermute | solution.py:53
  67.5 14.8 %collective-permute-start.19 = (bf16[192,384]{1,0:T(8,128)(2,1)S(1)}, bf16[192,384]{1,0:T(8,128)(2,1)S(1)}, u32[]{:S(2)}, u32[]{:S(2)}) collective-permute-start(bf16[192,384]{1,0:T(8,128)(2,1)S(1)} %constant_dynamic-slice_fusion), channel_id=1, source_target_pairs={{12,0},{13,1},{14,2},{15,3},{0,4},{1,5},{2,6},{3,7},{4,8},{5,9},{6... | collective-permute-start | bytes 442376 | tf_op jit(solution)/shard_map/z_exchange/ppermute | solution.py:53
  71.4 10.9 %collective-permute-start.18 = (bf16[192,384]{1,0:T(8,128)(2,1)S(1)}, bf16[192,384]{1,0:T(8,128)(2,1)S(1)}, u32[]{:S(2)}, u32[]{:S(2)}) collective-permute-start(bf16[192,384]{1,0:T(8,128)(2,1)S(1)} %constant_dynamic-slice_fusion), channel_id=1, source_target_pairs={{8,0},{9,1},{10,2},{11,3},{12,4},{13,5},{14,6},{15,7},{0,8},{1,9},... | collective-permute-start | bytes 442376 | tf_op jit(solution)/shard_map/z_exchange/ppermute | solution.py:53
  72.3 10.0 %collective-permute-start.17 = (bf16[192,384]{1,0:T(8,128)(2,1)S(1)}, bf16[192,384]{1,0:T(8,128)(2,1)S(1)}, u32[]{:S(2)}, u32[]{:S(2)}) collective-permute-start(bf16[192,384]{1,0:T(8,128)(2,1)S(1)} %constant_dynamic-slice_fusion), channel_id=1, source_target_pairs={{4,0},{5,1},{6,2},{7,3},{8,4},{9,5},{10,6},{11,7},{12,8},{13,9},{1... | collective-permute-start | bytes 442376 | tf_op jit(solution)/shard_map/z_exchange/ppermute | solution.py:53
  85.3 5.5 %collective-permute-start.20 = (bf16[2,4,48,1920]{3,2,1,0:T(8,128)(2,1)S(1)}, bf16[2,4,48,1920]{3,2,1,0:T(8,128)(2,1)}, u32[]{:S(2)}, u32[]{:S(2)}) collective-permute-start(bf16[2,4,48,1920]{3,2,1,0:T(8,128)(2,1)S(1)} %pad_maximum_fusion.refs_0_.refs_2_), channel_id=1, source_target_pairs={{16,0},{17,1},{18,2},{19,3},{20,4},{21,5},{22,6},{23,7},{24,8},{25... | collective-permute-start | bytes 4423688 | tf_op jit(solution)/shard_map/core_exchange/ppermute | solution.py:53
  85.3 5.7 %collective-permute-start.21 = (bf16[2,4,48,1920]{3,2,1,0:T(8,128)(2,1)}, bf16[2,4,48,1920]{3,2,1,0:T(8,128)(2,1)}, u32[]{:S(2)}, u32[]{:S(2)}) collective-permute-start(bf16[2,4,48,1920]{3,2,1,0:T(8,128)(2,1)} %collective-permute-done.16.refs_1_.refs_3_), channel_id=1, source_target_pairs={{16,0},{17,1},{18,2},{19,3},{20,4},{21,5},{22,6},{23,7},{24,8},{25... | collective-permute-start | bytes 4423688 | tf_op jit(solution)/shard_map/core_exchange/ppermute | solution.py:53
  91.0 19.7 %collective-permute-start.22 = (bf16[4,192,384]{2,1,0:T(8,128)(2,1)S(1)}, bf16[4,192,384]{2,1,0:T(8,128)(2,1)S(1)}, u32[]{:S(2)}, u32[]{:S(2)}) collective-permute-start(bf16[4,192,384]{2,1,0:T(8,128)(2,1)S(1)} %pad_maximum_fusion.4), channel_id=1, source_target_pairs={{1,0},{0,1},{3,2},{2,3},{5,4},{4,5},{7,6},{6,7},{9,8},{8,9},{11,10... | collective-permute-start | bytes 1769480 | tf_op jit(solution)/shard_map/first_exchange/ppermute | solution.py:53
  110.8 16.3 %collective-permute-start.23 = (bf16[2,4,192,384]{3,2,1,0:T(8,128)(2,1)S(1)}, bf16[2,4,192,384]{3,2,1,0:T(8,128)(2,1)S(1)}, u32[]{:S(2)}, u32[]{:S(2)}) collective-permute-start(bf16[2,4,192,384]{3,2,1,0:T(8,128)(2,1)S(1)} %pad_maximum_fusion.1.refs_6_.refs_0_), channel_id=1, source_target_pairs={{2,0},{3,1},{0,2},{1,3},{6,4},{7,5},{4,6},{5,7},{10,8},{11,9},{8,1... | collective-permute-start | bytes 3538952 | tf_op jit(solution)/shard_map/second_exchange/ppermute | solution.py:53
  128.1 8.1 %collective-permute-start.26 = (bf16[2,2,4,192,384]{4,3,2,1,0:T(8,128)(2,1)}, bf16[2,2,4,192,384]{4,3,2,1,0:T(8,128)(2,1)S(1)}, u32[]{:S(2)}, u32[]{:S(2)}) collective-permute-start(bf16[2,2,4,192,384]{4,3,2,1,0:T(8,128)(2,1)} %get-tuple-element.161), channel_id=1, source_target_pairs={{16,0},{17,1},{18,2},{19,3},{20,4},{21,5},{22,6},{23,7},{24,8},{25... | collective-permute-start | bytes 7077896 | tf_op jit(solution)/shard_map/core_exchange/ppermute | solution.py:53
  128.1 7.5 %collective-permute-start.24 = (bf16[2,4,192,384]{3,2,1,0:T(8,128)(2,1)S(1)}, bf16[2,4,192,384]{3,2,1,0:T(8,128)(2,1)S(1)}, u32[]{:S(2)}, u32[]{:S(2)}) collective-permute-start(bf16[2,4,192,384]{3,2,1,0:T(8,128)(2,1)S(1)} %pad_maximum_fusion.1.refs_6_.refs_0_), channel_id=1, source_target_pairs={{16,0},{17,1},{18,2},{19,3},{20,4},{21,5},{22,6},{23,7},{24,8},{25... | collective-permute-start | bytes 3538952 | tf_op jit(solution)/shard_map/core_exchange/ppermute | solution.py:53
  128.6 7.6 %collective-permute-start.25 = (bf16[2,4,192,384]{3,2,1,0:T(8,128)(2,1)}, bf16[2,4,192,384]{3,2,1,0:T(8,128)(2,1)S(1)}, u32[]{:S(2)}, u32[]{:S(2)}) collective-permute-start(bf16[2,4,192,384]{3,2,1,0:T(8,128)(2,1)} %copy-done.12), channel_id=1, source_target_pairs={{16,0},{17,1},{18,2},{19,3},{20,4},{21,5},{22,6},{23,7},{24,8},{25... | collective-permute-start | bytes 3538952 | tf_op jit(solution)/shard_map/core_exchange/ppermute | solution.py:53
  138.8 35.1 %collective-permute-start.27 = (bf16[2,4,192,384]{3,2,1,0:T(8,128)(2,1)S(1)}, bf16[2,4,192,384]{3,2,1,0:T(8,128)(2,1)}, u32[]{:S(2)}, u32[]{:S(2)}) collective-permute-start(bf16[2,4,192,384]{3,2,1,0:T(8,128)(2,1)S(1)} %fusion.1), channel_id=1, source_target_pairs={{2,0},{3,1},{0,2},{1,3},{6,4},{7,5},{4,6},{5,7},{10,8},{11,9},{8,1... | collective-permute-start | bytes 3538952 | tf_op jit(solution)/shard_map/second_exchange/ppermute | solution.py:53
  176.8 16.4 %collective-permute-start.28 = (bf16[2,2,4,48,1920]{4,3,2,1,0:T(8,128)(2,1)}, bf16[2,2,4,48,1920]{4,3,2,1,0:T(8,128)(2,1)S(1)}, u32[]{:S(2)}, u32[]{:S(2)}) collective-permute-start(bf16[2,2,4,48,1920]{4,3,2,1,0:T(8,128)(2,1)} %get-tuple-element.173), channel_id=1, source_target_pairs={{16,0},{17,1},{18,2},{19,3},{20,4},{21,5},{22,6},{23,7},{24,8},{25... | collective-permute-start | bytes 8847368 | tf_op jit(solution)/shard_map/core_exchange/ppermute | solution.py:53
  176.9 15.0 %collective-permute-start.29 = (bf16[4,192,384]{2,1,0:T(8,128)(2,1)}, bf16[4,192,384]{2,1,0:T(8,128)(2,1)}, u32[]{:S(2)}, u32[]{:S(2)}) collective-permute-start(bf16[4,192,384]{2,1,0:T(8,128)(2,1)} %get-tuple-element.175), channel_id=1, source_target_pairs={{1,0},{0,1},{3,2},{2,3},{5,4},{4,5},{7,6},{6,7},{9,8},{8,9},{11,10... | collective-permute-start | bytes 1769480 | tf_op jit(solution)/shard_map/first_exchange/ppermute | solution.py:53
  195.0 19.7 %collective-permute-start.30 = (bf16[2,4,48,1920]{3,2,1,0:T(8,128)(2,1)}, bf16[2,4,48,1920]{3,2,1,0:T(8,128)(2,1)}, u32[]{:S(2)}, u32[]{:S(2)}) collective-permute-start(bf16[2,4,48,1920]{3,2,1,0:T(8,128)(2,1)} %fusion), channel_id=1, source_target_pairs={{2,0},{3,1},{0,2},{1,3},{6,4},{7,5},{4,6},{5,7},{10,8},{11,9},{8,1... | collective-permute-start | bytes 4423688 | tf_op jit(solution)/shard_map/second_exchange/ppermute | solution.py:53
  196.0 16.2 %collective-permute-start.33 = (bf16[192,384]{1,0:T(8,128)(2,1)S(1)}, bf16[192,384]{1,0:T(8,128)(2,1)S(1)}, u32[]{:S(2)}, u32[]{:S(2)}) collective-permute-start(bf16[192,384]{1,0:T(8,128)(2,1)S(1)} %get-tuple-element.188), channel_id=1, source_target_pairs={{4,0},{5,1},{6,2},{7,3},{8,4},{9,5},{10,6},{11,7},{12,8},{13,9},{1... | collective-permute-start | bytes 442376 | tf_op jit(solution)/shard_map/z_exchange/ppermute | solution.py:53
  200.4 14.1 %collective-permute-start.32 = (bf16[192,384]{1,0:T(8,128)(2,1)S(1)}, bf16[192,384]{1,0:T(8,128)(2,1)S(1)}, u32[]{:S(2)}, u32[]{:S(2)}) collective-permute-start(bf16[192,384]{1,0:T(8,128)(2,1)S(1)} %get-tuple-element.187), channel_id=1, source_target_pairs={{8,0},{9,1},{10,2},{11,3},{12,4},{13,5},{14,6},{15,7},{0,8},{1,9},... | collective-permute-start | bytes 442376 | tf_op jit(solution)/shard_map/z_exchange/ppermute | solution.py:53
  201.3 13.2 %collective-permute-start.31 = (bf16[192,384]{1,0:T(8,128)(2,1)S(1)}, bf16[192,384]{1,0:T(8,128)(2,1)S(1)}, u32[]{:S(2)}, u32[]{:S(2)}) collective-permute-start(bf16[192,384]{1,0:T(8,128)(2,1)S(1)} %get-tuple-element.186), channel_id=1, source_target_pairs={{12,0},{13,1},{14,2},{15,3},{0,4},{1,5},{2,6},{3,7},{4,8},{5,9},{6... | collective-permute-start | bytes 442376 | tf_op jit(solution)/shard_map/z_exchange/ppermute | solution.py:53
  217.9 15.2 %collective-permute-start.34 = (bf16[2,2,4,48,1152]{4,3,2,1,0:T(8,128)(2,1)}, bf16[2,2,4,48,1152]{4,3,2,1,0:T(8,128)(2,1)S(1)}, u32[]{:S(2)}, u32[]{:S(2)}) collective-permute-start(bf16[2,2,4,48,1152]{4,3,2,1,0:T(8,128)(2,1)} %get-tuple-element.189), channel_id=1, source_target_pairs={{16,0},{17,1},{18,2},{19,3},{20,4},{21,5},{22,6},{23,7},{24,8},{25... | collective-permute-start | bytes 5308424 | tf_op jit(solution)/shard_map/core_exchange/ppermute | solution.py:53
  217.9 13.1 %collective-permute-start.35 = (bf16[4,48,1920]{2,1,0:T(8,128)(2,1)}, bf16[4,48,1920]{2,1,0:T(8,128)(2,1)}, u32[]{:S(2)}, u32[]{:S(2)}) collective-permute-start(bf16[4,48,1920]{2,1,0:T(8,128)(2,1)} %get-tuple-element.191), channel_id=1, source_target_pairs={{1,0},{0,1},{3,2},{2,3},{5,4},{4,5},{7,6},{6,7},{9,8},{8,9},{11,10... | collective-permute-start | bytes 2211848 | tf_op jit(solution)/shard_map/first_exchange/ppermute | solution.py:53
  234.3 24.6 %collective-permute-start.36 = (bf16[2,4,48,1152]{3,2,1,0:T(8,128)(2,1)}, bf16[2,4,48,1152]{3,2,1,0:T(8,128)(2,1)S(1)}, u32[]{:S(2)}, u32[]{:S(2)}) collective-permute-start(bf16[2,4,48,1152]{3,2,1,0:T(8,128)(2,1)} %fusion.2), channel_id=1, source_target_pairs={{2,0},{3,1},{0,2},{1,3},{6,4},{7,5},{4,6},{5,7},{10,8},{11,9},{8,1... | collective-permute-start | bytes 2654216 | tf_op jit(solution)/shard_map/second_exchange/ppermute | solution.py:53
  235.4 18.2 %collective-permute-start.39 = (bf16[48,1920]{1,0:T(8,128)(2,1)}, bf16[48,1920]{1,0:T(8,128)(2,1)S(1)}, u32[]{:S(2)}, u32[]{:S(2)}) collective-permute-start(bf16[48,1920]{1,0:T(8,128)(2,1)} %get-tuple-element.201), channel_id=1, source_target_pairs={{4,0},{5,1},{6,2},{7,3},{8,4},{9,5},{10,6},{11,7},{12,8},{13,9},{1... | collective-permute-start | bytes 552968 | tf_op jit(solution)/shard_map/z_exchange/ppermute | solution.py:53
  239.5 17.7 %collective-permute-start.38 = (bf16[48,1920]{1,0:T(8,128)(2,1)}, bf16[48,1920]{1,0:T(8,128)(2,1)S(1)}, u32[]{:S(2)}, u32[]{:S(2)}) collective-permute-start(bf16[48,1920]{1,0:T(8,128)(2,1)} %get-tuple-element.200), channel_id=1, source_target_pairs={{8,0},{9,1},{10,2},{11,3},{12,4},{13,5},{14,6},{15,7},{0,8},{1,9},... | collective-permute-start | bytes 552968 | tf_op jit(solution)/shard_map/z_exchange/ppermute | solution.py:53
  240.7 16.5 %collective-permute-start.37 = (bf16[48,1920]{1,0:T(8,128)(2,1)}, bf16[48,1920]{1,0:T(8,128)(2,1)}, u32[]{:S(2)}, u32[]{:S(2)}) collective-permute-start(bf16[48,1920]{1,0:T(8,128)(2,1)} %get-tuple-element.199), channel_id=1, source_target_pairs={{12,0},{13,1},{14,2},{15,3},{0,4},{1,5},{2,6},{3,7},{4,8},{5,9},{6... | collective-permute-start | bytes 552968 | tf_op jit(solution)/shard_map/z_exchange/ppermute | solution.py:53
  241.5 12.0 %collective-permute-start.40 = (bf16[12,768]{1,0:T(8,128)(2,1)S(1)}, bf16[12,768]{1,0:T(8,128)(2,1)S(1)}, u32[]{:S(2)}, u32[]{:S(2)}) collective-permute-start(bf16[12,768]{1,0:T(8,128)(2,1)S(1)} %concatenate.26), channel_id=1, source_target_pairs={{1,0},{0,1},{3,2},{2,3},{5,4},{4,5},{7,6},{6,7},{9,8},{8,9},{11,10... | collective-permute-start | bytes 55304 | tf_op jit(solution)/shard_map/first_exchange/ppermute | solution.py:53
  261.1 12.9 %collective-permute-start.52 = (bf16[192,384]{1,0:T(8,128)(2,1)S(1)}, bf16[192,384]{1,0:T(8,128)(2,1)S(1)}, u32[]{:S(2)}, u32[]{:S(2)}) collective-permute-start(bf16[192,384]{1,0:T(8,128)(2,1)S(1)} %add_convert_fusion.5), channel_id=1, source_target_pairs={{16,0},{17,1},{18,2},{19,3},{20,4},{21,5},{22,6},{23,7},{24,8},{25... | collective-permute-start | bytes 442376 | tf_op jit(solution)/shard_map/core_exchange/ppermute | solution.py:53
  261.1 8.5 %collective-permute-start.41 = (bf16[4,48,1152]{2,1,0:T(8,128)(2,1)}, bf16[4,48,1152]{2,1,0:T(8,128)(2,1)S(1)}, u32[]{:S(2)}, u32[]{:S(2)}) collective-permute-start(bf16[4,48,1152]{2,1,0:T(8,128)(2,1)} %get-tuple-element.210), channel_id=1, source_target_pairs={{1,0},{0,1},{3,2},{2,3},{5,4},{4,5},{7,6},{6,7},{9,8},{8,9},{11,10... | collective-permute-start | bytes 1327112 | tf_op jit(solution)/shard_map/first_exchange/ppermute | solution.py:53
  269.7 6.1 %collective-permute-start.49 = (bf16[12,768]{1,0:T(8,128)(2,1)S(1)}, bf16[12,768]{1,0:T(8,128)(2,1)S(1)}, u32[]{:S(2)}, u32[]{:S(2)}) collective-permute-start(bf16[12,768]{1,0:T(8,128)(2,1)S(1)} %add_convert_fusion.20), channel_id=1, source_target_pairs={{12,0},{13,1},{14,2},{15,3},{0,4},{1,5},{2,6},{3,7},{4,8},{5,9},{6... | collective-permute-start | bytes 55304 | tf_op jit(solution)/shard_map/z_exchange/ppermute | solution.py:53
  269.8 8.0 %collective-permute-start.48 = (bf16[12,768]{1,0:T(8,128)(2,1)S(1)}, bf16[12,768]{1,0:T(8,128)(2,1)S(1)}, u32[]{:S(2)}, u32[]{:S(2)}) collective-permute-start(bf16[12,768]{1,0:T(8,128)(2,1)S(1)} %add_convert_fusion.20), channel_id=1, source_target_pairs={{8,0},{9,1},{10,2},{11,3},{12,4},{13,5},{14,6},{15,7},{0,8},{1,9},... | collective-permute-start | bytes 55304 | tf_op jit(solution)/shard_map/z_exchange/ppermute | solution.py:53
  271.1 6.6 %collective-permute-start.47 = (bf16[12,768]{1,0:T(8,128)(2,1)S(1)}, bf16[12,768]{1,0:T(8,128)(2,1)S(1)}, u32[]{:S(2)}, u32[]{:S(2)}) collective-permute-start(bf16[12,768]{1,0:T(8,128)(2,1)S(1)} %add_convert_fusion.20), channel_id=1, source_target_pairs={{4,0},{5,1},{6,2},{7,3},{8,4},{9,5},{10,6},{11,7},{12,8},{13,9},{1... | collective-permute-start | bytes 55304 | tf_op jit(solution)/shard_map/z_exchange/ppermute | solution.py:53
  274.0 4.9 %collective-permute-start.46 = (bf16[48,1152]{1,0:T(8,128)(2,1)S(1)}, bf16[48,1152]{1,0:T(8,128)(2,1)S(1)}, u32[]{:S(2)}, u32[]{:S(2)}) collective-permute-start(bf16[48,1152]{1,0:T(8,128)(2,1)S(1)} %get-tuple-element.216), channel_id=1, source_target_pairs={{4,0},{5,1},{6,2},{7,3},{8,4},{9,5},{10,6},{11,7},{12,8},{13,9},{1... | collective-permute-start | bytes 331784 | tf_op jit(solution)/shard_map/z_exchange/ppermute | solution.py:53
  274.3 11.3 %collective-permute-start.45 = (bf16[48,1152]{1,0:T(8,128)(2,1)S(1)}, bf16[48,1152]{1,0:T(8,128)(2,1)S(1)}, u32[]{:S(2)}, u32[]{:S(2)}) collective-permute-start(bf16[48,1152]{1,0:T(8,128)(2,1)S(1)} %get-tuple-element.215), channel_id=1, source_target_pairs={{8,0},{9,1},{10,2},{11,3},{12,4},{13,5},{14,6},{15,7},{0,8},{1,9},... | collective-permute-start | bytes 331784 | tf_op jit(solution)/shard_map/z_exchange/ppermute | solution.py:53
  275.8 9.9 %collective-permute-start.44 = (bf16[48,1152]{1,0:T(8,128)(2,1)S(1)}, bf16[48,1152]{1,0:T(8,128)(2,1)S(1)}, u32[]{:S(2)}, u32[]{:S(2)}) collective-permute-start(bf16[48,1152]{1,0:T(8,128)(2,1)S(1)} %get-tuple-element.214), channel_id=1, source_target_pairs={{12,0},{13,1},{14,2},{15,3},{0,4},{1,5},{2,6},{3,7},{4,8},{5,9},{6... | collective-permute-start | bytes 331784 | tf_op jit(solution)/shard_map/z_exchange/ppermute | solution.py:53
  (25 other events, 175.5 us)
